TPU v7x, 256 devices: a whole 4x4x8 slice. The times are simulated.
256 devices in a mesh: grp: 8 (over z_hi, y), dev: 32 (over x, z_lo, core).
Axes of the slice: x: 4, y: 4, z: 8 (z_hi: 2, z_lo: 4; z = z_hi * 4 + z_lo), core: 2. Of those that a mesh axis runs over, the one named last changes fastest.
Arguments:
- hidden_in: bfloat16 [256, 256, 1024], P(('grp', 'dev'))
- w_query: bfloat16 [1024, 1024], P('grp'), may hold values from -0.1875 to 0.1875
- w_keyval: bfloat16 [1024, 2048], P('grp'), may hold values from -0.1875 to 0.1875
- w_out: bfloat16 [1024, 1024], P('grp'), may hold values from -0.1875 to 0.1875
- ln_gain: float32 [1024], replicated, may hold values from 0.1 to 1.9
- ln_bias: float32 [1024], replicated, may hold values from -3 to 3
- bank: bfloat16 [65536, 1024], P(('grp', 'dev')), may hold values from -6 to 6
- owner: int32 [256], P(('grp', 'dev')), may hold values from 0 to 255, as said below
- slot: int32 [256], P(('grp', 'dev')), may hold values from 0 to 255
Outputs:
- updated: bfloat16 [65536, 1024], P(('grp', 'dev'))
Inputs may be any that keep to these rules, and one draw needn't show every extreme that they name: `owner`: each device owns at most 8 sampled passages, and some device owns exactly 8.
All inputs are finite; a program needn't handle non-finite values.
Results may differ from a plain program's by a relative error of at most 0.012.
The roundings to bfloat16 on the way count: a program that leaves them out, or rounds other values in their place, can miss the bound.
Values may be sent and summed in bfloat16 or wider, within the bound.
No kernel may reach another device: no remote copies, remote signals or barrier semaphores. Data moves between devices by JAX's collectives and lax.ppermute only.
A program may use at most 128 MiB of HBM per device.

v0:
```python
import jax
import jax.numpy as jnp
from jax import lax
from jax.sharding import PartitionSpec as P

HEADS = 16
HEAD = 64
MOST = 8


def local(hidden_in, w_query, w_keyval, w_out, ln_gain, ln_bias, bank, owner, slot):
    count = hidden_in.shape[0]
    length = hidden_in.shape[1]
    width = hidden_in.shape[2]
    owner_all, slot_all = (
        lax.all_gather(owner, ("grp", "dev"), axis=0, tiled=True),
        lax.all_gather(slot, ("grp", "dev"), axis=0, tiled=True),
    )
    flat = hidden_in.reshape(count * length, width)
    keyval = jnp.dot(
        flat,
        lax.all_gather(w_keyval, "grp", axis=0, tiled=True),
        preferred_element_type=jnp.float32,
    ).astype(jnp.bfloat16)
    keyval = keyval.reshape(count, length, 2, HEADS, HEAD)
    query_whole, out_whole = (
        lax.all_gather(w_query, "grp", axis=0, tiled=True),
        lax.all_gather(w_out, "grp", axis=0, tiled=True),
    )
    cls = hidden_in[:, 0, :]
    query = (0.125 * jnp.dot(cls, query_whole, preferred_element_type=jnp.float32)).astype(
        jnp.bfloat16
    )
    query = query.reshape(count, HEADS, HEAD)
    scores = jnp.einsum("she,slhe->shl", query, keyval[:, :, 0], preferred_element_type=jnp.float32)
    probs = jax.nn.softmax(scores, axis=-1).astype(jnp.bfloat16)
    context = jnp.einsum(
        "shl,slhe->she", probs, keyval[:, :, 1], preferred_element_type=jnp.float32
    )
    context = context.astype(jnp.bfloat16).reshape(count, width)
    joined = cls.astype(jnp.float32) + jnp.dot(
        context, out_whole, preferred_element_type=jnp.float32
    )
    center = joined - jnp.mean(joined, axis=-1, keepdims=True)
    normed = (
        center / jnp.sqrt(jnp.mean(center * center, axis=-1, keepdims=True) + 1e-05) * ln_gain
        + ln_bias
    )
    fresh = (normed / jnp.sqrt(jnp.mean(normed * normed, axis=-1, keepdims=True) + 1e-06)).astype(
        jnp.bfloat16
    )
    fresh_all = lax.all_gather(fresh, ("grp", "dev"), axis=0, tiled=True)
    myself = lax.axis_index("grp") * lax.axis_size("dev") + lax.axis_index("dev")
    owned = owner_all == myself
    ranking = jnp.cumsum(owned.astype(jnp.int32)) - 1
    places = jnp.arange(MOST, dtype=jnp.int32)
    select = owned[None, :] & (ranking[None, :] == places[:, None])
    valid = jnp.any(select, axis=1)
    packed_slot = jnp.sum(jnp.where(select, slot_all[None, :], 0), axis=1)
    old_rows = jnp.where(valid[:, None], bank[packed_slot], jnp.zeros((), jnp.bfloat16))
    samples = owner_all.shape[0]
    identity = jnp.eye(width, dtype=jnp.float32)
    fresh_rows = jnp.dot(
        select.astype(jnp.bfloat16), fresh_all, preferred_element_type=jnp.float32
    ).astype(jnp.bfloat16)
    gram_part = jnp.einsum("md,me->de", old_rows, old_rows, preferred_element_type=jnp.float32)
    cross_part = jnp.einsum("md,me->de", old_rows, fresh_rows, preferred_element_type=jnp.float32)
    gram_part, cross_part = (gram_part, cross_part)
    gram, cross = lax.psum((gram_part, cross_part), ("grp", "dev"))
    factor = jnp.linalg.cholesky(gram + 0.25 * samples * identity)
    adapter = jax.scipy.linalg.cho_solve((factor, True), cross).astype(jnp.bfloat16)
    return jnp.dot(bank, adapter, preferred_element_type=jnp.float32).astype(jnp.bfloat16)


def solution(mesh):
    in_specs = (
        P(("grp", "dev"), None, None),
        P("grp", None),
        P("grp", None),
        P("grp", None),
        P(),
        P(),
        P(("grp", "dev"), None),
        P(("grp", "dev")),
        P(("grp", "dev")),
    )
    out_specs = P(("grp", "dev"), None)
    return jax.shard_map(local, mesh=mesh, in_specs=in_specs, out_specs=out_specs, check_vma=False)
```

profile of v0, /device:TPU:1, one launch (start us, length us, event | category | flops | bytes accessed | tf_op | source)
XLA Modules:
  0.0 1269.2 jit_solution(780324188457631988)
XLA Ops:
  10.3 97.0 %all-reduce.3 = (s32[256]{0:T(256)S(1)}, s32[256]{0:T(256)S(1)}) all-reduce(s32[256]{0:T(256)S(1)} %dynamic-update-slice.48, s32[256]{0:T(256)S(1)} %dynamic-update-slice.47), channel_id=1, replica_groups=mesh['grp'=8,'dev'=32] {'grp','dev'}, use_global_device_ids=true, to_apply=%add.2 | all-reduce | flops 512 | bytes 4096
  114.4 81.5 %all-gather.7.cloned.1.call-done = bf16[1024,2048]{1,0:T(8,128)(2,1)} async-done(((bf16[128,2048]{1,0:T(8,128)(2,1)}), bf16[1024,2048]{1,0:T(8,128)(2,1)}) %all-gather.7.cloned.1.call-update) | async-done | bytes 4194320 | tf_op jit(solution)/shard_map/all_gather | solution.py:22
  200.9 67.7 %all-gather.9.cloned.1.call-done = bf16[1024,1024]{1,0:T(8,128)(2,1)} async-done(((bf16[128,1024]{1,0:T(8,128)(2,1)}), bf16[1024,1024]{1,0:T(8,128)(2,1)}) %all-gather.9.cloned.1.call-update) | async-done | bytes 2097168 | tf_op jit(solution)/shard_map/all_gather | solution.py:28
  274.5 344.4 %all-gather = bf16[262144]{0:T(1024)(128)(2,1)S(1)} all-gather(bf16[1024]{0:T(1024)(128)(2,1)S(1)} %divide_convert_fusion.1), channel_id=2, replica_groups=mesh['grp'=8,'dev'=32] {'grp','dev'}, dimensions={0}, use_global_device_ids=true | all-gather | bytes 526336 | tf_op jit(solution)/shard_map/all_gather | solution.py:52
  621.9 273.2 %all-reduce.7.cloned.1.call-done = (f32[1024,1024]{1,0:T(8,128)}, f32[1024,1024]{0,1:T(8,128)}) async-done(((f32[1024,1024]{1,0:T(8,128)}, f32[1024,1024]{0,1:T(8,128)}), (f32[1024,1024]{1,0:T(8,128)}, f32[1024,1024]{0,1:T(8,128)})) %all-reduce.7.cloned.1.call-update) | async-done | bytes 8388624 | tf_op jit(solution)/shard_map/psum | solution.py:69
  899.9 5.5 copy.70
  911.8 11.7 cholesky.222
  923.7 9.8 custom-call.66
  936.8 11.7 cholesky.243
  948.8 9.8 custom-call.67
  964.2 11.7 cholesky.466
  976.7 9.8 custom-call.68
  991.2 11.7 cholesky.485
  1003.7 9.8 custom-call.69
  1017.8 11.9 cholesky.504
  1030.5 9.8 custom-call.70
  1044.7 11.7 cholesky.524
  1057.2 9.8 custom-call.71
  1071.2 11.7 cholesky.544
  1083.6 9.8 custom-call.72
  1096.6 11.7 cholesky.562
  1118.7 4.9 select_select_fusion
  1123.6 23.5 %while.1 = (s32[]{:T(128)}, f32[1024,1024]{0,1:T(8,128)}, s32[8,2]{0,1:T(2,128)S(1)}, f32[8,128,128]{2,1,0:T(8,128)S(1)}, s32[]{:T(128)}) while((s32[]{:T(128)}, f32[1024,1024]{0,1:T(8,128)}, s32[8,2]{0,1:T(2,128)S(1)}, f32[8,128,128]{2,1,0:T(8,128)S(1)}, s32[]{:T(128)}) %tuple.55), condition=%wide.while_cond, body=%wide.while_body.sunk | while | flops 2 | bytes 393329 | solution.py:71
  1147.1 78.8 %custom-call.73 = f32[8,128,128]{1,2,0:T(8,128)S(1)} custom-call(f32[8,128,128]{2,1,0:T(8,128)S(1)} %get-tuple-element.12), custom_call_target="InvertDiagBlocksLowerTriangular" | custom-call | tf_op jit(solution)/shard_map/jit(_cho_solve)/triangular_solve | solution.py:71
  (214 shorter events, 130.8 us)
Async XLA Ops:
  6.5 101.6 %copy-start = (bf16[256,1024]{1,0:T(8,128)(2,1)S(1)}, bf16[256,1024]{1,0:T(8,128)(2,1)}, u32[]{:S(2)}) copy-start(bf16[256,1024]{1,0:T(8,128)(2,1)} %param.15) | copy-start | bytes 1572868
  6.5 105.8 %copy-start.7 = (bf16[1,256,1024]{2,1,0:T(8,128)(2,1)S(1)}, bf16[1,256,1024]{2,1,0:T(8,128)(2,1)}, u32[]{:S(2)}) copy-start(bf16[1,256,1024]{2,1,0:T(8,128)(2,1)} %param.9) | copy-start | bytes 1572868
  6.5 105.8 %all-gather.5.cloned.1.call-start = ((), (), s32[]{:S(2)}) async-start(), calls=%async_computation | async-start | bytes 2359296 | tf_op jit(solution)/shard_map/all_gather | solution.py:27
  7.3 188.7 %all-gather.7.cloned.1.call-start = ((), (), s32[]{:S(2)}) async-start(), calls=%async_computation.1 | async-start | bytes 4718592 | tf_op jit(solution)/shard_map/all_gather | solution.py:22
  8.0 260.6 %all-gather.9.cloned.1.call-start = ((), (), s32[]{:S(2)}) async-start(), calls=%async_computation.2 | async-start | bytes 2359296 | tf_op jit(solution)/shard_map/all_gather | solution.py:28
  8.7 886.3 %all-reduce.7.cloned.1.call-start = ((), (), s32[]{:S(2)}) async-start(), calls=%async_computation.3 | async-start | bytes 16777216 | tf_op jit(solution)/shard_map/psum | solution.py:69
  199.4 73.7 %copy-start.5 = (f32[1024]{0:T(1024)S(1)}, f32[1024]{0:T(1024)}, u32[]{:S(2)}) copy-start(f32[1024]{0:T(1024)} %param.14) | copy-start | bytes 12292
  199.4 73.7 %copy-start.6 = (f32[1024]{0:T(1024)S(1)}, f32[1024]{0:T(1024)}, u32[]{:S(2)}) copy-start(f32[1024]{0:T(1024)} %param.13) | copy-start | bytes 12292
  909.8 2.0 copy-start.3
  959.8 2.0 copy-start.1
  1225.8 4.4 copy-start.2
  1229.5 3.6 copy-start.4
Sparse Core Ops, SparseCore 0:
  10.0 78.8 all-gather.4
  91.6 104.3 all-gather.6
  198.6 69.9 all-gather.8
  622.0 273.0 all-reduce.6
where the time goes:
time: 1280 us; the launch traced here: 1270 us
  blocking collectives  441 us (34%)
  waiting for transfers between devices  425 us (33%)
  other arithmetic  263 us (21%)
  matrix products  74.1 us (6%)
  local copies, waits for them, and re-layouts  42.6 us (3%)
  between operations  22.8 us (2%)
    all_gather x1, blocking collectives, local(): fresh_all = lax.all_gather(fresh, ('grp', 'dev'), axis=0, tiled=True)  344 us
    psum x1, waiting for transfers between devices, local(): gram, cross = lax.psum((gram_part, cross_part), ('grp', 'dev'))  273 us
    another operation x30, other arithmetic, local(): factor = jnp.linalg.cholesky(gram + 0.25 * samples * identity)  167 us
    unnamed x1, blocking collectives  97 us
    another operation x4, other arithmetic, local(): jax.scipy.linalg.cho_solve((factor, True), cross).astype(jnp.bfloat16)  83.7 us
    all_gather x1, waiting for transfers between devices, local(): lax.all_gather(w_keyval, 'grp', axis=0, tiled=True)  81.5 us
    all_gather x1, waiting for transfers between devices, local(): lax.all_gather(w_out, 'grp', axis=0, tiled=True)  67.7 us
    another operation x30, matrix products, local(): jax.scipy.linalg.cho_solve((factor, True), cross).astype(jnp.bfloat16)  33.3 us
  transfers between devices with their start and end apart: 4, of which 3 were waited for; matrix products, arithmetic and copies ran while one was open for 1% of the time, Pallas kernels for 0%

commit v1 on v0

v1 whole, which is shorter than its diff:
```python
import jax
import jax.numpy as jnp
from jax import lax
from jax.experimental import pallas as pl
from jax.experimental.pallas import tpu as pltpu
from jax.sharding import PartitionSpec as P

HEADS = 16
HEAD = 64
WIDTH = 1024
CUT = 128
PLANE = 32
BF = jnp.bfloat16
F32 = jnp.float32
NT = (((1,), (1,)), ((), ()))
TN = (((0,), (0,)), ((), ()))


def plane(apart=False):
    split = [(0,), (1,)] if apart else [(0, 1)]
    return [
        [(zh * 4 + y) * 32 + x * 8 + zl * 2 + c for y in range(4) for x in range(4) for c in cores]
        for zh in range(2)
        for zl in range(4)
        for cores in split
    ]


def exchange(x, groups):
    return lax.all_to_all(x, ("grp", "dev"), split_axis=0, concat_axis=0, tiled=True, axis_index_groups=groups)


def spread(x, groups):
    return exchange(jnp.broadcast_to(x[None], (len(groups[0]), *x.shape)), groups)


def after(x, *others):
    return lax.optimization_barrier((x, *others))[0]


def call(kernel, out, flops, *args, where=None, scratch=(), hbm=False, mib=12):
    vmem = pl.BlockSpec(memory_space=pltpu.VMEM)
    first = [] if where is None else [where]
    return pl.pallas_call(
        kernel,
        out_shape=out,
        in_specs=[pl.BlockSpec(memory_space=pltpu.SMEM)] * len(first)
        + [pl.BlockSpec(memory_space=pltpu.HBM) if hbm else vmem] * len(args),
        out_specs=jax.tree.map(lambda _: vmem, out),
        scratch_shapes=list(scratch),
        compiler_params=pltpu.CompilerParams(vmem_limit_bytes=mib * 2**20),
        cost_estimate=pl.CostEstimate(flops=flops, bytes_accessed=2**20, transcendentals=0),
    )(*first, *args)


def shape(dims, kind):
    return jax.ShapeDtypeStruct(dims, kind)


def dot(a, b, dims=(((1,), (0,)), ((), ()))):
    return lax.dot_general(a, b, dims, preferred_element_type=F32)


def exact(a, b):
    return jnp.dot(a, b, preferred_element_type=F32, precision=lax.Precision.HIGHEST)


def terms(x):
    high = x.astype(BF)
    rest = x - high.astype(F32)
    mid = rest.astype(BF)
    return high, mid, (rest - mid.astype(F32)).astype(BF)


def stack(refs):
    return jnp.concatenate([r[...].astype(F32) for r in refs], axis=0)


def head_mask(rows):
    row = lax.broadcasted_iota(jnp.int32, (rows, 4 * HEAD), 0)
    col = lax.broadcasted_iota(jnp.int32, (rows, 4 * HEAD), 1)
    return lax.rem(row, 4) == lax.div(col, HEAD)


def cut_kernel(where, query_ref, keyval_ref, own_ref, sent_ref, sems):
    zl, c = where[2], where[3]
    copies = []
    for ref, block in ((sent_ref, 4 * c + 3 - zl), (own_ref, 4 * c + zl)):
        at = pl.multiple_of(block * CUT, CUT)
        value_at = pl.multiple_of(block * CUT + WIDTH, CUT)
        parts = (query_ref.at[:, pl.ds(at, CUT)], keyval_ref.at[:, pl.ds(at, CUT)])
        for i, source in enumerate((*parts, keyval_ref.at[:, pl.ds(value_at, CUT)])):
            target = ref.at[:, i * CUT : (i + 1) * CUT]
            copies.append(pltpu.make_async_copy(source, target, sems.at[len(copies)]))
            copies[-1].start()
    for copy in copies:
        copy.wait()


def pick_kernel(where, near_ref, far_ref, bank_ref, keep_ref, give_ref, select_ref):
    info = jnp.concatenate([near_ref[...], far_ref[...]], axis=0)
    n = bank_ref.shape[0]
    number = lax.broadcasted_iota(jnp.int32, (n, n), 1).astype(F32)
    own, slot, place = [info[:, i : i + 1] for i in range(3)]
    a = jnp.where((place == number) & (own == where[7].astype(F32)), 1.0, 0.0).astype(BF)
    b = jnp.where(slot == number, 1.0, 0.0).astype(BF)
    select_ref[...] = dot(a, b, TN)
    for ref, c in ((keep_ref, where[3]), (give_ref, 1 - where[3])):
        select = select_ref[pl.ds(pl.multiple_of(c * (n // 2), n // 2), n // 2), :].astype(BF)
        ref[...] = dot(select, bank_ref[...]).astype(BF)


def row_blocks(where):
    zh, y = where[0], where[1]
    for k in range(4):
        yk = lax.rem(y + 4 - k, 4)
        for h in range(2):
            at = ((zh if h == 0 else 1 - zh) * 4 + yk) * CUT
            yield k, slice(h * CUT, (h + 1) * CUT), pl.ds(pl.multiple_of(at, CUT), CUT)


def cls_row(ref):
    return jnp.concatenate([ref[i : i + 1, :] for i in range(8)], axis=1)


def key_kernel(where, c0, c1, c2, c3, n0, n1, n2, n3, f0, f1, f2, f3, u0, u1, u2, u3, cls_ref):
    near, far = (n0, n1, n2, n3), (f0, f1, f2, f3)
    for k, ref in enumerate((c0, c1, c2, c3)):
        cls_ref[k : k + 1, :] = cls_row(ref)
    query = jnp.zeros((4, 4 * HEAD), F32)
    for k, rows, features in row_blocks(where):
        cls = cls_ref[0:4, features].astype(BF)
        query += jnp.concatenate([dot(cls, near[k][rows, :CUT]), dot(cls, far[k][rows, :CUT])], axis=1)
    query = (0.125 * query).astype(BF).astype(F32)
    query = jnp.concatenate([jnp.broadcast_to(query[k : k + 1], (4, 4 * HEAD)) for k in range(4)], axis=0)
    query = jnp.where(head_mask(16), query, 0.0).astype(BF)
    for k, rows, features in row_blocks(where):
        u = dot(query[:, :CUT], near[k][rows, CUT : 2 * CUT], NT) + dot(
            query[:, CUT:], far[k][rows, CUT : 2 * CUT], NT
        )
        for j, ref in enumerate((u0, u1, u2, u3)):
            ref[:, features] = u[4 * j : 4 * j + 4]


def attend_kernel(x_ref, u0, u1, u2, u3, y0, y1, y2, y3):
    x = x_ref[...]
    parts = dot(jnp.concatenate(terms(stack((u0, u1, u2, u3))), axis=0), x, NT)
    scores = parts[2 * HEADS :] + parts[HEADS : 2 * HEADS] + parts[:HEADS]
    e = jnp.exp(scores - jnp.max(scores, axis=1, keepdims=True))
    probs = (e / jnp.sum(e, axis=1, keepdims=True)).astype(BF)
    y = dot(probs, x)
    for k, ref in enumerate((y0, y1, y2, y3)):
        ref[...] = y[4 * k : 4 * k + 4]


def value_kernel(
    where, y0, y1, y2, y3, n0, n1, n2, n3, f0, f1, f2, f3, out_ref, out2_ref, old_ref, part_ref, y_ref
):
    near, far = (n0, n1, n2, n3), (f0, f1, f2, f3)
    y_ref[...] = jnp.concatenate(terms(stack((y0, y1, y2, y3))), axis=0)
    parts = jnp.zeros((3 * HEADS, 4 * HEAD), F32)
    for k, rows, features in row_blocks(where):
        y = y_ref[:, features]
        parts += jnp.concatenate([dot(y, near[k][rows, 2 * CUT :]), dot(y, far[k][rows, 2 * CUT :])], axis=1)
    parts = jnp.where(head_mask(HEADS), parts[2 * HEADS :] + parts[HEADS : 2 * HEADS] + parts[:HEADS], 0.0)
    context = [jnp.sum(parts[4 * k : 4 * k + 4], axis=0, keepdims=True) for k in range(4)]
    context = jnp.concatenate(context, axis=0).astype(BF)
    part = dot(context[:, :CUT], out_ref[...]) + dot(context[:, CUT:], out2_ref[...])
    part_ref[0:8, :] = jnp.zeros((8, WIDTH), F32)
    for k in range(4):
        part_ref[pl.ds(lax.rem(where[2] + 4 - k, 4), 1), :] = part[k : k + 1]
    part_ref[8:16, :] = jnp.sum(old_ref[...].astype(F32), axis=0)


def norm_kernel(where, t0, t1, t2, t3, c0, c1, c2, c3, gain_ref, bias_ref, rows_ref, cls_ref):
    for k, ref in enumerate((c0, c1, c2, c3)):
        cls_ref[pl.ds(lax.rem(where[2] + 4 - k, 4), 1), :] = cls_row(ref)
    total = (t0[...] + t1[...]) + (t2[...] + t3[...])
    joined = cls_ref[0:4, :] + total[0:4]
    center = joined - jnp.mean(joined, axis=-1, keepdims=True)
    var = jnp.mean(center * center, axis=-1, keepdims=True)
    normed = center / jnp.sqrt(var + 1e-05) * gain_ref[...] + bias_ref[...]
    fresh = normed / jnp.sqrt(jnp.mean(normed * normed, axis=-1, keepdims=True) + 1e-06)
    rows_ref[...] = jnp.concatenate([fresh, jnp.zeros_like(fresh), total[8:]], axis=0).astype(BF)


def product(a, b):
    a1, a2, _ = terms(a)
    b1, b2, _ = terms(b)
    return dot(a2, b1) + dot(a1, b2) + dot(a1, b1)


def update_kernel(old_ref, fresh_ref, bank_ref, out_ref):
    old = old_ref[...]
    n = old.shape[0]
    rows = lax.broadcasted_iota(jnp.int32, (n, n), 0)
    cols = lax.broadcasted_iota(jnp.int32, (n, n), 1)
    eye = jnp.where(rows == cols, 1.0, 0.0).astype(F32)
    ridge = 0.25 * n
    a = dot(old, old, NT) + ridge * eye
    norm = jnp.max(jnp.sum(jnp.abs(a), axis=1, keepdims=True))
    c = 2.0 / (ridge + norm)
    r = eye - c * a
    x = c * (eye + r)

    def size(r):
        return jnp.max(jnp.sum(jnp.abs(r), axis=1, keepdims=True))

    def step(times, state):
        t, _, x, r = state
        both = times(jnp.concatenate([x, r], axis=0), r)
        r = both[n:]
        return 2.0 * t, size(r), x + both[:n], r

    def more(state):
        return (state[0] < 9.0) & (state[1] > 1e-4)

    r = exact(r, r)
    state = (2.0 * c * ridge, size(r), x, r)
    state = lax.while_loop(lambda s: more(s) & (norm < 512.0 * ridge), lambda s: step(product, s), state)
    x = lax.while_loop(more, lambda s: step(exact, s), state)[2]

    def refine(state):
        i, _, x = state
        e = eye - exact(a, x)
        return i + 1, jnp.sum(e * e), x + exact(x, e)

    _, _, x = lax.while_loop(
        lambda s: (s[0] == 0) | ((s[1] > 1e-7) & (s[0] < 4)), refine, (jnp.int32(0), jnp.float32(1.0), x)
    )
    high, mid, low = terms(x)
    fresh = fresh_ref[...]
    z1, z2, z3 = terms(dot(low, fresh) + dot(mid, fresh) + dot(high, fresh))
    adapter = (dot(old, z3, TN) + dot(old, z2, TN) + dot(old, z1, TN)).astype(BF)
    out_ref[...] = dot(bank_ref[...], adapter).astype(BF)


def shift(x, move):
    perm = []
    for i in range(256):
        zh, y, xx, zl, c = i // 128, i // 32 % 4, i // 8 % 4, i // 2 % 4, i % 2
        zh, y, xx, zl, c = move(zh, y, xx, zl, c)
        perm.append((i, (((zh % 2) * 4 + y % 4) * 4 + xx % 4) * 8 + (zl % 4) * 2 + c % 2))
    return lax.ppermute(x, ("grp", "dev"), perm)


def along_y(x, k):
    return shift(x, lambda zh, y, xx, zl, c: (zh, y + k, xx, zl, c)) if k % 4 else x


def along_z(x, k):
    return shift(x, lambda zh, y, xx, zl, c: (zh, y, xx, zl + k, c)) if k % 4 else x


def other_core(x):
    return shift(x, lambda zh, y, xx, zl, c: (zh, y, xx, zl, c + 1))


def mirror(x):
    return shift(x, lambda zh, y, xx, zl, c: (zh + 1, y, xx, 3 - zl, c))


def local(hidden_in, w_query, w_keyval, w_out, ln_gain, ln_bias, bank, owner, slot):
    hidden = hidden_in[0]
    grp, dev = lax.axis_index("grp"), lax.axis_index("dev")
    zh, y, zl, c = grp // 4, grp % 4, dev // 2 % 4, dev % 2
    place = ((c * 4 + y) * 4 + dev // 8) * 8 + zh * 4 + zl
    where = jnp.stack([zh, y, zl, c, owner[0], slot[0], place, grp * 32 + dev])

    lane = lax.broadcasted_iota(jnp.int32, (1, 128), 1)
    info = jnp.where(lane == 0, where[4], jnp.where(lane == 1, where[5], where[6])).astype(F32)
    info = spread(info, plane()).reshape(PLANE, 128)

    own, sent = call(
        cut_kernel,
        [shape((CUT, 3 * CUT), BF)] * 2,
        2**10,
        w_query,
        w_keyval,
        where=where,
        scratch=[pltpu.SemaphoreType.DMA((6,))],
        hbm=True,
    )
    out1 = shift(w_out, lambda zh, y, xx, zl, c: (c, zl, xx, y, zh))
    own = jnp.concatenate([own, mirror(after(sent, info, out1))], axis=0)
    out2 = other_core(out1)
    near = [along_y(own, k) for k in range(4)]
    far = [other_core(w) for w in near]
    cls = jnp.concatenate([hidden[:1].astype(F32).reshape(8, 128), info], axis=0)
    cls = [along_z(cls, k) for k in range(4)]
    info = jnp.concatenate([p[8:] for p in cls], axis=0)
    half = shape((bank.shape[0] // 2, WIDTH), BF)
    keep, give = call(
        pick_kernel,
        [half, half],
        2**28,
        info,
        mirror(info),
        bank,
        where=where,
        scratch=[pltpu.VMEM((bank.shape[0], bank.shape[0]), F32)],
    )
    rows = keep + other_core(give)

    u = call(
        key_kernel,
        [shape((4, WIDTH), F32)] * 4,
        2**23,
        *cls,
        *near,
        *far,
        where=where,
        scratch=[pltpu.VMEM((8, WIDTH), F32)],
    )
    u = [along_z(a, -k) for k, a in enumerate(u)]
    rows = exchange(after(rows, *u[1:]).reshape(PLANE // 2, 8, WIDTH), plane(apart=True))
    y = call(attend_kernel, [shape((4, WIDTH), F32)] * 4, 2**25, hidden, *u)
    y = [along_z(a, k) for k, a in enumerate(y)]
    part = call(
        value_kernel,
        shape((16, WIDTH), F32),
        2**24,
        *y,
        *near,
        *far,
        out1,
        out2,
        rows,
        where=where,
        scratch=[pltpu.VMEM((3 * HEADS, WIDTH), BF)],
    )
    part = [along_z(part, k) for k in range(4)]
    mine = call(
        norm_kernel,
        shape((16, WIDTH), BF),
        2**14,
        *part,
        *cls,
        ln_gain.reshape(1, -1),
        ln_bias.reshape(1, -1),
        where=where,
        scratch=[pltpu.VMEM((8, WIDTH), F32)],
    )
    other = mirror(mine)
    low = jnp.where(zh == 0, mine[:4], other[:4])
    high = jnp.where(zh == 0, other[:4], mine[:4])
    both = spread(jnp.concatenate([low, high, mine[8:] + other[8:]], axis=0), plane(apart=True))
    both = jnp.concatenate([both, other_core(both)], axis=0)
    fresh, old = both[:, :8].reshape(256, WIDTH), both[:, 8:].reshape(256, WIDTH)
    return call(update_kernel, shape(bank.shape, BF), 2**31, old, fresh, bank, mib=32)


def solution(mesh):
    in_specs = (
        P(("grp", "dev"), None, None),
        P("grp", None),
        P("grp", None),
        P("grp", None),
        P(),
        P(),
        P(("grp", "dev"), None),
        P(("grp", "dev")),
        P(("grp", "dev")),
    )
    out_specs = P(("grp", "dev"), None)
    return jax.shard_map(local, mesh=mesh, in_specs=in_specs, out_specs=out_specs, check_vma=False)
```

time: 1280 us -> 127 us (0.10)
  blocking collectives: 441 us -> 14.2 us
  waiting for transfers between devices: 425 us -> 17.1 us
  other arithmetic: 263 us -> 1.55 us
  matrix products: 74.1 us -> 0 us
  starting transfers between devices: 0.12 us -> 66.8 us
  local copies, waits for them, and re-layouts: 42.6 us -> 5.73 us
  between operations: 22.8 us -> 1.54 us
  Pallas kernels: 0 us -> 19.9 us
    all_gather x1 -> x0, blocking collectives: 344 us -> none  [local(): fresh_all = lax.all_gather(fresh, ('grp', 'dev'), axis=0, tiled=True)]
    psum x1 -> x0, waiting for transfers between devices: 273 us -> none  [local(): gram, cross = lax.psum((gram_part, cross_part), ('grp', 'dev'))]
    another operation x37 -> x0, other arithmetic: 251 us -> none  [the longest x30 167 us: local(): factor = jnp.linalg.cholesky(gram + 0.25 * samples * identity)]
    all_gather x3 -> x0, waiting for transfers between devices: 149 us -> none  [the longest x1 81.5 us: local(): lax.all_gather(w_keyval, 'grp', axis=0, tiled=True)]
    unnamed x1 -> x0, blocking collectives: 97 us -> none
    another operation x44 -> x0, matrix products: 60 us -> none  [the longest x30 33.3 us: local(): jax.scipy.linalg.cho_solve((factor, True), cross).astype(jnp.bfloat16)]
    ppermute x0 -> x26, starting transfers between devices: none -> 52.2 us  [shift(): return lax.ppermute(x, ('grp', 'dev'), perm)]
    another operation x73 -> x1, local copies, waits for them, and re-layouts: 29.3 us -> 0.08 us  [local(): where = jnp.stack([zh, y, zl, c, owner[0], slot[0], place, grp * 32 + dev])]
  transfers between devices with their start and end apart: 4 -> 28, of which waited for: 3 -> 15; matrix products, arithmetic and copies ran while one was open for 1% -> 1% of each run, Pallas kernels for 0% -> 3%
where the time goes in v1:
time: 127 us
  starting transfers between devices  66.8 us (53%)
  Pallas kernels  19.9 us (16%)
  waiting for transfers between devices  17.1 us (13%)
  blocking collectives  14.2 us (11%)
  local copies, waits for them, and re-layouts  5.73 us (5%)
  other arithmetic  1.55 us (1%)
  between operations  1.54 us (1%)
    ppermute x26, starting transfers between devices, shift(): return lax.ppermute(x, ('grp', 'dev'), perm)  52.2 us
    pallas_call x7, Pallas kernels, call(): pl.pallas_call(kernel, out_shape=out, in_specs=[pl.BlockSpec(memory_space...  19.9 us
    ppermute x26, waiting for transfers between devices, shift(): return lax.ppermute(x, ('grp', 'dev'), perm)  14.9 us
    all_to_all x2, starting transfers between devices, exchange(): lax.all_to_all(x, ('grp', 'dev'), split_axis=0, concat_axis=0, tiled=True...  14.6 us
    all_to_all x1, blocking collectives, exchange(): lax.all_to_all(x, ('grp', 'dev'), split_axis=0, concat_axis=0, tiled=True...  14.2 us
    unnamed x28, local copies, waits for them, and re-layouts  4.84 us
  transfers between devices with their start and end apart: 28, of which 15 were waited for; matrix products, arithmetic and copies ran while one was open for 1% of the time, Pallas kernels for 3%

profile of v1, /device:TPU:1, one launch (start us, length us, event | category | flops | bytes accessed | tf_op | source)
XLA Modules:
  0.0 126.8 jit_solution(33039974060297289)
XLA Ops:
  1.9 8.6 %all-to-all-start = ((f32[32,1,128]{2,1,0:T(1,128)}), f32[32,1,128]{2,1,0:T(1,128)S(1)}, u32[]{:S(2)}, u32[]{:S(2)}) async-start(f32[32,1,128]{2,1,0:T(1,128)} %broadcast_in_dim.27), calls=%async_computation | async-start | bytes 32768 | tf_op jit(solution)/shard_map/all_to_all | solution.py:30
  10.5 8.9 %collective-permute-start.3 = (bf16[128,1024]{1,0:T(8,128)(2,1)}, bf16[128,1024]{1,0:T(8,128)(2,1)S(1)}, u32[]{:S(2)}, u32[]{:S(2)}) collective-permute-start(bf16[128,1024]{1,0:T(8,128)(2,1)} %param.12), channel_id=1, source_target_pairs={{0,0},{1,128},{2,32},{3,160},{4,64},{5,192},{6,96},{7,224},{8,8},{... | collective-permute-start | bytes 786440 | tf_op jit(solution)/shard_map/ppermute | solution.py:244
  23.0 1.6 %collective-permute-start = (f32[40,128]{1,0:T(8,128)S(1)}, f32[40,128]{1,0:T(8,128)S(1)}, u32[]{:S(2)}, u32[]{:S(2)}) collective-permute-start(f32[40,128]{1,0:T(8,128)S(1)} %pad_maximum_fusion.2.c0), channel_id=1, source_target_pairs={{0,2},{1,3},{2,4},{3,5},{4,6},{5,7},{6,0},{7,1},{8,10},{9,11},{10,... | collective-permute-start | bytes 61448 | tf_op jit(solution)/shard_map/ppermute | solution.py:244
  24.6 1.6 %collective-permute-start.1 = (f32[40,128]{1,0:T(8,128)S(1)}, f32[40,128]{1,0:T(8,128)S(1)}, u32[]{:S(2)}, u32[]{:S(2)}) collective-permute-start(f32[40,128]{1,0:T(8,128)S(1)} %pad_maximum_fusion.2.c0), channel_id=1, source_target_pairs={{0,4},{1,5},{2,6},{3,7},{4,0},{5,1},{6,2},{7,3},{8,12},{9,13},{10,... | collective-permute-start | bytes 61448 | tf_op jit(solution)/shard_map/ppermute | solution.py:244
  26.2 2.3 %collective-permute-start.2 = (f32[40,128]{1,0:T(8,128)S(1)}, f32[40,128]{1,0:T(8,128)S(1)}, u32[]{:S(2)}, u32[]{:S(2)}) collective-permute-start(f32[40,128]{1,0:T(8,128)S(1)} %pad_maximum_fusion.2.c0), channel_id=1, source_target_pairs={{0,6},{1,7},{2,0},{3,1},{4,2},{5,3},{6,4},{7,5},{8,14},{9,15},{10,... | collective-permute-start | bytes 61448 | tf_op jit(solution)/shard_map/ppermute | solution.py:244
  31.0 2.2 %collective-permute-done.4 = bf16[128,384]{1,0:T(8,128)(2,1)S(1)} collective-permute-done((bf16[128,384]{1,0:T(8,128)(2,1)S(1)}, bf16[128,384]{1,0:T(8,128)(2,1)S(1)}, u32[]{:S(2)}, u32[]{:S(2)}) %collective-permute-start.4) | collective-permute-done | bytes 98336 | tf_op jit(solution)/shard_map/ppermute | solution.py:244
  33.2 5.4 %collective-permute-start.6 = (bf16[256,384]{1,0:T(8,128)(2,1)S(1)}, bf16[256,384]{1,0:T(8,128)(2,1)S(1)}, u32[]{:S(2)}, u32[]{:S(2)}) collective-permute-start(bf16[256,384]{1,0:T(8,128)(2,1)S(1)} %constant_dynamic-update-slice_fusion.n0), channel_id=1, source_target_pairs={{0,64},{1,65},{2,66},{3,67},{4,68},{5,69},{6,70},{7,71},{8,72},{9,... | collective-permute-start | bytes 589832 | tf_op jit(solution)/shard_map/ppermute | solution.py:244
  40.1 1.7 %collective-permute-start.19 = (f32[128,128]{1,0:T(8,128)S(1)}, f32[128,128]{1,0:T(8,128)S(1)}, u32[]{:S(2)}, u32[]{:S(2)}) collective-permute-start(f32[128,128]{1,0:T(8,128)S(1)} %pad_maximum_fusion.near_ref), channel_id=1, source_target_pairs={{0,134},{1,135},{2,132},{3,133},{4,130},{5,131},{6,128},{7,129},{8... | collective-permute-start | bytes 196616 | tf_op jit(solution)/shard_map/ppermute | solution.py:244
  41.8 3.0 %collective-permute-done.19.far_ref = f32[128,128]{1,0:T(8,128)S(1)} collective-permute-done((f32[128,128]{1,0:T(8,128)S(1)}, f32[128,128]{1,0:T(8,128)S(1)}, u32[]{:S(2)}, u32[]{:S(2)}) %collective-permute-start.19) | collective-permute-done | bytes 65568 | tf_op jit(solution)/shard_map/ppermute | solution.py:244
  46.0 4.7 %collective-permute-start.20 = (bf16[128,1024]{1,0:T(8,128)(2,1)S(1)}, bf16[128,1024]{1,0:T(8,128)(2,1)S(1)}, u32[]{:S(2)}, u32[]{:S(2)}) collective-permute-start(bf16[128,1024]{1,0:T(8,128)(2,1)S(1)} %get-tuple-element.31), channel_id=1, source_target_pairs={{0,1},{1,0},{2,3},{3,2},{4,5},{5,4},{6,7},{7,6},{8,9},{9,8},{10,11... | collective-permute-start | bytes 786440 | tf_op jit(solution)/shard_map/ppermute | solution.py:244
  54.2 3.3 %collective-permute-start.12 = (f32[4,1024]{1,0:T(4,128)S(1)}, f32[4,1024]{1,0:T(4,128)S(1)}, u32[]{:S(2)}, u32[]{:S(2)}) collective-permute-start(f32[4,1024]{1,0:T(4,128)S(1)} %get-tuple-element.23), channel_id=1, source_target_pairs={{0,6},{1,7},{2,0},{3,1},{4,2},{5,3},{6,4},{7,5},{8,14},{9,15},{10,... | collective-permute-start | bytes 49160 | tf_op jit(solution)/shard_map/ppermute | solution.py:244
  61.1 1.3 %collective-permute-done.14.u3 = f32[4,1024]{1,0:T(4,128)S(1)} collective-permute-done((f32[4,1024]{1,0:T(4,128)S(1)}, f32[4,1024]{1,0:T(4,128)S(1)}, u32[]{:S(2)}, u32[]{:S(2)}) %collective-permute-start.14) | collective-permute-done | bytes 16416 | tf_op jit(solution)/shard_map/ppermute | solution.py:244
  62.3 6.0 %all-to-all-start.1 = ((bf16[16,8,1024]{2,1,0:T(8,128)(2,1)}), bf16[16,8,1024]{2,1,0:T(8,128)(2,1)S(1)}, u32[]{:S(2)}, u32[]{:S(2)}) async-start(bf16[16,8,1024]{2,1,0:T(8,128)(2,1)} %bitcast.11), calls=%async_computation.1 | async-start | bytes 524288 | tf_op jit(solution)/shard_map/all_to_all | solution.py:30
  70.0 2.4 %collective-permute-start.17 = (f32[4,1024]{1,0:T(4,128)S(1)}, f32[4,1024]{1,0:T(4,128)S(1)}, u32[]{:S(2)}, u32[]{:S(2)}) collective-permute-start(f32[4,1024]{1,0:T(4,128)S(1)} %get-tuple-element.29), channel_id=1, source_target_pairs={{0,6},{1,7},{2,0},{3,1},{4,2},{5,3},{6,4},{7,5},{8,14},{9,15},{10,... | collective-permute-start | bytes 49160 | tf_op jit(solution)/shard_map/ppermute | solution.py:244
  73.7 2.1 %all-to-all-done.1.old_ref = bf16[16,8,1024]{2,1,0:T(8,128)(2,1)S(1)} async-done(((bf16[16,8,1024]{2,1,0:T(8,128)(2,1)}), bf16[16,8,1024]{2,1,0:T(8,128)(2,1)S(1)}, u32[]{:S(2)}, u32[]{:S(2)}) %all-to-all-start.1) | async-done | bytes 262176 | tf_op jit(solution)/shard_map/all_to_all | solution.py:30
  77.0 1.5 %collective-permute-start.22 = (f32[16,1024]{1,0:T(8,128)S(1)}, f32[16,1024]{1,0:T(8,128)S(1)}, u32[]{:S(2)}, u32[]{:S(2)}) collective-permute-start(f32[16,1024]{1,0:T(8,128)S(1)} %shard_map.95.t0), channel_id=1, source_target_pairs={{0,4},{1,5},{2,6},{3,7},{4,0},{5,1},{6,2},{7,3},{8,12},{9,13},{10,... | collective-permute-start | bytes 196616 | tf_op jit(solution)/shard_map/ppermute | solution.py:244
  78.5 1.7 %collective-permute-start.23 = (f32[16,1024]{1,0:T(8,128)S(1)}, f32[16,1024]{1,0:T(8,128)S(1)}, u32[]{:S(2)}, u32[]{:S(2)}) collective-permute-start(f32[16,1024]{1,0:T(8,128)S(1)} %shard_map.95.t0), channel_id=1, source_target_pairs={{0,6},{1,7},{2,0},{3,1},{4,2},{5,3},{6,4},{7,5},{8,14},{9,15},{10,... | collective-permute-start | bytes 196616 | tf_op jit(solution)/shard_map/ppermute | solution.py:244
  80.3 1.7 %collective-permute-done.21.t1 = f32[16,1024]{1,0:T(8,128)S(1)} collective-permute-done((f32[16,1024]{1,0:T(8,128)S(1)}, f32[16,1024]{1,0:T(8,128)S(1)}, u32[]{:S(2)}, u32[]{:S(2)}) %collective-permute-start.21) | collective-permute-done | bytes 65568 | tf_op jit(solution)/shard_map/ppermute | solution.py:244
  83.4 3.3 %collective-permute-start.24 = (bf16[16,1024]{1,0:T(8,128)(2,1)S(1)}, bf16[16,1024]{1,0:T(8,128)(2,1)S(1)}, u32[]{:S(2)}, u32[]{:S(2)}) collective-permute-start(bf16[16,1024]{1,0:T(8,128)(2,1)S(1)} %shard_map.96), channel_id=1, source_target_pairs={{0,134},{1,135},{2,132},{3,133},{4,130},{5,131},{6,128},{7,129},{8... | collective-permute-start | bytes 98312 | tf_op jit(solution)/shard_map/ppermute | solution.py:244
  86.7 1.3 %collective-permute-done.24 = bf16[16,1024]{1,0:T(8,128)(2,1)S(1)} collective-permute-done((bf16[16,1024]{1,0:T(8,128)(2,1)S(1)}, bf16[16,1024]{1,0:T(8,128)(2,1)S(1)}, u32[]{:S(2)}, u32[]{:S(2)}) %collective-permute-start.24) | collective-permute-done | bytes 32800 | tf_op jit(solution)/shard_map/ppermute | solution.py:244
  88.1 14.2 %all_to_all.15 = bf16[16,16,1024]{2,1,0:T(8,128)(2,1)S(1)} all-to-all(bf16[16,16,1024]{2,1,0:T(8,128)(2,1)S(1)} %broadcast_in_dim.28), channel_id=1, replica_groups={{0,8,16,24,32,40,48,56,64,72,80,88,96,104,112,120},{1,9,17,25,33,41,49,..., dimensions={0} | all-to-all | bytes 1048576 | tf_op jit(solution)/shard_map/all_to_all | solution.py:30
  102.3 7.6 %collective-permute-start.25 = (bf16[16,16,1024]{2,1,0:T(8,128)(2,1)S(1)}, bf16[16,16,1024]{2,1,0:T(8,128)(2,1)S(1)}, u32[]{:S(2)}, u32[]{:S(2)}) collective-permute-start(bf16[16,16,1024]{2,1,0:T(8,128)(2,1)S(1)} %all_to_all.15), channel_id=1, source_target_pairs={{0,1},{1,0},{2,3},{3,2},{4,5},{5,4},{6,7},{7,6},{8,9},{9,8},{10,11... | collective-permute-start | bytes 1572872 | tf_op jit(solution)/shard_map/ppermute | solution.py:244
  110.0 1.5 %collective-permute-done.25 = bf16[16,16,1024]{2,1,0:T(8,128)(2,1)S(1)} collective-permute-done((bf16[16,16,1024]{2,1,0:T(8,128)(2,1)S(1)}, bf16[16,16,1024]{2,1,0:T(8,128)(2,1)S(1)}, u32[]{:S(2)}, u32[]{:S(2)}) %collective-permute-start.25) | collective-permute-done | bytes 524320 | tf_op jit(solution)/shard_map/ppermute | solution.py:244
  112.5 14.3 %shard_map.97 = bf16[256,1024]{1,0:T(8,128)(2,1)} custom-call(bf16[256,1024]{1,0:T(8,128)(2,1)S(1)} %get-tuple-element.34.old_ref, bf16[256,1024]{1,0:T(8,128)(2,1)S(1)} %get-tuple-element.33.fresh_ref, bf16[256,1024]{1,0:T(8,128)(2,1)S(1)} %copy-done.12), custom_call_target="tpu_custom_call" | custom-call | flops 2147483648 | bytes 1048576 | tf_op jit(solution)/shard_map/pallas_call | solution.py:44
  (88 shorter events, 23.1 us)
Async XLA Ops:
  1.9 21.0 %all-to-all-start = ((f32[32,1,128]{2,1,0:T(1,128)}), f32[32,1,128]{2,1,0:T(1,128)S(1)}, u32[]{:S(2)}, u32[]{:S(2)}) async-start(f32[32,1,128]{2,1,0:T(1,128)} %broadcast_in_dim.27), calls=%async_computation | async-start | bytes 32768 | tf_op jit(solution)/shard_map/all_to_all | solution.py:30
  10.5 17.9 %collective-permute-start.3 = (bf16[128,1024]{1,0:T(8,128)(2,1)}, bf16[128,1024]{1,0:T(8,128)(2,1)S(1)}, u32[]{:S(2)}, u32[]{:S(2)}) collective-permute-start(bf16[128,1024]{1,0:T(8,128)(2,1)} %param.12), channel_id=1, source_target_pairs={{0,0},{1,128},{2,32},{3,160},{4,64},{5,192},{6,96},{7,224},{8,8},{... | collective-permute-start | bytes 786440 | tf_op jit(solution)/shard_map/ppermute | solution.py:244
  23.0 6.1 %collective-permute-start = (f32[40,128]{1,0:T(8,128)S(1)}, f32[40,128]{1,0:T(8,128)S(1)}, u32[]{:S(2)}, u32[]{:S(2)}) collective-permute-start(f32[40,128]{1,0:T(8,128)S(1)} %pad_maximum_fusion.2.c0), channel_id=1, source_target_pairs={{0,2},{1,3},{2,4},{3,5},{4,6},{5,7},{6,0},{7,1},{8,10},{9,11},{10,... | collective-permute-start | bytes 61448 | tf_op jit(solution)/shard_map/ppermute | solution.py:244
  24.6 5.2 %collective-permute-start.1 = (f32[40,128]{1,0:T(8,128)S(1)}, f32[40,128]{1,0:T(8,128)S(1)}, u32[]{:S(2)}, u32[]{:S(2)}) collective-permute-start(f32[40,128]{1,0:T(8,128)S(1)} %pad_maximum_fusion.2.c0), channel_id=1, source_target_pairs={{0,4},{1,5},{2,6},{3,7},{4,0},{5,1},{6,2},{7,3},{8,12},{9,13},{10,... | collective-permute-start | bytes 61448 | tf_op jit(solution)/shard_map/ppermute | solution.py:244
  26.2 4.2 %collective-permute-start.2 = (f32[40,128]{1,0:T(8,128)S(1)}, f32[40,128]{1,0:T(8,128)S(1)}, u32[]{:S(2)}, u32[]{:S(2)}) collective-permute-start(f32[40,128]{1,0:T(8,128)S(1)} %pad_maximum_fusion.2.c0), channel_id=1, source_target_pairs={{0,6},{1,7},{2,0},{3,1},{4,2},{5,3},{6,4},{7,5},{8,14},{9,15},{10,... | collective-permute-start | bytes 61448 | tf_op jit(solution)/shard_map/ppermute | solution.py:244
  28.5 4.7 %collective-permute-start.4 = (bf16[128,384]{1,0:T(8,128)(2,1)S(1)}, bf16[128,384]{1,0:T(8,128)(2,1)S(1)}, u32[]{:S(2)}, u32[]{:S(2)}) collective-permute-start(bf16[128,384]{1,0:T(8,128)(2,1)S(1)} %get-tuple-element.21), channel_id=1, source_target_pairs={{0,134},{1,135},{2,132},{3,133},{4,130},{5,131},{6,128},{7,129},{8... | collective-permute-start | bytes 294920 | tf_op jit(solution)/shard_map/ppermute | solution.py:244
  33.2 17.7 %collective-permute-start.6 = (bf16[256,384]{1,0:T(8,128)(2,1)S(1)}, bf16[256,384]{1,0:T(8,128)(2,1)S(1)}, u32[]{:S(2)}, u32[]{:S(2)}) collective-permute-start(bf16[256,384]{1,0:T(8,128)(2,1)S(1)} %constant_dynamic-update-slice_fusion.n0), channel_id=1, source_target_pairs={{0,64},{1,65},{2,66},{3,67},{4,68},{5,69},{6,70},{7,71},{8,72},{9,... | collective-permute-start | bytes 589832 | tf_op jit(solution)/shard_map/ppermute | solution.py:244
  38.5 12.8 %collective-permute-start.7 = (bf16[256,384]{1,0:T(8,128)(2,1)S(1)}, bf16[256,384]{1,0:T(8,128)(2,1)S(1)}, u32[]{:S(2)}, u32[]{:S(2)}) collective-permute-start(bf16[256,384]{1,0:T(8,128)(2,1)S(1)} %constant_dynamic-update-slice_fusion.n0), channel_id=1, source_target_pairs={{0,96},{1,97},{2,98},{3,99},{4,100},{5,101},{6,102},{7,103},{8,104... | collective-permute-start | bytes 589832 | tf_op jit(solution)/shard_map/ppermute | solution.py:244
  38.9 12.5 %collective-permute-start.5 = (bf16[256,384]{1,0:T(8,128)(2,1)S(1)}, bf16[256,384]{1,0:T(8,128)(2,1)S(1)}, u32[]{:S(2)}, u32[]{:S(2)}) collective-permute-start(bf16[256,384]{1,0:T(8,128)(2,1)S(1)} %constant_dynamic-update-slice_fusion.n0), channel_id=1, source_target_pairs={{0,32},{1,33},{2,34},{3,35},{4,36},{5,37},{6,38},{7,39},{8,40},{9,... | collective-permute-start | bytes 589832 | tf_op jit(solution)/shard_map/ppermute | solution.py:244
  40.1 4.7 %collective-permute-start.19 = (f32[128,128]{1,0:T(8,128)S(1)}, f32[128,128]{1,0:T(8,128)S(1)}, u32[]{:S(2)}, u32[]{:S(2)}) collective-permute-start(f32[128,128]{1,0:T(8,128)S(1)} %pad_maximum_fusion.near_ref), channel_id=1, source_target_pairs={{0,134},{1,135},{2,132},{3,133},{4,130},{5,131},{6,128},{7,129},{8... | collective-permute-start | bytes 196616 | tf_op jit(solution)/shard_map/ppermute | solution.py:244
  46.0 13.6 %collective-permute-start.20 = (bf16[128,1024]{1,0:T(8,128)(2,1)S(1)}, bf16[128,1024]{1,0:T(8,128)(2,1)S(1)}, u32[]{:S(2)}, u32[]{:S(2)}) collective-permute-start(bf16[128,1024]{1,0:T(8,128)(2,1)S(1)} %get-tuple-element.31), channel_id=1, source_target_pairs={{0,1},{1,0},{2,3},{3,2},{4,5},{5,4},{6,7},{7,6},{8,9},{9,8},{10,11... | collective-permute-start | bytes 786440 | tf_op jit(solution)/shard_map/ppermute | solution.py:244
  54.2 6.2 %collective-permute-start.12 = (f32[4,1024]{1,0:T(4,128)S(1)}, f32[4,1024]{1,0:T(4,128)S(1)}, u32[]{:S(2)}, u32[]{:S(2)}) collective-permute-start(f32[4,1024]{1,0:T(4,128)S(1)} %get-tuple-element.23), channel_id=1, source_target_pairs={{0,6},{1,7},{2,0},{3,1},{4,2},{5,3},{6,4},{7,5},{8,14},{9,15},{10,... | collective-permute-start | bytes 49160 | tf_op jit(solution)/shard_map/ppermute | solution.py:244
  57.6 3.5 %collective-permute-start.13 = (f32[4,1024]{1,0:T(4,128)S(1)}, f32[4,1024]{1,0:T(4,128)S(1)}, u32[]{:S(2)}, u32[]{:S(2)}) collective-permute-start(f32[4,1024]{1,0:T(4,128)S(1)} %get-tuple-element.24), channel_id=1, source_target_pairs={{0,4},{1,5},{2,6},{3,7},{4,0},{5,1},{6,2},{7,3},{8,12},{9,13},{10,... | collective-permute-start | bytes 49160 | tf_op jit(solution)/shard_map/ppermute | solution.py:244
  57.9 4.5 %collective-permute-start.14 = (f32[4,1024]{1,0:T(4,128)S(1)}, f32[4,1024]{1,0:T(4,128)S(1)}, u32[]{:S(2)}, u32[]{:S(2)}) collective-permute-start(f32[4,1024]{1,0:T(4,128)S(1)} %get-tuple-element.25), channel_id=1, source_target_pairs={{0,2},{1,3},{2,4},{3,5},{4,6},{5,7},{6,0},{7,1},{8,10},{9,11},{10,... | collective-permute-start | bytes 49160 | tf_op jit(solution)/shard_map/ppermute | solution.py:244
  58.4 14.0 %collective-permute-start.18 = (bf16[128,1024]{1,0:T(8,128)(2,1)S(1)}, bf16[128,1024]{1,0:T(8,128)(2,1)S(1)}, u32[]{:S(2)}, u32[]{:S(2)}) collective-permute-start(bf16[128,1024]{1,0:T(8,128)(2,1)S(1)} %collective-permute-done.3.out_ref), channel_id=1, source_target_pairs={{0,1},{1,0},{2,3},{3,2},{4,5},{5,4},{6,7},{7,6},{8,9},{9,8},{10,11... | collective-permute-start | bytes 786440 | tf_op jit(solution)/shard_map/ppermute | solution.py:244
  62.3 13.5 %all-to-all-start.1 = ((bf16[16,8,1024]{2,1,0:T(8,128)(2,1)}), bf16[16,8,1024]{2,1,0:T(8,128)(2,1)S(1)}, u32[]{:S(2)}, u32[]{:S(2)}) async-start(bf16[16,8,1024]{2,1,0:T(8,128)(2,1)} %bitcast.11), calls=%async_computation.1 | async-start | bytes 524288 | tf_op jit(solution)/shard_map/all_to_all | solution.py:30
  69.0 4.4 %collective-permute-start.15 = (f32[4,1024]{1,0:T(4,128)S(1)}, f32[4,1024]{1,0:T(4,128)S(1)}, u32[]{:S(2)}, u32[]{:S(2)}) collective-permute-start(f32[4,1024]{1,0:T(4,128)S(1)} %get-tuple-element.27), channel_id=1, source_target_pairs={{0,2},{1,3},{2,4},{3,5},{4,6},{5,7},{6,0},{7,1},{8,10},{9,11},{10,... | collective-permute-start | bytes 49160 | tf_op jit(solution)/shard_map/ppermute | solution.py:244
  69.1 4.4 %collective-permute-start.16 = (f32[4,1024]{1,0:T(4,128)S(1)}, f32[4,1024]{1,0:T(4,128)S(1)}, u32[]{:S(2)}, u32[]{:S(2)}) collective-permute-start(f32[4,1024]{1,0:T(4,128)S(1)} %get-tuple-element.28), channel_id=1, source_target_pairs={{0,4},{1,5},{2,6},{3,7},{4,0},{5,1},{6,2},{7,3},{8,12},{9,13},{10,... | collective-permute-start | bytes 49160 | tf_op jit(solution)/shard_map/ppermute | solution.py:244
  70.0 3.8 %collective-permute-start.17 = (f32[4,1024]{1,0:T(4,128)S(1)}, f32[4,1024]{1,0:T(4,128)S(1)}, u32[]{:S(2)}, u32[]{:S(2)}) collective-permute-start(f32[4,1024]{1,0:T(4,128)S(1)} %get-tuple-element.29), channel_id=1, source_target_pairs={{0,6},{1,7},{2,0},{3,1},{4,2},{5,3},{6,4},{7,5},{8,14},{9,15},{10,... | collective-permute-start | bytes 49160 | tf_op jit(solution)/shard_map/ppermute | solution.py:244
  76.9 5.0 %collective-permute-start.21 = (f32[16,1024]{1,0:T(8,128)S(1)}, f32[16,1024]{1,0:T(8,128)S(1)}, u32[]{:S(2)}, u32[]{:S(2)}) collective-permute-start(f32[16,1024]{1,0:T(8,128)S(1)} %shard_map.95.t0), channel_id=1, source_target_pairs={{0,2},{1,3},{2,4},{3,5},{4,6},{5,7},{6,0},{7,1},{8,10},{9,11},{10,... | collective-permute-start | bytes 196616 | tf_op jit(solution)/shard_map/ppermute | solution.py:244
  77.0 4.9 %collective-permute-start.22 = (f32[16,1024]{1,0:T(8,128)S(1)}, f32[16,1024]{1,0:T(8,128)S(1)}, u32[]{:S(2)}, u32[]{:S(2)}) collective-permute-start(f32[16,1024]{1,0:T(8,128)S(1)} %shard_map.95.t0), channel_id=1, source_target_pairs={{0,4},{1,5},{2,6},{3,7},{4,0},{5,1},{6,2},{7,3},{8,12},{9,13},{10,... | collective-permute-start | bytes 196616 | tf_op jit(solution)/shard_map/ppermute | solution.py:244
  78.5 4.1 %collective-permute-start.23 = (f32[16,1024]{1,0:T(8,128)S(1)}, f32[16,1024]{1,0:T(8,128)S(1)}, u32[]{:S(2)}, u32[]{:S(2)}) collective-permute-start(f32[16,1024]{1,0:T(8,128)S(1)} %shard_map.95.t0), channel_id=1, source_target_pairs={{0,6},{1,7},{2,0},{3,1},{4,2},{5,3},{6,4},{7,5},{8,14},{9,15},{10,... | collective-permute-start | bytes 196616 | tf_op jit(solution)/shard_map/ppermute | solution.py:244
  83.4 4.6 %collective-permute-start.24 = (bf16[16,1024]{1,0:T(8,128)(2,1)S(1)}, bf16[16,1024]{1,0:T(8,128)(2,1)S(1)}, u32[]{:S(2)}, u32[]{:S(2)}) collective-permute-start(bf16[16,1024]{1,0:T(8,128)(2,1)S(1)} %shard_map.96), channel_id=1, source_target_pairs={{0,134},{1,135},{2,132},{3,133},{4,130},{5,131},{6,128},{7,129},{8... | collective-permute-start | bytes 98312 | tf_op jit(solution)/shard_map/ppermute | solution.py:244
  102.3 9.1 %collective-permute-start.25 = (bf16[16,16,1024]{2,1,0:T(8,128)(2,1)S(1)}, bf16[16,16,1024]{2,1,0:T(8,128)(2,1)S(1)}, u32[]{:S(2)}, u32[]{:S(2)}) collective-permute-start(bf16[16,16,1024]{2,1,0:T(8,128)(2,1)S(1)} %all_to_all.15), channel_id=1, source_target_pairs={{0,1},{1,0},{2,3},{3,2},{4,5},{5,4},{6,7},{7,6},{8,9},{9,8},{10,11... | collective-permute-start | bytes 1572872 | tf_op jit(solution)/shard_map/ppermute | solution.py:244
  (20 other events, 119.8 us)

commit v2 on v1

v2 whole, which is shorter than its diff:
```python
import jax
import jax.numpy as jnp
from jax import lax
from jax.experimental import pallas as pl
from jax.experimental.pallas import tpu as pltpu
from jax.sharding import PartitionSpec as P

HEAD = 64
WIDTH = 1024
CUT = 128
PLACES = 256
BF = jnp.bfloat16
F32 = jnp.float32
NT = (((1,), (1,)), ((), ()))
TN = (((0,), (0,)), ((), ()))


def columns(cores):
    return [
        [(zh * 4 + y) * 32 + x * 8 + zl * 2 + c for zh in range(2) for zl in range(4) for y in range(4) for c in cs]
        for x in range(4)
        for cs in ([(0, 1)] if cores == 2 else [(0,), (1,)])
    ]


def exchange(x, cores):
    return lax.all_to_all(
        x, ("grp", "dev"), split_axis=0, concat_axis=0, tiled=True, axis_index_groups=columns(cores)
    )


def spread(x, cores):
    return exchange(jnp.broadcast_to(x[None], (32 * cores, *x.shape)), cores)


def after(x, *others):
    return lax.optimization_barrier((x, *others))[0]


def call(kernel, out, flops, *args, where=None, scratch=(), hbm=(), mib=12):
    vmem = pl.BlockSpec(memory_space=pltpu.VMEM)
    first = [] if where is None else [where]
    return pl.pallas_call(
        kernel,
        out_shape=out,
        in_specs=[pl.BlockSpec(memory_space=pltpu.SMEM)] * len(first)
        + [pl.BlockSpec(memory_space=pltpu.HBM) if i in hbm else vmem for i in range(len(args))],
        out_specs=jax.tree.map(lambda _: vmem, out),
        scratch_shapes=list(scratch),
        compiler_params=pltpu.CompilerParams(vmem_limit_bytes=mib * 2**20),
        cost_estimate=pl.CostEstimate(flops=flops, bytes_accessed=2**20, transcendentals=0),
    )(*first, *args)


def shape(dims, kind):
    return jax.ShapeDtypeStruct(dims, kind)


def dot(a, b, dims=(((1,), (0,)), ((), ()))):
    return lax.dot_general(a, b, dims, preferred_element_type=F32)


def exact(a, b):
    return jnp.dot(a, b, preferred_element_type=F32, precision=lax.Precision.HIGHEST)


def terms(x):
    high = x.astype(BF)
    rest = x - high.astype(F32)
    mid = rest.astype(BF)
    return high, mid, (rest - mid.astype(F32)).astype(BF)


def head_mask(rows):
    row = lax.broadcasted_iota(jnp.int32, (rows, 4 * HEAD), 0)
    col = lax.broadcasted_iota(jnp.int32, (rows, 4 * HEAD), 1)
    return lax.rem(row, 4) == lax.div(col, HEAD)


def cut_kernel(where, query_ref, keyval_ref, own_ref):
    block = 4 * where[3] + where[2]
    at = pl.ds(pl.multiple_of(block * CUT, CUT), CUT)
    own_ref[:, :CUT] = query_ref[:, at]
    own_ref[:, CUT : 2 * CUT] = keyval_ref[:, at]
    own_ref[:, 2 * CUT :] = keyval_ref[:, pl.ds(pl.multiple_of(block * CUT + WIDTH, CUT), CUT)]


def pick_kernel(where, info_ref, bank_ref, rows_ref):
    n = bank_ref.shape[0]
    number = lax.broadcasted_iota(jnp.int32, (PLACES, n), 1).astype(F32)
    own, slot, place = [info_ref[:, i : i + 1] for i in range(3)]
    a = jnp.where((place == number) & (own == where[6].astype(F32)), 1.0, 0.0).astype(BF)
    b = jnp.where(slot == number, 1.0, 0.0).astype(BF)
    rows_ref[...] = dot(dot(a, b, TN).astype(BF), bank_ref[...]).astype(BF)


def row_blocks(where):
    zh, y = where[0], where[1]
    for k in range(4):
        yk = lax.rem(y + 4 - k, 4)
        for h in range(2):
            at = ((zh if h == 0 else 1 - zh) * 4 + yk) * CUT
            yield k, slice(h * CUT, (h + 1) * CUT), pl.ds(pl.multiple_of(at, CUT), CUT)


def encode_kernel(
    where, h0, h1, h2, h2b, h3, n0, n1, n2, n3, f0, f1, f2, f3, out_ref, out2_ref, part_ref, w_ref
):
    near, far = (n0, n1, n2, n3), (f0, f1, f2, f3)
    for k, rows, features in row_blocks(where):
        for i in range(3):
            cols = slice(i * CUT, (i + 1) * CUT)
            w_ref[features, 2 * i * CUT : (2 * i + 1) * CUT] = near[k][rows, cols]
            w_ref[features, (2 * i + 1) * CUT : (2 * i + 2) * CUT] = far[k][rows, cols]
    four = 4 * HEAD
    mask = head_mask(4)
    contexts = []
    for refs in ((h0,), (h1,), (h2, h2b), (h3,)):
        x = jnp.concatenate([r[...] for r in refs], axis=0)
        keyval = dot(x, w_ref[:, four:]).astype(BF)
        query = (0.125 * dot(x[0:16], w_ref[:, :four])[0:1]).astype(BF).astype(F32)
        query = jnp.where(mask, jnp.broadcast_to(query, (4, four)), 0.0).astype(BF)
        scores = dot(query, keyval[:, :four], NT)
        e = jnp.exp(scores - jnp.max(scores, axis=1, keepdims=True))
        probs = (e / jnp.sum(e, axis=1, keepdims=True)).astype(BF)
        context = jnp.where(mask, dot(probs, keyval[:, four:]), 0.0)
        contexts.append(jnp.sum(context, axis=0, keepdims=True))
    context = jnp.concatenate(contexts, axis=0).astype(BF)
    part = dot(context[:, :CUT], out_ref[...]) + dot(context[:, CUT:], out2_ref[...])
    for k in range(4):
        row = part[k : k + 1]
        if k == 0:
            row = row + h0[0:1, :].astype(F32)
        part_ref[pl.ds(lax.rem(where[2] + 4 - k, 4), 1), :] = row


def pack_kernel(part_ref, old_ref, both_ref):
    both_ref[...] = jnp.concatenate([part_ref[...], jnp.sum(old_ref[...].astype(F32), axis=0)], axis=0)


def norm_kernel(t0, t1, t2, t3, gain_ref, bias_ref, rows_ref):
    total = (t0[...] + t1[...]) + (t2[...] + t3[...])
    joined = total[0:4]
    center = joined - jnp.mean(joined, axis=-1, keepdims=True)
    var = jnp.mean(center * center, axis=-1, keepdims=True)
    normed = center / jnp.sqrt(var + 1e-05) * gain_ref[...] + bias_ref[...]
    fresh = normed / jnp.sqrt(jnp.mean(normed * normed, axis=-1, keepdims=True) + 1e-06)
    rows_ref[...] = jnp.concatenate([fresh, total[4:8]], axis=0).astype(BF)


def product(a, b):
    a1, a2, _ = terms(a)
    b1, b2, _ = terms(b)
    return dot(a2, b1) + dot(a1, b2) + dot(a1, b1)


def update_kernel(here_ref, there_ref, bank_ref, out_ref):
    half = here_ref.shape[0] // 2
    row = lax.broadcasted_iota(jnp.int32, (half, 2 * half), 0)
    col = lax.broadcasted_iota(jnp.int32, (half, 2 * half), 1)
    at = lax.div(row, 4) * 8 + lax.rem(row, 4)

    def take(first):
        pick = jnp.where(col == at + first, 1.0, 0.0).astype(BF)
        return jnp.concatenate([dot(pick, ref[...]).astype(BF) for ref in (here_ref, there_ref)], axis=0)

    old, fresh = take(4), take(0)
    n = 2 * half
    rows = lax.broadcasted_iota(jnp.int32, (n, n), 0)
    cols = lax.broadcasted_iota(jnp.int32, (n, n), 1)
    eye = jnp.where(rows == cols, 1.0, 0.0).astype(F32)
    ridge = 0.25 * n
    a = dot(old, old, NT) + ridge * eye
    norm = jnp.max(jnp.sum(jnp.abs(a), axis=1, keepdims=True))
    c = 2.0 / (ridge + norm)
    r = eye - c * a
    x = c * (eye + r)

    def size(r):
        return jnp.max(jnp.sum(jnp.abs(r), axis=1, keepdims=True))

    def step(times, state):
        t, _, x, r = state
        both = times(jnp.concatenate([x, r], axis=0), r)
        r = both[n:]
        return 2.0 * t, size(r), x + both[:n], r

    def more(state):
        return (state[0] < 9.0) & (state[1] > 1e-4)

    r = exact(r, r)
    state = (2.0 * c * ridge, size(r), x, r)
    state = lax.while_loop(lambda s: more(s) & (norm < 512.0 * ridge), lambda s: step(product, s), state)
    x = lax.while_loop(more, lambda s: step(exact, s), state)[2]

    def refine(state):
        i, _, x = state
        e = eye - exact(a, x)
        return i + 1, jnp.sum(e * e), x + exact(x, e)

    _, _, x = lax.while_loop(
        lambda s: (s[0] == 0) | ((s[1] > 1e-7) & (s[0] < 4)), refine, (jnp.int32(0), jnp.float32(1.0), x)
    )
    high, mid, low = terms(x)
    z1, z2, z3 = terms(dot(low, fresh) + dot(mid, fresh) + dot(high, fresh))
    adapter = (dot(old, z3, TN) + dot(old, z2, TN) + dot(old, z1, TN)).astype(BF)
    out_ref[...] = dot(bank_ref[...], adapter).astype(BF)


def shift(x, move):
    perm = []
    for i in range(256):
        zh, y, xx, zl, c = i // 128, i // 32 % 4, i // 8 % 4, i // 2 % 4, i % 2
        zh, y, xx, zl, c = move(zh, y, xx, zl, c)
        perm.append((i, (((zh % 2) * 4 + y % 4) * 4 + xx % 4) * 8 + (zl % 4) * 2 + c % 2))
    return lax.ppermute(x, ("grp", "dev"), perm)


def along_y(x, k):
    return shift(x, lambda zh, y, xx, zl, c: (zh, y + k, xx, zl, c)) if k % 4 else x


def along_x(x, k):
    return shift(x, lambda zh, y, xx, zl, c: (zh, y, xx + k, zl, c)) if k % 4 else x


def other_core(x):
    return shift(x, lambda zh, y, xx, zl, c: (zh, y, xx, zl, c + 1))


def mirror(x):
    return shift(x, lambda zh, y, xx, zl, c: (zh + 1, y, xx, 3 - zl, c))


def local(hidden_in, w_query, w_keyval, w_out, ln_gain, ln_bias, bank, owner, slot):
    hidden = hidden_in[0]
    grp, dev = lax.axis_index("grp"), lax.axis_index("dev")
    zh, y, x, zl, c = grp // 4, grp % 4, dev // 8, dev // 2 % 4, dev % 2
    where = jnp.stack([zh, y, x, c, owner[0], slot[0], grp * 32 + dev])

    h1, h3 = along_x(hidden, 1), along_x(hidden, 3)
    h2, h2b = along_x(h1[:128], 1), along_x(h3[128:], 3)

    place = (((zh * 4 + zl) * 4 + y) * 2 + c) * 4 + x
    lane = lax.broadcasted_iota(jnp.int32, (PLACES, 1, 128), 2)
    info = jnp.where(lane == 0, where[4], jnp.where(lane == 1, where[5], place)).astype(F32)
    info = lax.all_to_all(info, ("grp", "dev"), split_axis=0, concat_axis=0, tiled=True).reshape(PLACES, 128)
    rows = call(pick_kernel, shape((PLACES, WIDTH), BF), 2**27, info, bank, where=where)

    own = call(cut_kernel, shape((CUT, 3 * CUT), BF), 2**10, w_query, w_keyval, where=where)
    out1 = shift(w_out, lambda zh, y, xx, zl, c: (c, xx, y, zl if c == zh else 3 - zl, zh))
    own = after(jnp.concatenate([own, mirror(own)], axis=0), h1, h3)
    out2 = other_core(out1)
    near = [along_y(own, k) for k in range(4)]
    near[0] = after(near[0], *near[1:], out1, h2, h2b)
    far = [other_core(w) for w in near]

    rows = exchange(after(rows, *near[1:]).reshape(64, 4, WIDTH), 2)

    part = call(
        encode_kernel,
        shape((4, WIDTH), F32),
        2**30,
        hidden,
        h1,
        h2,
        h2b,
        h3,
        *near,
        *far,
        out1,
        out2,
        where=where,
        scratch=[pltpu.VMEM((WIDTH, 6 * CUT), BF)],
        mib=24,
    )
    both = call(pack_kernel, shape((8, WIDTH), F32), 2**18, part, rows)
    both = [along_x(both, k) for k in range(4)]
    mine = call(
        norm_kernel, shape((8, WIDTH), BF), 2**14, *both, ln_gain.reshape(1, -1), ln_bias.reshape(1, -1)
    )
    here = spread(mine, 1)
    there = other_core(here)
    return call(
        update_kernel,
        shape(bank.shape, BF),
        2**31,
        here.reshape(256, WIDTH),
        there.reshape(256, WIDTH),
        bank,
        mib=32,
    )


def solution(mesh):
    in_specs = (
        P(("grp", "dev"), None, None),
        P("grp", None),
        P("grp", None),
        P("grp", None),
        P(),
        P(),
        P(("grp", "dev"), None),
        P(("grp", "dev")),
        P(("grp", "dev")),
    )
    out_specs = P(("grp", "dev"), None)
    return jax.shard_map(local, mesh=mesh, in_specs=in_specs, out_specs=out_specs, check_vma=False)
```

time: 127 us -> 130 us (1.024)
  starting transfers between devices: 66.8 us -> 58.2 us
  blocking collectives: 14.2 us -> 21.5 us
  waiting for transfers between devices: 17.1 us -> 22.9 us
  local copies, waits for them, and re-layouts: 5.73 us -> 3.2 us
  Pallas kernels: 19.9 us -> 21.3 us
    ppermute x26 -> x18, starting transfers between devices: 52.2 us -> 38.1 us  [shift(): return lax.ppermute(x, ('grp', 'dev'), perm)]
    all_to_all x0 -> x1, starting transfers between devices: none -> 9.62 us  [local(): lax.all_to_all(info, ('grp', 'dev'), split_axis=0, concat_axis=0, tiled=T...]
    all_to_all x0 -> x1, waiting for transfers between devices: none -> 7.61 us  [local(): lax.all_to_all(info, ('grp', 'dev'), split_axis=0, concat_axis=0, tiled=T...]
    all_to_all x1, blocking collectives: 14.2 us -> 21.5 us  [exchange(): lax.all_to_all(x, ('grp', 'dev'), split_axis=0, concat_axis=0, tiled=True...]
    all_to_all x2 -> x1, starting transfers between devices: 14.6 us -> 10.5 us  [exchange(): lax.all_to_all(x, ('grp', 'dev'), split_axis=0, concat_axis=0, tiled=True...]
    unnamed x28 -> x14, local copies, waits for them, and re-layouts: 4.84 us -> 2.02 us
    all_to_all x2 -> x1, waiting for transfers between devices: 2.13 us -> 0.01 us  [exchange(): lax.all_to_all(x, ('grp', 'dev'), split_axis=0, concat_axis=0, tiled=True...]
    pallas_call x7 -> x6, Pallas kernels: 19.9 us -> 21.3 us  [call(): pl.pallas_call(kernel, out_shape=out, in_specs=[pl.BlockSpec(memory_space...]
  transfers between devices with their start and end apart: 28 -> 20, of which waited for: 15 -> 7; matrix products, arithmetic and copies ran while one was open for 1% -> 1% of each run, Pallas kernels for 3% -> 5%
where the time goes in v2:
time: 130 us; the launch traced here: 129 us
  starting transfers between devices  58.2 us (45%)
  waiting for transfers between devices  22.9 us (18%)
  blocking collectives  21.5 us (17%)
  Pallas kernels  21.3 us (16%)
  local copies, waits for them, and re-layouts  3.2 us (2%)
  between operations  1.51 us (1%)
    ppermute x18, starting transfers between devices, shift(): return lax.ppermute(x, ('grp', 'dev'), perm)  38.1 us
    all_to_all x1, blocking collectives, exchange(): lax.all_to_all(x, ('grp', 'dev'), split_axis=0, concat_axis=0, tiled=True...  21.5 us
    pallas_call x6, Pallas kernels, call(): pl.pallas_call(kernel, out_shape=out, in_specs=[pl.BlockSpec(memory_space...  21.3 us
    ppermute x18, waiting for transfers between devices, shift(): return lax.ppermute(x, ('grp', 'dev'), perm)  15.2 us
    all_to_all x1, starting transfers between devices, exchange(): lax.all_to_all(x, ('grp', 'dev'), split_axis=0, concat_axis=0, tiled=True...  10.5 us
    all_to_all x1, starting transfers between devices, local(): lax.all_to_all(info, ('grp', 'dev'), split_axis=0, concat_axis=0, tiled=T...  9.62 us
    all_to_all x1, waiting for transfers between devices, local(): lax.all_to_all(info, ('grp', 'dev'), split_axis=0, concat_axis=0, tiled=T...  7.61 us
  transfers between devices with their start and end apart: 20, of which 7 were waited for; matrix products, arithmetic and copies ran while one was open for 1% of the time, Pallas kernels for 5%

profile of v2, /device:TPU:1, one launch (start us, length us, event | category | flops | bytes accessed | tf_op | source)
XLA Modules:
  0.0 129.3 jit_solution(7017055507417057493)
XLA Ops:
  0.0 2.0 %collective-permute-start = (bf16[256,1024]{1,0:T(8,128)(2,1)}, bf16[256,1024]{1,0:T(8,128)(2,1)S(1)}, u32[]{:S(2)}, u32[]{:S(2)}) collective-permute-start(bf16[256,1024]{1,0:T(8,128)(2,1)} %bitcast.15), channel_id=1, source_target_pairs={{0,8},{1,9},{2,10},{3,11},{4,12},{5,13},{6,14},{7,15},{8,16},{9,17... | collective-permute-start | bytes 1572872 | tf_op jit(solution)/shard_map/ppermute | solution.py:216
  2.0 1.3 collective-permute-start.2
  4.7 1.0 copy-done.1
  7.3 5.9 %collective-permute-start.4 = (bf16[128,384]{1,0:T(8,128)(2,1)S(1)}, bf16[128,384]{1,0:T(8,128)(2,1)S(1)}, u32[]{:S(2)}, u32[]{:S(2)}) collective-permute-start(bf16[128,384]{1,0:T(8,128)(2,1)S(1)} %shard_map.91), channel_id=1, source_target_pairs={{0,134},{1,135},{2,132},{3,133},{4,130},{5,131},{6,128},{7,129},{8... | collective-permute-start | bytes 294920 | tf_op jit(solution)/shard_map/ppermute | solution.py:216
  13.9 9.6 %all-to-all-start = ((f32[256,1,128]{2,1,0:T(1,128)}), f32[256,1,128]{2,1,0:T(1,128)S(1)}, u32[]{:S(2)}, u32[]{:S(2)}) async-start(f32[256,1,128]{2,1,0:T(1,128)} %fusion), calls=%async_computation | async-start | bytes 262144 | tf_op jit(solution)/shard_map/all_to_all | solution.py:247
  23.6 1.5 %collective-permute-start.5 = (bf16[256,384]{1,0:T(8,128)(2,1)S(1)}, bf16[256,384]{1,0:T(8,128)(2,1)S(1)}, u32[]{:S(2)}, u32[]{:S(2)}) collective-permute-start(bf16[256,384]{1,0:T(8,128)(2,1)S(1)} %pad_maximum_fusion.n0), channel_id=1, source_target_pairs={{0,32},{1,33},{2,34},{3,35},{4,36},{5,37},{6,38},{7,39},{8,40},{9,... | collective-permute-start | bytes 589832 | tf_op jit(solution)/shard_map/ppermute | solution.py:216
  25.1 2.4 %collective-permute-start.6 = (bf16[256,384]{1,0:T(8,128)(2,1)S(1)}, bf16[256,384]{1,0:T(8,128)(2,1)S(1)}, u32[]{:S(2)}, u32[]{:S(2)}) collective-permute-start(bf16[256,384]{1,0:T(8,128)(2,1)S(1)} %pad_maximum_fusion.n0), channel_id=1, source_target_pairs={{0,64},{1,65},{2,66},{3,67},{4,68},{5,69},{6,70},{7,71},{8,72},{9,... | collective-permute-start | bytes 589832 | tf_op jit(solution)/shard_map/ppermute | solution.py:216
  27.5 1.1 collective-permute-start.7
  28.6 7.6 %all-to-all-done = f32[256,1,128]{2,1,0:T(1,128)S(1)} async-done(((f32[256,1,128]{2,1,0:T(1,128)}), f32[256,1,128]{2,1,0:T(1,128)S(1)}, u32[]{:S(2)}, u32[]{:S(2)}) %all-to-all-start) | async-done | bytes 131104 | tf_op jit(solution)/shard_map/all_to_all | solution.py:247
  36.2 1.1 shard_map.93
  38.7 10.5 %all-to-all-start.1 = ((bf16[64,4,1024]{2,1,0:T(4,128)(2,1)}), bf16[64,4,1024]{2,1,0:T(4,128)(2,1)S(1)}, u32[]{:S(2)}, u32[]{:S(2)}) async-start(bf16[64,4,1024]{2,1,0:T(4,128)(2,1)} %reshape.60), calls=%async_computation.1 | async-start | bytes 1048576 | tf_op jit(solution)/shard_map/all_to_all | solution.py:27
  49.2 5.1 %collective-permute-start.8 = (bf16[128,1024]{1,0:T(8,128)(2,1)S(1)}, bf16[128,1024]{1,0:T(8,128)(2,1)S(1)}, u32[]{:S(2)}, u32[]{:S(2)}) collective-permute-start(bf16[128,1024]{1,0:T(8,128)(2,1)S(1)} %copy-done.6), channel_id=1, source_target_pairs={{0,0},{1,134},{2,2},{3,132},{4,4},{5,130},{6,6},{7,128},{8,32},{9,... | collective-permute-start | bytes 786440 | tf_op jit(solution)/shard_map/ppermute | solution.py:216
  54.4 2.2 %collective-permute-start.1 = (bf16[128,1024]{1,0:T(8,128)(2,1)S(1)}, bf16[128,1024]{1,0:T(8,128)(2,1)S(1)}, u32[]{:S(2)}, u32[]{:S(2)}) collective-permute-start(bf16[128,1024]{1,0:T(8,128)(2,1)S(1)} %slice.8), channel_id=1, source_target_pairs={{0,8},{1,9},{2,10},{3,11},{4,12},{5,13},{6,14},{7,15},{8,16},{9,17... | collective-permute-start | bytes 786440 | tf_op jit(solution)/shard_map/ppermute | solution.py:216
  56.6 2.5 %collective-permute-start.3 = (bf16[128,1024]{1,0:T(8,128)(2,1)S(1)}, bf16[128,1024]{1,0:T(8,128)(2,1)S(1)}, u32[]{:S(2)}, u32[]{:S(2)}) collective-permute-start(bf16[128,1024]{1,0:T(8,128)(2,1)S(1)} %slice.9), channel_id=1, source_target_pairs={{0,24},{1,25},{2,26},{3,27},{4,28},{5,29},{6,30},{7,31},{8,0},{9,1... | collective-permute-start | bytes 786440 | tf_op jit(solution)/shard_map/ppermute | solution.py:216
  59.2 10.9 %collective-permute-done.8.out_ref = bf16[128,1024]{1,0:T(8,128)(2,1)S(1)} collective-permute-done((bf16[128,1024]{1,0:T(8,128)(2,1)S(1)}, bf16[128,1024]{1,0:T(8,128)(2,1)S(1)}, u32[]{:S(2)}, u32[]{:S(2)}) %collective-permute-start.8) | collective-permute-done | bytes 262176 | tf_op jit(solution)/shard_map/ppermute | solution.py:216
  70.5 5.0 %collective-permute-start.12 = (bf16[256,384]{1,0:T(8,128)(2,1)S(1)}, bf16[256,384]{1,0:T(8,128)(2,1)S(1)}, u32[]{:S(2)}, u32[]{:S(2)}) collective-permute-start(bf16[256,384]{1,0:T(8,128)(2,1)S(1)} %collective-permute-done.7.n3), channel_id=1, source_target_pairs={{0,1},{1,0},{2,3},{3,2},{4,5},{5,4},{6,7},{7,6},{8,9},{9,8},{10,11... | collective-permute-start | bytes 589832 | tf_op jit(solution)/shard_map/ppermute | solution.py:216
  77.0 4.4 %shard_map.92.part_ref = f32[4,1024]{1,0:T(4,128)S(1)} custom-call(s32[7]{0:T(128)S(1)} %stack.23.where, bf16[256,1024]{1,0:T(8,128)(2,1)S(1)} %bitcast.17, bf16[256,1024]{1,0:T(8,128)(2,1)S(1)} %collective-permute-done.h1, bf16[128,1024]{1,0:T(8,128)(2,1)S(1)} %collective-permute-done.1.h2, bf16[128,1024]{1,0:T(8,128)(2,1)S(1)} %collective-permute-done.3.h2b, ...), custom_call_target="tpu_custom_call" | custom-call | flops 1073741824 | bytes 1048576 | tf_op jit(solution)/shard_map/pallas_call | solution.py:43
  81.8 2.8 %collective-permute-start.15 = (f32[8,1024]{1,0:T(8,128)S(1)}, f32[8,1024]{1,0:T(8,128)S(1)}, u32[]{:S(2)}, u32[]{:S(2)}) collective-permute-start(f32[8,1024]{1,0:T(8,128)S(1)} %shard_map.94.t0), channel_id=1, source_target_pairs={{0,16},{1,17},{2,18},{3,19},{4,20},{5,21},{6,22},{7,23},{8,24},{9,... | collective-permute-start | bytes 98312 | tf_op jit(solution)/shard_map/ppermute | solution.py:216
  84.6 2.0 %collective-permute-start.16 = (f32[8,1024]{1,0:T(8,128)S(1)}, f32[8,1024]{1,0:T(8,128)S(1)}, u32[]{:S(2)}, u32[]{:S(2)}) collective-permute-start(f32[8,1024]{1,0:T(8,128)S(1)} %shard_map.94.t0), channel_id=1, source_target_pairs={{0,24},{1,25},{2,26},{3,27},{4,28},{5,29},{6,30},{7,31},{8,0},{9,1... | collective-permute-start | bytes 98312 | tf_op jit(solution)/shard_map/ppermute | solution.py:216
  86.6 1.1 collective-permute-done.16.t3
  88.0 21.5 %all_to_all.15 = bf16[32,8,1024]{2,1,0:T(8,128)(2,1)S(1)} all-to-all(bf16[32,8,1024]{2,1,0:T(8,128)(2,1)S(1)} %broadcast_in_dim.21), channel_id=1, replica_groups={{0,32,64,96,2,34,66,98,4,36,68,100,6,38,70,102,128,160,192,224,130,162,..., dimensions={0} | all-to-all | bytes 1048576 | tf_op jit(solution)/shard_map/all_to_all | solution.py:27
  109.6 3.6 %collective-permute-start.17 = (bf16[32,8,1024]{2,1,0:T(8,128)(2,1)S(1)}, bf16[32,8,1024]{2,1,0:T(8,128)(2,1)S(1)}, u32[]{:S(2)}, u32[]{:S(2)}) collective-permute-start(bf16[32,8,1024]{2,1,0:T(8,128)(2,1)S(1)} %all_to_all.15), channel_id=1, source_target_pairs={{0,1},{1,0},{2,3},{3,2},{4,5},{5,4},{6,7},{7,6},{8,9},{9,8},{10,11... | collective-permute-start | bytes 1572872 | tf_op jit(solution)/shard_map/ppermute | solution.py:216
  113.2 1.5 %collective-permute-done.17 = bf16[32,8,1024]{2,1,0:T(8,128)(2,1)S(1)} collective-permute-done((bf16[32,8,1024]{2,1,0:T(8,128)(2,1)S(1)}, bf16[32,8,1024]{2,1,0:T(8,128)(2,1)S(1)}, u32[]{:S(2)}, u32[]{:S(2)}) %collective-permute-start.17) | collective-permute-done | bytes 524320 | tf_op jit(solution)/shard_map/ppermute | solution.py:216
  114.7 14.6 %shard_map.96 = bf16[256,1024]{1,0:T(8,128)(2,1)} custom-call(bf16[256,1024]{1,0:T(8,128)(2,1)S(1)} %bitcast.19, bf16[256,1024]{1,0:T(8,128)(2,1)S(1)} %bitcast.22, bf16[256,1024]{1,0:T(8,128)(2,1)S(1)} %copy-done.2), custom_call_target="tpu_custom_call" | custom-call | flops 2147483648 | bytes 1048576 | tf_op jit(solution)/shard_map/pallas_call | solution.py:43
  (46 shorter events, 6.4 us)
Async XLA Ops:
  0.0 23.6 %collective-permute-start = (bf16[256,1024]{1,0:T(8,128)(2,1)}, bf16[256,1024]{1,0:T(8,128)(2,1)S(1)}, u32[]{:S(2)}, u32[]{:S(2)}) collective-permute-start(bf16[256,1024]{1,0:T(8,128)(2,1)} %bitcast.15), channel_id=1, source_target_pairs={{0,8},{1,9},{2,10},{3,11},{4,12},{5,13},{6,14},{7,15},{8,16},{9,17... | collective-permute-start | bytes 1572872 | tf_op jit(solution)/shard_map/ppermute | solution.py:216
  2.0 21.5 %collective-permute-start.2 = (bf16[256,1024]{1,0:T(8,128)(2,1)}, bf16[256,1024]{1,0:T(8,128)(2,1)S(1)}, u32[]{:S(2)}, u32[]{:S(2)}) collective-permute-start(bf16[256,1024]{1,0:T(8,128)(2,1)} %bitcast.16), channel_id=1, source_target_pairs={{0,24},{1,25},{2,26},{3,27},{4,28},{5,29},{6,30},{7,31},{8,0},{9,1... | collective-permute-start | bytes 1572872 | tf_op jit(solution)/shard_map/ppermute | solution.py:216
  7.3 29.0 %copy-start.2 = (bf16[256,1024]{1,0:T(8,128)(2,1)S(1)}, bf16[256,1024]{1,0:T(8,128)(2,1)}, u32[]{:S(2)}) copy-start(bf16[256,1024]{1,0:T(8,128)(2,1)} %bank_ref.3) | copy-start | bytes 1572868
  7.3 16.2 %collective-permute-start.4 = (bf16[128,384]{1,0:T(8,128)(2,1)S(1)}, bf16[128,384]{1,0:T(8,128)(2,1)S(1)}, u32[]{:S(2)}, u32[]{:S(2)}) collective-permute-start(bf16[128,384]{1,0:T(8,128)(2,1)S(1)} %shard_map.91), channel_id=1, source_target_pairs={{0,134},{1,135},{2,132},{3,133},{4,130},{5,131},{6,128},{7,129},{8... | collective-permute-start | bytes 294920 | tf_op jit(solution)/shard_map/ppermute | solution.py:216
  13.9 22.3 %all-to-all-start = ((f32[256,1,128]{2,1,0:T(1,128)}), f32[256,1,128]{2,1,0:T(1,128)S(1)}, u32[]{:S(2)}, u32[]{:S(2)}) async-start(f32[256,1,128]{2,1,0:T(1,128)} %fusion), calls=%async_computation | async-start | bytes 262144 | tf_op jit(solution)/shard_map/all_to_all | solution.py:247
  23.6 13.8 %collective-permute-start.5 = (bf16[256,384]{1,0:T(8,128)(2,1)S(1)}, bf16[256,384]{1,0:T(8,128)(2,1)S(1)}, u32[]{:S(2)}, u32[]{:S(2)}) collective-permute-start(bf16[256,384]{1,0:T(8,128)(2,1)S(1)} %pad_maximum_fusion.n0), channel_id=1, source_target_pairs={{0,32},{1,33},{2,34},{3,35},{4,36},{5,37},{6,38},{7,39},{8,40},{9,... | collective-permute-start | bytes 589832 | tf_op jit(solution)/shard_map/ppermute | solution.py:216
  25.1 12.7 %collective-permute-start.6 = (bf16[256,384]{1,0:T(8,128)(2,1)S(1)}, bf16[256,384]{1,0:T(8,128)(2,1)S(1)}, u32[]{:S(2)}, u32[]{:S(2)}) collective-permute-start(bf16[256,384]{1,0:T(8,128)(2,1)S(1)} %pad_maximum_fusion.n0), channel_id=1, source_target_pairs={{0,64},{1,65},{2,66},{3,67},{4,68},{5,69},{6,70},{7,71},{8,72},{9,... | collective-permute-start | bytes 589832 | tf_op jit(solution)/shard_map/ppermute | solution.py:216
  27.5 10.2 %collective-permute-start.7 = (bf16[256,384]{1,0:T(8,128)(2,1)S(1)}, bf16[256,384]{1,0:T(8,128)(2,1)S(1)}, u32[]{:S(2)}, u32[]{:S(2)}) collective-permute-start(bf16[256,384]{1,0:T(8,128)(2,1)S(1)} %pad_maximum_fusion.n0), channel_id=1, source_target_pairs={{0,96},{1,97},{2,98},{3,99},{4,100},{5,101},{6,102},{7,103},{8,104... | collective-permute-start | bytes 589832 | tf_op jit(solution)/shard_map/ppermute | solution.py:216
  38.7 10.5 %copy-start.6 = (bf16[128,1024]{1,0:T(8,128)(2,1)S(1)}, bf16[128,1024]{1,0:T(8,128)(2,1)}, u32[]{:S(2)}) copy-start(bf16[128,1024]{1,0:T(8,128)(2,1)} %param.12) | copy-start | bytes 786436
  38.7 42.7 %all-to-all-start.1 = ((bf16[64,4,1024]{2,1,0:T(4,128)(2,1)}), bf16[64,4,1024]{2,1,0:T(4,128)(2,1)S(1)}, u32[]{:S(2)}, u32[]{:S(2)}) async-start(bf16[64,4,1024]{2,1,0:T(4,128)(2,1)} %reshape.60), calls=%async_computation.1 | async-start | bytes 1048576 | tf_op jit(solution)/shard_map/all_to_all | solution.py:27
  49.2 27.8 %copy-start = (bf16[1,256,1024]{2,1,0:T(8,128)(2,1)S(1)}, bf16[1,256,1024]{2,1,0:T(8,128)(2,1)}, u32[]{:S(2)}) copy-start(bf16[1,256,1024]{2,1,0:T(8,128)(2,1)} %param.9) | copy-start | bytes 1572868
  49.2 20.8 %collective-permute-start.8 = (bf16[128,1024]{1,0:T(8,128)(2,1)S(1)}, bf16[128,1024]{1,0:T(8,128)(2,1)S(1)}, u32[]{:S(2)}, u32[]{:S(2)}) collective-permute-start(bf16[128,1024]{1,0:T(8,128)(2,1)S(1)} %copy-done.6), channel_id=1, source_target_pairs={{0,0},{1,134},{2,2},{3,132},{4,4},{5,130},{6,6},{7,128},{8,32},{9,... | collective-permute-start | bytes 786440 | tf_op jit(solution)/shard_map/ppermute | solution.py:216
  54.4 16.1 %collective-permute-start.1 = (bf16[128,1024]{1,0:T(8,128)(2,1)S(1)}, bf16[128,1024]{1,0:T(8,128)(2,1)S(1)}, u32[]{:S(2)}, u32[]{:S(2)}) collective-permute-start(bf16[128,1024]{1,0:T(8,128)(2,1)S(1)} %slice.8), channel_id=1, source_target_pairs={{0,8},{1,9},{2,10},{3,11},{4,12},{5,13},{6,14},{7,15},{8,16},{9,17... | collective-permute-start | bytes 786440 | tf_op jit(solution)/shard_map/ppermute | solution.py:216
  56.6 19.0 %collective-permute-start.3 = (bf16[128,1024]{1,0:T(8,128)(2,1)S(1)}, bf16[128,1024]{1,0:T(8,128)(2,1)S(1)}, u32[]{:S(2)}, u32[]{:S(2)}) collective-permute-start(bf16[128,1024]{1,0:T(8,128)(2,1)S(1)} %slice.9), channel_id=1, source_target_pairs={{0,24},{1,25},{2,26},{3,27},{4,28},{5,29},{6,30},{7,31},{8,0},{9,1... | collective-permute-start | bytes 786440 | tf_op jit(solution)/shard_map/ppermute | solution.py:216
  70.0 5.6 %collective-permute-start.13 = (bf16[128,1024]{1,0:T(8,128)(2,1)S(1)}, bf16[128,1024]{1,0:T(8,128)(2,1)S(1)}, u32[]{:S(2)}, u32[]{:S(2)}) collective-permute-start(bf16[128,1024]{1,0:T(8,128)(2,1)S(1)} %collective-permute-done.8.out_ref), channel_id=1, source_target_pairs={{0,1},{1,0},{2,3},{3,2},{4,5},{5,4},{6,7},{7,6},{8,9},{9,8},{10,11... | collective-permute-start | bytes 786440 | tf_op jit(solution)/shard_map/ppermute | solution.py:216
  70.0 5.6 %collective-permute-start.10 = (bf16[256,384]{1,0:T(8,128)(2,1)S(1)}, bf16[256,384]{1,0:T(8,128)(2,1)S(1)}, u32[]{:S(2)}, u32[]{:S(2)}) collective-permute-start(bf16[256,384]{1,0:T(8,128)(2,1)S(1)} %collective-permute-done.5.n1), channel_id=1, source_target_pairs={{0,1},{1,0},{2,3},{3,2},{4,5},{5,4},{6,7},{7,6},{8,9},{9,8},{10,11... | collective-permute-start | bytes 589832 | tf_op jit(solution)/shard_map/ppermute | solution.py:216
  70.5 5.1 %collective-permute-start.11 = (bf16[256,384]{1,0:T(8,128)(2,1)S(1)}, bf16[256,384]{1,0:T(8,128)(2,1)S(1)}, u32[]{:S(2)}, u32[]{:S(2)}) collective-permute-start(bf16[256,384]{1,0:T(8,128)(2,1)S(1)} %collective-permute-done.6.n2), channel_id=1, source_target_pairs={{0,1},{1,0},{2,3},{3,2},{4,5},{5,4},{6,7},{7,6},{8,9},{9,8},{10,11... | collective-permute-start | bytes 589832 | tf_op jit(solution)/shard_map/ppermute | solution.py:216
  70.5 6.1 %collective-permute-start.12 = (bf16[256,384]{1,0:T(8,128)(2,1)S(1)}, bf16[256,384]{1,0:T(8,128)(2,1)S(1)}, u32[]{:S(2)}, u32[]{:S(2)}) collective-permute-start(bf16[256,384]{1,0:T(8,128)(2,1)S(1)} %collective-permute-done.7.n3), channel_id=1, source_target_pairs={{0,1},{1,0},{2,3},{3,2},{4,5},{5,4},{6,7},{7,6},{8,9},{9,8},{10,11... | collective-permute-start | bytes 589832 | tf_op jit(solution)/shard_map/ppermute | solution.py:216
  75.6 1.4 %collective-permute-start.9 = (bf16[256,384]{1,0:T(8,128)(2,1)S(1)}, bf16[256,384]{1,0:T(8,128)(2,1)S(1)}, u32[]{:S(2)}, u32[]{:S(2)}) collective-permute-start(bf16[256,384]{1,0:T(8,128)(2,1)S(1)} %pad_maximum_fusion.n0), channel_id=1, source_target_pairs={{0,1},{1,0},{2,3},{3,2},{4,5},{5,4},{6,7},{7,6},{8,9},{9,8},{10,11... | collective-permute-start | bytes 589832 | tf_op jit(solution)/shard_map/ppermute | solution.py:216
  81.4 6.2 %copy-start.4 = (f32[1024]{0:T(1024)S(1)}, f32[1024]{0:T(1024)}, u32[]{:S(2)}) copy-start(f32[1024]{0:T(1024)} %param.13) | copy-start | bytes 12292
  81.7 4.8 %collective-permute-start.14 = (f32[8,1024]{1,0:T(8,128)S(1)}, f32[8,1024]{1,0:T(8,128)S(1)}, u32[]{:S(2)}, u32[]{:S(2)}) collective-permute-start(f32[8,1024]{1,0:T(8,128)S(1)} %shard_map.94.t0), channel_id=1, source_target_pairs={{0,8},{1,9},{2,10},{3,11},{4,12},{5,13},{6,14},{7,15},{8,16},{9,17... | collective-permute-start | bytes 98312 | tf_op jit(solution)/shard_map/ppermute | solution.py:216
  81.8 4.8 %collective-permute-start.15 = (f32[8,1024]{1,0:T(8,128)S(1)}, f32[8,1024]{1,0:T(8,128)S(1)}, u32[]{:S(2)}, u32[]{:S(2)}) collective-permute-start(f32[8,1024]{1,0:T(8,128)S(1)} %shard_map.94.t0), channel_id=1, source_target_pairs={{0,16},{1,17},{2,18},{3,19},{4,20},{5,21},{6,22},{7,23},{8,24},{9,... | collective-permute-start | bytes 98312 | tf_op jit(solution)/shard_map/ppermute | solution.py:216
  84.6 3.1 %collective-permute-start.16 = (f32[8,1024]{1,0:T(8,128)S(1)}, f32[8,1024]{1,0:T(8,128)S(1)}, u32[]{:S(2)}, u32[]{:S(2)}) collective-permute-start(f32[8,1024]{1,0:T(8,128)S(1)} %shard_map.94.t0), channel_id=1, source_target_pairs={{0,24},{1,25},{2,26},{3,27},{4,28},{5,29},{6,30},{7,31},{8,0},{9,1... | collective-permute-start | bytes 98312 | tf_op jit(solution)/shard_map/ppermute | solution.py:216
  109.6 5.2 %collective-permute-start.17 = (bf16[32,8,1024]{2,1,0:T(8,128)(2,1)S(1)}, bf16[32,8,1024]{2,1,0:T(8,128)(2,1)S(1)}, u32[]{:S(2)}, u32[]{:S(2)}) collective-permute-start(bf16[32,8,1024]{2,1,0:T(8,128)(2,1)S(1)} %all_to_all.15), channel_id=1, source_target_pairs={{0,1},{1,0},{2,3},{3,2},{4,5},{5,4},{6,7},{7,6},{8,9},{9,8},{10,11... | collective-permute-start | bytes 1572872 | tf_op jit(solution)/shard_map/ppermute | solution.py:216
  (3 other events, 8.2 us)

commit v3 on v2

--- a/solution.py
+++ b/solution.py
@@ -255,7 +255,7 @@
     near[0] = after(near[0], *near[1:], out1, h2, h2b)
     far = [other_core(w) for w in near]
 
-    rows = exchange(after(rows, *near[1:]).reshape(64, 4, WIDTH), 2)
+    rows = exchange(after(rows, *near[1:], out1, h2, h2b).reshape(64, 4, WIDTH), 2)
 
     part = call(
         encode_kernel,

time: 130 us -> 123 us (0.946)
  starting transfers between devices: 58.2 us -> 52.9 us
  local copies, waits for them, and re-layouts: 3.2 us -> 6.84 us
  waiting for transfers between devices: 22.9 us -> 20 us
  blocking collectives: 21.5 us -> 18.8 us
    all_to_all x1, waiting for transfers between devices: 0.01 us -> 8.44 us  [exchange(): lax.all_to_all(x, ('grp', 'dev'), split_axis=0, concat_axis=0, tiled=True...]
    ppermute x18, starting transfers between devices: 38.1 us -> 29.9 us  [shift(): return lax.ppermute(x, ('grp', 'dev'), perm)]
    ppermute x18, waiting for transfers between devices: 15.2 us -> 7.95 us  [shift(): return lax.ppermute(x, ('grp', 'dev'), perm)]
    all_to_all x1, waiting for transfers between devices: 7.61 us -> 3.58 us  [local(): lax.all_to_all(info, ('grp', 'dev'), split_axis=0, concat_axis=0, tiled=T...]
    all_to_all x1, blocking collectives: 21.5 us -> 18.8 us  [exchange(): lax.all_to_all(x, ('grp', 'dev'), split_axis=0, concat_axis=0, tiled=True...]
    unnamed x14 -> x22, local copies, waits for them, and re-layouts: 2.02 us -> 4.26 us
    all_to_all x1, starting transfers between devices: 9.62 us -> 11.5 us  [local(): lax.all_to_all(info, ('grp', 'dev'), split_axis=0, concat_axis=0, tiled=T...]
    slice x2, local copies, waits for them, and re-layouts: 0.04 us -> 1.43 us  [local(): h2, h2b = (along_x(h1[:128], 1), along_x(h3[128:], 3))]
  transfers between devices with their start and end apart: 20 -> 20, of which waited for: 7 -> 12; matrix products, arithmetic and copies ran while one was open for 1% -> 2% of each run, Pallas kernels for 5% -> 5%
where the time goes in v3:
time: 123 us
  starting transfers between devices  52.9 us (43%)
  Pallas kernels  21.7 us (18%)
  waiting for transfers between devices  20 us (16%)
  blocking collectives  18.8 us (15%)
  local copies, waits for them, and re-layouts  6.84 us (6%)
  between operations  1.49 us (1%)
    ppermute x18, starting transfers between devices, shift(): return lax.ppermute(x, ('grp', 'dev'), perm)  29.9 us
    pallas_call x6, Pallas kernels, call(): pl.pallas_call(kernel, out_shape=out, in_specs=[pl.BlockSpec(memory_space...  21.7 us
    all_to_all x1, blocking collectives, exchange(): lax.all_to_all(x, ('grp', 'dev'), split_axis=0, concat_axis=0, tiled=True...  18.8 us
    all_to_all x1, starting transfers between devices, local(): lax.all_to_all(info, ('grp', 'dev'), split_axis=0, concat_axis=0, tiled=T...  11.5 us
    all_to_all x1, starting transfers between devices, exchange(): lax.all_to_all(x, ('grp', 'dev'), split_axis=0, concat_axis=0, tiled=True...  11.5 us
    all_to_all x1, waiting for transfers between devices, exchange(): lax.all_to_all(x, ('grp', 'dev'), split_axis=0, concat_axis=0, tiled=True...  8.44 us
    ppermute x18, waiting for transfers between devices, shift(): return lax.ppermute(x, ('grp', 'dev'), perm)  7.95 us
    unnamed x22, local copies, waits for them, and re-layouts  4.26 us
  transfers between devices with their start and end apart: 20, of which 12 were waited for; matrix products, arithmetic and copies ran while one was open for 2% of the time, Pallas kernels for 5%

profile of v3, /device:TPU:1, one launch (start us, length us, event | category | flops | bytes accessed | tf_op | source)
XLA Modules:
  0.0 122.5 jit_solution(593379468428816703)
XLA Ops:
  0.0 2.0 %collective-permute-start = (bf16[256,1024]{1,0:T(8,128)(2,1)}, bf16[256,1024]{1,0:T(8,128)(2,1)S(1)}, u32[]{:S(2)}, u32[]{:S(2)}) collective-permute-start(bf16[256,1024]{1,0:T(8,128)(2,1)} %bitcast.15), channel_id=1, source_target_pairs={{0,8},{1,9},{2,10},{3,11},{4,12},{5,13},{6,14},{7,15},{8,16},{9,17... | collective-permute-start | bytes 1572872 | tf_op jit(solution)/shard_map/ppermute | solution.py:216
  2.0 1.3 %collective-permute-start.2 = (bf16[256,1024]{1,0:T(8,128)(2,1)}, bf16[256,1024]{1,0:T(8,128)(2,1)S(1)}, u32[]{:S(2)}, u32[]{:S(2)}) collective-permute-start(bf16[256,1024]{1,0:T(8,128)(2,1)} %bitcast.16), channel_id=1, source_target_pairs={{0,24},{1,25},{2,26},{3,27},{4,28},{5,29},{6,30},{7,31},{8,0},{9,1... | collective-permute-start | bytes 1572872 | tf_op jit(solution)/shard_map/ppermute | solution.py:216
  4.7 1.0 copy-done.1
  7.3 5.9 %collective-permute-start.4 = (bf16[128,384]{1,0:T(8,128)(2,1)S(1)}, bf16[128,384]{1,0:T(8,128)(2,1)S(1)}, u32[]{:S(2)}, u32[]{:S(2)}) collective-permute-start(bf16[128,384]{1,0:T(8,128)(2,1)S(1)} %shard_map.91), channel_id=1, source_target_pairs={{0,134},{1,135},{2,132},{3,133},{4,130},{5,131},{6,128},{7,129},{8... | collective-permute-start | bytes 294920 | tf_op jit(solution)/shard_map/ppermute | solution.py:216
  13.2 3.3 %collective-permute-start.8 = (bf16[128,1024]{1,0:T(8,128)(2,1)S(1)}, bf16[128,1024]{1,0:T(8,128)(2,1)S(1)}, u32[]{:S(2)}, u32[]{:S(2)}) collective-permute-start(bf16[128,1024]{1,0:T(8,128)(2,1)S(1)} %copy-done.10), channel_id=1, source_target_pairs={{0,0},{1,134},{2,2},{3,132},{4,4},{5,130},{6,6},{7,128},{8,32},{9,... | collective-permute-start | bytes 786440 | tf_op jit(solution)/shard_map/ppermute | solution.py:216
  17.3 11.5 %all-to-all-start = ((f32[256,1,128]{2,1,0:T(1,128)}), f32[256,1,128]{2,1,0:T(1,128)S(1)}, u32[]{:S(2)}, u32[]{:S(2)}) async-start(f32[256,1,128]{2,1,0:T(1,128)} %fusion), calls=%async_computation | async-start | bytes 262144 | tf_op jit(solution)/shard_map/all_to_all | solution.py:247
  29.5 1.4 %collective-permute-start.1 = (bf16[128,1024]{1,0:T(8,128)(2,1)}, bf16[128,1024]{1,0:T(8,128)(2,1)S(1)}, u32[]{:S(2)}, u32[]{:S(2)}) collective-permute-start(bf16[128,1024]{1,0:T(8,128)(2,1)} %slice.8), channel_id=1, source_target_pairs={{0,8},{1,9},{2,10},{3,11},{4,12},{5,13},{6,14},{7,15},{8,16},{9,17... | collective-permute-start | bytes 786440 | tf_op jit(solution)/shard_map/ppermute | solution.py:216
  31.6 1.3 %collective-permute-start.3 = (bf16[128,1024]{1,0:T(8,128)(2,1)}, bf16[128,1024]{1,0:T(8,128)(2,1)S(1)}, u32[]{:S(2)}, u32[]{:S(2)}) collective-permute-start(bf16[128,1024]{1,0:T(8,128)(2,1)} %slice.9), channel_id=1, source_target_pairs={{0,24},{1,25},{2,26},{3,27},{4,28},{5,29},{6,30},{7,31},{8,0},{9,1... | collective-permute-start | bytes 786440 | tf_op jit(solution)/shard_map/ppermute | solution.py:216
  33.0 1.5 %collective-permute-start.5 = (bf16[256,384]{1,0:T(8,128)(2,1)S(1)}, bf16[256,384]{1,0:T(8,128)(2,1)S(1)}, u32[]{:S(2)}, u32[]{:S(2)}) collective-permute-start(bf16[256,384]{1,0:T(8,128)(2,1)S(1)} %pad_maximum_fusion.n0), channel_id=1, source_target_pairs={{0,32},{1,33},{2,34},{3,35},{4,36},{5,37},{6,38},{7,39},{8,40},{9,... | collective-permute-start | bytes 589832 | tf_op jit(solution)/shard_map/ppermute | solution.py:216
  34.4 2.4 %collective-permute-start.6 = (bf16[256,384]{1,0:T(8,128)(2,1)S(1)}, bf16[256,384]{1,0:T(8,128)(2,1)}, u32[]{:S(2)}, u32[]{:S(2)}) collective-permute-start(bf16[256,384]{1,0:T(8,128)(2,1)S(1)} %pad_maximum_fusion.n0), channel_id=1, source_target_pairs={{0,64},{1,65},{2,66},{3,67},{4,68},{5,69},{6,70},{7,71},{8,72},{9,... | collective-permute-start | bytes 589832 | tf_op jit(solution)/shard_map/ppermute | solution.py:216
  36.9 1.1 collective-permute-start.7
  38.0 3.6 %all-to-all-done = f32[256,1,128]{2,1,0:T(1,128)S(1)} async-done(((f32[256,1,128]{2,1,0:T(1,128)}), f32[256,1,128]{2,1,0:T(1,128)S(1)}, u32[]{:S(2)}, u32[]{:S(2)}) %all-to-all-start) | async-done | bytes 131104 | tf_op jit(solution)/shard_map/all_to_all | solution.py:247
  41.6 1.1 shard_map.93
  42.8 3.2 %collective-permute-done.6.n2 = bf16[256,384]{1,0:T(8,128)(2,1)} collective-permute-done((bf16[256,384]{1,0:T(8,128)(2,1)S(1)}, bf16[256,384]{1,0:T(8,128)(2,1)}, u32[]{:S(2)}, u32[]{:S(2)}) %collective-permute-start.6) | collective-permute-done | bytes 196640 | tf_op jit(solution)/shard_map/ppermute | solution.py:216
  46.7 1.0 reshape.60
  47.7 11.5 %all-to-all-start.1 = ((bf16[64,4,1024]{2,1,0:T(4,128)(2,1)}), bf16[64,4,1024]{2,1,0:T(4,128)(2,1)S(1)}, u32[]{:S(2)}, u32[]{:S(2)}) async-start(bf16[64,4,1024]{2,1,0:T(4,128)(2,1)} %reshape.60), calls=%async_computation.1 | async-start | bytes 1048576 | tf_op jit(solution)/shard_map/all_to_all | solution.py:27
  63.6 4.9 %shard_map.92.part_ref = f32[4,1024]{1,0:T(4,128)S(1)} custom-call(s32[7]{0:T(128)S(1)} %copy-done.7, bf16[256,1024]{1,0:T(8,128)(2,1)S(1)} %bitcast.17, bf16[256,1024]{1,0:T(8,128)(2,1)S(1)} %collective-permute-done.h1, bf16[128,1024]{1,0:T(8,128)(2,1)S(1)} %collective-permute-done.1.h2, bf16[128,1024]{1,0:T(8,128)(2,1)S(1)} %copy-done.5, ...), custom_call_target="tpu_custom_call" | custom-call | flops 1073741824 | bytes 1048576 | tf_op jit(solution)/shard_map/pallas_call | solution.py:43
  68.5 8.4 %all-to-all-done.1.old_ref = bf16[64,4,1024]{2,1,0:T(4,128)(2,1)S(1)} async-done(((bf16[64,4,1024]{2,1,0:T(4,128)(2,1)}), bf16[64,4,1024]{2,1,0:T(4,128)(2,1)S(1)}, u32[]{:S(2)}, u32[]{:S(2)}) %all-to-all-start.1) | async-done | bytes 524320 | tf_op jit(solution)/shard_map/all_to_all | solution.py:27
  77.3 2.4 %collective-permute-start.15 = (f32[8,1024]{1,0:T(8,128)S(1)}, f32[8,1024]{1,0:T(8,128)S(1)}, u32[]{:S(2)}, u32[]{:S(2)}) collective-permute-start(f32[8,1024]{1,0:T(8,128)S(1)} %shard_map.94.t0), channel_id=1, source_target_pairs={{0,16},{1,17},{2,18},{3,19},{4,20},{5,21},{6,22},{7,23},{8,24},{9,... | collective-permute-start | bytes 98312 | tf_op jit(solution)/shard_map/ppermute | solution.py:216
  79.7 1.2 collective-permute-start.16
  83.1 18.8 %all_to_all.15 = bf16[32,8,1024]{2,1,0:T(8,128)(2,1)S(1)} all-to-all(bf16[32,8,1024]{2,1,0:T(8,128)(2,1)S(1)} %broadcast_in_dim.21), channel_id=1, replica_groups={{0,32,64,96,2,34,66,98,4,36,68,100,6,38,70,102,128,160,192,224,130,162,..., dimensions={0} | all-to-all | bytes 1048576 | tf_op jit(solution)/shard_map/all_to_all | solution.py:27
  101.9 4.5 %collective-permute-start.17 = (bf16[32,8,1024]{2,1,0:T(8,128)(2,1)S(1)}, bf16[32,8,1024]{2,1,0:T(8,128)(2,1)S(1)}, u32[]{:S(2)}, u32[]{:S(2)}) collective-permute-start(bf16[32,8,1024]{2,1,0:T(8,128)(2,1)S(1)} %all_to_all.15), channel_id=1, source_target_pairs={{0,1},{1,0},{2,3},{3,2},{4,5},{5,4},{6,7},{7,6},{8,9},{9,8},{10,11... | collective-permute-start | bytes 1572872 | tf_op jit(solution)/shard_map/ppermute | solution.py:216
  106.4 1.5 %collective-permute-done.17 = bf16[32,8,1024]{2,1,0:T(8,128)(2,1)S(1)} collective-permute-done((bf16[32,8,1024]{2,1,0:T(8,128)(2,1)S(1)}, bf16[32,8,1024]{2,1,0:T(8,128)(2,1)S(1)}, u32[]{:S(2)}, u32[]{:S(2)}) %collective-permute-start.17) | collective-permute-done | bytes 524320 | tf_op jit(solution)/shard_map/ppermute | solution.py:216
  107.9 14.6 %shard_map.96 = bf16[256,1024]{1,0:T(8,128)(2,1)} custom-call(bf16[256,1024]{1,0:T(8,128)(2,1)S(1)} %bitcast.19, bf16[256,1024]{1,0:T(8,128)(2,1)S(1)} %bitcast.22, bf16[256,1024]{1,0:T(8,128)(2,1)S(1)} %copy-done.2), custom_call_target="tpu_custom_call" | custom-call | flops 2147483648 | bytes 1048576 | tf_op jit(solution)/shard_map/pallas_call | solution.py:43
  (54 shorter events, 11.5 us)
Async XLA Ops:
  0.0 28.8 %collective-permute-start = (bf16[256,1024]{1,0:T(8,128)(2,1)}, bf16[256,1024]{1,0:T(8,128)(2,1)S(1)}, u32[]{:S(2)}, u32[]{:S(2)}) collective-permute-start(bf16[256,1024]{1,0:T(8,128)(2,1)} %bitcast.15), channel_id=1, source_target_pairs={{0,8},{1,9},{2,10},{3,11},{4,12},{5,13},{6,14},{7,15},{8,16},{9,17... | collective-permute-start | bytes 1572872 | tf_op jit(solution)/shard_map/ppermute | solution.py:216
  2.0 28.9 %collective-permute-start.2 = (bf16[256,1024]{1,0:T(8,128)(2,1)}, bf16[256,1024]{1,0:T(8,128)(2,1)S(1)}, u32[]{:S(2)}, u32[]{:S(2)}) collective-permute-start(bf16[256,1024]{1,0:T(8,128)(2,1)} %bitcast.16), channel_id=1, source_target_pairs={{0,24},{1,25},{2,26},{3,27},{4,28},{5,29},{6,30},{7,31},{8,0},{9,1... | collective-permute-start | bytes 1572872 | tf_op jit(solution)/shard_map/ppermute | solution.py:216
  6.7 34.9 %copy-start.6 = (s32[7]{0:T(128)}, s32[7]{0:T(128)S(1)}, u32[]{:S(2)}) copy-start(s32[7]{0:T(128)S(1)} %stack.23.where) | copy-start | bytes 88
  6.7 6.4 %copy-start.10 = (bf16[128,1024]{1,0:T(8,128)(2,1)S(1)}, bf16[128,1024]{1,0:T(8,128)(2,1)}, u32[]{:S(2)}) copy-start(bf16[128,1024]{1,0:T(8,128)(2,1)} %param.12) | copy-start | bytes 786436
  7.3 25.7 %collective-permute-start.4 = (bf16[128,384]{1,0:T(8,128)(2,1)S(1)}, bf16[128,384]{1,0:T(8,128)(2,1)S(1)}, u32[]{:S(2)}, u32[]{:S(2)}) collective-permute-start(bf16[128,384]{1,0:T(8,128)(2,1)S(1)} %shard_map.91), channel_id=1, source_target_pairs={{0,134},{1,135},{2,132},{3,133},{4,130},{5,131},{6,128},{7,129},{8... | collective-permute-start | bytes 294920 | tf_op jit(solution)/shard_map/ppermute | solution.py:216
  13.2 23.7 %collective-permute-start.8 = (bf16[128,1024]{1,0:T(8,128)(2,1)S(1)}, bf16[128,1024]{1,0:T(8,128)(2,1)S(1)}, u32[]{:S(2)}, u32[]{:S(2)}) collective-permute-start(bf16[128,1024]{1,0:T(8,128)(2,1)S(1)} %copy-done.10), channel_id=1, source_target_pairs={{0,0},{1,134},{2,2},{3,132},{4,4},{5,130},{6,6},{7,128},{8,32},{9,... | collective-permute-start | bytes 786440 | tf_op jit(solution)/shard_map/ppermute | solution.py:216
  17.3 24.3 %all-to-all-start = ((f32[256,1,128]{2,1,0:T(1,128)}), f32[256,1,128]{2,1,0:T(1,128)S(1)}, u32[]{:S(2)}, u32[]{:S(2)}) async-start(f32[256,1,128]{2,1,0:T(1,128)} %fusion), calls=%async_computation | async-start | bytes 262144 | tf_op jit(solution)/shard_map/all_to_all | solution.py:247
  29.5 12.1 %copy-start.2 = (bf16[256,1024]{1,0:T(8,128)(2,1)S(1)}, bf16[256,1024]{1,0:T(8,128)(2,1)}, u32[]{:S(2)}) copy-start(bf16[256,1024]{1,0:T(8,128)(2,1)} %bank_ref.3) | copy-start | bytes 1572868
  29.5 16.5 %collective-permute-start.1 = (bf16[128,1024]{1,0:T(8,128)(2,1)}, bf16[128,1024]{1,0:T(8,128)(2,1)S(1)}, u32[]{:S(2)}, u32[]{:S(2)}) collective-permute-start(bf16[128,1024]{1,0:T(8,128)(2,1)} %slice.8), channel_id=1, source_target_pairs={{0,8},{1,9},{2,10},{3,11},{4,12},{5,13},{6,14},{7,15},{8,16},{9,17... | collective-permute-start | bytes 786440 | tf_op jit(solution)/shard_map/ppermute | solution.py:216
  31.6 14.4 %collective-permute-start.3 = (bf16[128,1024]{1,0:T(8,128)(2,1)}, bf16[128,1024]{1,0:T(8,128)(2,1)S(1)}, u32[]{:S(2)}, u32[]{:S(2)}) collective-permute-start(bf16[128,1024]{1,0:T(8,128)(2,1)} %slice.9), channel_id=1, source_target_pairs={{0,24},{1,25},{2,26},{3,27},{4,28},{5,29},{6,30},{7,31},{8,0},{9,1... | collective-permute-start | bytes 786440 | tf_op jit(solution)/shard_map/ppermute | solution.py:216
  33.0 9.8 %collective-permute-start.5 = (bf16[256,384]{1,0:T(8,128)(2,1)S(1)}, bf16[256,384]{1,0:T(8,128)(2,1)S(1)}, u32[]{:S(2)}, u32[]{:S(2)}) collective-permute-start(bf16[256,384]{1,0:T(8,128)(2,1)S(1)} %pad_maximum_fusion.n0), channel_id=1, source_target_pairs={{0,32},{1,33},{2,34},{3,35},{4,36},{5,37},{6,38},{7,39},{8,40},{9,... | collective-permute-start | bytes 589832 | tf_op jit(solution)/shard_map/ppermute | solution.py:216
  34.4 11.6 %collective-permute-start.6 = (bf16[256,384]{1,0:T(8,128)(2,1)S(1)}, bf16[256,384]{1,0:T(8,128)(2,1)}, u32[]{:S(2)}, u32[]{:S(2)}) collective-permute-start(bf16[256,384]{1,0:T(8,128)(2,1)S(1)} %pad_maximum_fusion.n0), channel_id=1, source_target_pairs={{0,64},{1,65},{2,66},{3,67},{4,68},{5,69},{6,70},{7,71},{8,72},{9,... | collective-permute-start | bytes 589832 | tf_op jit(solution)/shard_map/ppermute | solution.py:216
  36.9 9.1 %collective-permute-start.7 = (bf16[256,384]{1,0:T(8,128)(2,1)S(1)}, bf16[256,384]{1,0:T(8,128)(2,1)}, u32[]{:S(2)}, u32[]{:S(2)}) collective-permute-start(bf16[256,384]{1,0:T(8,128)(2,1)S(1)} %pad_maximum_fusion.n0), channel_id=1, source_target_pairs={{0,96},{1,97},{2,98},{3,99},{4,100},{5,101},{6,102},{7,103},{8,104... | collective-permute-start | bytes 589832 | tf_op jit(solution)/shard_map/ppermute | solution.py:216
  47.7 14.3 %copy-start = (bf16[1,256,1024]{2,1,0:T(8,128)(2,1)S(1)}, bf16[1,256,1024]{2,1,0:T(8,128)(2,1)}, u32[]{:S(2)}) copy-start(bf16[1,256,1024]{2,1,0:T(8,128)(2,1)} %param.9) | copy-start | bytes 1572868
  47.7 29.2 %all-to-all-start.1 = ((bf16[64,4,1024]{2,1,0:T(4,128)(2,1)}), bf16[64,4,1024]{2,1,0:T(4,128)(2,1)S(1)}, u32[]{:S(2)}, u32[]{:S(2)}) async-start(bf16[64,4,1024]{2,1,0:T(4,128)(2,1)} %reshape.60), calls=%async_computation.1 | async-start | bytes 1048576 | tf_op jit(solution)/shard_map/all_to_all | solution.py:27
  59.2 1.7 %collective-permute-start.13 = (bf16[128,1024]{1,0:T(8,128)(2,1)S(1)}, bf16[128,1024]{1,0:T(8,128)(2,1)S(1)}, u32[]{:S(2)}, u32[]{:S(2)}) collective-permute-start(bf16[128,1024]{1,0:T(8,128)(2,1)S(1)} %collective-permute-done.8.out_ref), channel_id=1, source_target_pairs={{0,1},{1,0},{2,3},{3,2},{4,5},{5,4},{6,7},{7,6},{8,9},{9,8},{10,11... | collective-permute-start | bytes 786440 | tf_op jit(solution)/shard_map/ppermute | solution.py:216
  59.8 1.4 %collective-permute-start.10 = (bf16[256,384]{1,0:T(8,128)(2,1)S(1)}, bf16[256,384]{1,0:T(8,128)(2,1)S(1)}, u32[]{:S(2)}, u32[]{:S(2)}) collective-permute-start(bf16[256,384]{1,0:T(8,128)(2,1)S(1)} %collective-permute-done.5.n1), channel_id=1, source_target_pairs={{0,1},{1,0},{2,3},{3,2},{4,5},{5,4},{6,7},{7,6},{8,9},{9,8},{10,11... | collective-permute-start | bytes 589832 | tf_op jit(solution)/shard_map/ppermute | solution.py:216
  59.9 1.8 %collective-permute-start.11 = (bf16[256,384]{1,0:T(8,128)(2,1)}, bf16[256,384]{1,0:T(8,128)(2,1)S(1)}, u32[]{:S(2)}, u32[]{:S(2)}) collective-permute-start(bf16[256,384]{1,0:T(8,128)(2,1)} %collective-permute-done.6.n2), channel_id=1, source_target_pairs={{0,1},{1,0},{2,3},{3,2},{4,5},{5,4},{6,7},{7,6},{8,9},{9,8},{10,11... | collective-permute-start | bytes 589832 | tf_op jit(solution)/shard_map/ppermute | solution.py:216
  60.3 1.7 %collective-permute-start.12 = (bf16[256,384]{1,0:T(8,128)(2,1)}, bf16[256,384]{1,0:T(8,128)(2,1)S(1)}, u32[]{:S(2)}, u32[]{:S(2)}) collective-permute-start(bf16[256,384]{1,0:T(8,128)(2,1)} %collective-permute-done.7.n3), channel_id=1, source_target_pairs={{0,1},{1,0},{2,3},{3,2},{4,5},{5,4},{6,7},{7,6},{8,9},{9,8},{10,11... | collective-permute-start | bytes 589832 | tf_op jit(solution)/shard_map/ppermute | solution.py:216
  60.4 1.7 %collective-permute-start.9 = (bf16[256,384]{1,0:T(8,128)(2,1)S(1)}, bf16[256,384]{1,0:T(8,128)(2,1)S(1)}, u32[]{:S(2)}, u32[]{:S(2)}) collective-permute-start(bf16[256,384]{1,0:T(8,128)(2,1)S(1)} %pad_maximum_fusion.n0), channel_id=1, source_target_pairs={{0,1},{1,0},{2,3},{3,2},{4,5},{5,4},{6,7},{7,6},{8,9},{9,8},{10,11... | collective-permute-start | bytes 589832 | tf_op jit(solution)/shard_map/ppermute | solution.py:216
  77.2 4.0 %collective-permute-start.14 = (f32[8,1024]{1,0:T(8,128)S(1)}, f32[8,1024]{1,0:T(8,128)S(1)}, u32[]{:S(2)}, u32[]{:S(2)}) collective-permute-start(f32[8,1024]{1,0:T(8,128)S(1)} %shard_map.94.t0), channel_id=1, source_target_pairs={{0,8},{1,9},{2,10},{3,11},{4,12},{5,13},{6,14},{7,15},{8,16},{9,17... | collective-permute-start | bytes 98312 | tf_op jit(solution)/shard_map/ppermute | solution.py:216
  77.3 4.5 %collective-permute-start.15 = (f32[8,1024]{1,0:T(8,128)S(1)}, f32[8,1024]{1,0:T(8,128)S(1)}, u32[]{:S(2)}, u32[]{:S(2)}) collective-permute-start(f32[8,1024]{1,0:T(8,128)S(1)} %shard_map.94.t0), channel_id=1, source_target_pairs={{0,16},{1,17},{2,18},{3,19},{4,20},{5,21},{6,22},{7,23},{8,24},{9,... | collective-permute-start | bytes 98312 | tf_op jit(solution)/shard_map/ppermute | solution.py:216
  79.7 3.1 %collective-permute-start.16 = (f32[8,1024]{1,0:T(8,128)S(1)}, f32[8,1024]{1,0:T(8,128)S(1)}, u32[]{:S(2)}, u32[]{:S(2)}) collective-permute-start(f32[8,1024]{1,0:T(8,128)S(1)} %shard_map.94.t0), channel_id=1, source_target_pairs={{0,24},{1,25},{2,26},{3,27},{4,28},{5,29},{6,30},{7,31},{8,0},{9,1... | collective-permute-start | bytes 98312 | tf_op jit(solution)/shard_map/ppermute | solution.py:216
  101.9 6.0 %collective-permute-start.17 = (bf16[32,8,1024]{2,1,0:T(8,128)(2,1)S(1)}, bf16[32,8,1024]{2,1,0:T(8,128)(2,1)S(1)}, u32[]{:S(2)}, u32[]{:S(2)}) collective-permute-start(bf16[32,8,1024]{2,1,0:T(8,128)(2,1)S(1)} %all_to_all.15), channel_id=1, source_target_pairs={{0,1},{1,0},{2,3},{3,2},{4,5},{5,4},{6,7},{7,6},{8,9},{9,8},{10,11... | collective-permute-start | bytes 1572872 | tf_op jit(solution)/shard_map/ppermute | solution.py:216
  (7 other events, 15.9 us)

commit v4 on v3

--- a/solution.py
+++ b/solution.py
@@ -85,13 +85,16 @@
     own_ref[:, 2 * CUT :] = keyval_ref[:, pl.ds(pl.multiple_of(block * CUT + WIDTH, CUT), CUT)]
 
 
-def pick_kernel(where, info_ref, bank_ref, rows_ref):
+def pick_kernel(where, info_ref, bank_ref, keep_ref, give_ref, select_ref):
     n = bank_ref.shape[0]
     number = lax.broadcasted_iota(jnp.int32, (PLACES, n), 1).astype(F32)
     own, slot, place = [info_ref[:, i : i + 1] for i in range(3)]
     a = jnp.where((place == number) & (own == where[6].astype(F32)), 1.0, 0.0).astype(BF)
     b = jnp.where(slot == number, 1.0, 0.0).astype(BF)
-    rows_ref[...] = dot(dot(a, b, TN).astype(BF), bank_ref[...]).astype(BF)
+    select_ref[...] = dot(a, b, TN)
+    for ref, c in ((keep_ref, where[3]), (give_ref, 1 - where[3])):
+        half = pl.ds(pl.multiple_of(c * (PLACES // 2), PLACES // 2), PLACES // 2)
+        ref[...] = dot(select_ref[half, :].astype(BF), bank_ref[...]).astype(BF)
 
 
 def row_blocks(where):
@@ -104,7 +107,7 @@
 
 
 def encode_kernel(
-    where, h0, h1, h2, h2b, h3, n0, n1, n2, n3, f0, f1, f2, f3, out_ref, out2_ref, part_ref, w_ref
+    where, h0, h1, h2, h3, n0, n1, n2, n3, f0, f1, f2, f3, out_ref, out2_ref, part_ref, w_ref
 ):
     near, far = (n0, n1, n2, n3), (f0, f1, f2, f3)
     for k, rows, features in row_blocks(where):
@@ -115,8 +118,8 @@
     four = 4 * HEAD
     mask = head_mask(4)
     contexts = []
-    for refs in ((h0,), (h1,), (h2, h2b), (h3,)):
-        x = jnp.concatenate([r[...] for r in refs], axis=0)
+    for ref in (h0, h1, h2, h3):
+        x = ref[...]
         keyval = dot(x, w_ref[:, four:]).astype(BF)
         query = (0.125 * dot(x[0:16], w_ref[:, :four])[0:1]).astype(BF).astype(F32)
         query = jnp.where(mask, jnp.broadcast_to(query, (4, four)), 0.0).astype(BF)
@@ -239,23 +242,27 @@
     where = jnp.stack([zh, y, x, c, owner[0], slot[0], grp * 32 + dev])
 
     h1, h3 = along_x(hidden, 1), along_x(hidden, 3)
-    h2, h2b = along_x(h1[:128], 1), along_x(h3[128:], 3)
-
-    place = (((zh * 4 + zl) * 4 + y) * 2 + c) * 4 + x
+    h2 = along_x(h1, 1)
+
+    own = call(cut_kernel, shape((CUT, 3 * CUT), BF), 2**10, w_query, w_keyval, where=where)
+    out1 = shift(w_out, lambda zh, y, xx, zl, c: (c, xx, y, zl if c == zh else 3 - zl, zh))
+    got = mirror(own)
+    own = after(jnp.concatenate([own, got], axis=0), h1, h3)
+    out2 = other_core(out1)
+    near = [along_y(own, k) for k in range(4)]
+    near[0] = after(near[0], *near[1:], out1, h2)
+    far = [other_core(w) for w in near]
+
+    place = (((c * 2 + zh) * 4 + zl) * 4 + y) * 4 + x
     lane = lax.broadcasted_iota(jnp.int32, (PLACES, 1, 128), 2)
     info = jnp.where(lane == 0, where[4], jnp.where(lane == 1, where[5], place)).astype(F32)
-    info = lax.all_to_all(info, ("grp", "dev"), split_axis=0, concat_axis=0, tiled=True).reshape(PLACES, 128)
-    rows = call(pick_kernel, shape((PLACES, WIDTH), BF), 2**27, info, bank, where=where)
-
-    own = call(cut_kernel, shape((CUT, 3 * CUT), BF), 2**10, w_query, w_keyval, where=where)
-    out1 = shift(w_out, lambda zh, y, xx, zl, c: (c, xx, y, zl if c == zh else 3 - zl, zh))
-    own = after(jnp.concatenate([own, mirror(own)], axis=0), h1, h3)
-    out2 = other_core(out1)
-    near = [along_y(own, k) for k in range(4)]
-    near[0] = after(near[0], *near[1:], out1, h2, h2b)
-    far = [other_core(w) for w in near]
-
-    rows = exchange(after(rows, *near[1:], out1, h2, h2b).reshape(64, 4, WIDTH), 2)
+    info = lax.all_to_all(after(info, got), ("grp", "dev"), split_axis=0, concat_axis=0, tiled=True).reshape(PLACES, 128)
+    half = shape((PLACES // 2, WIDTH), BF)
+    keep, give = call(
+        pick_kernel, [half, half], 2**27, info, bank, where=where, scratch=[pltpu.VMEM((PLACES, PLACES), F32)]
+    )
+    rows = keep + other_core(after(give, *near[1:]))
+    rows = exchange(after(rows, *far, out2).reshape(32, 4, WIDTH), 1)
 
     part = call(
         encode_kernel,
@@ -264,7 +271,6 @@
         hidden,
         h1,
         h2,
-        h2b,
         h3,
         *near,
         *far,
@@ -272,7 +278,6 @@
         out2,
         where=where,
         scratch=[pltpu.VMEM((WIDTH, 6 * CUT), BF)],
-        mib=24,
     )
     both = call(pack_kernel, shape((8, WIDTH), F32), 2**18, part, rows)
     both = [along_x(both, k) for k in range(4)]
@@ -288,7 +293,7 @@
         here.reshape(256, WIDTH),
         there.reshape(256, WIDTH),
         bank,
-        mib=32,
+        mib=24,
     )
 
 

time: 123 us -> 133 us (1.081)
  starting transfers between devices: 52.9 us -> 60.2 us
  waiting for transfers between devices: 20 us -> 14.2 us
  local copies, waits for them, and re-layouts: 6.84 us -> 11.7 us
  blocking collectives: 18.8 us -> 22.3 us
    all_to_all x1, waiting for transfers between devices: 8.44 us -> 1.46 us  [exchange(): lax.all_to_all(x, ('grp', 'dev'), split_axis=0, concat_axis=0, tiled=True...]
    unnamed x22 -> x36, local copies, waits for them, and re-layouts: 4.26 us -> 10.7 us
    ppermute x18, waiting for transfers between devices: 7.95 us -> 12.8 us  [shift(): return lax.ppermute(x, ('grp', 'dev'), perm)]
    all_to_all x1, starting transfers between devices: 11.5 us -> 15.8 us  [exchange(): lax.all_to_all(x, ('grp', 'dev'), split_axis=0, concat_axis=0, tiled=True...]
    all_to_all x1, waiting for transfers between devices: 3.58 us -> 0.01 us  [local(): lax.all_to_all(after(info, got), ('grp', 'dev'), split_axis=0, concat_axi...]
    all_to_all x1, blocking collectives: 18.8 us -> 22.3 us  [exchange(): lax.all_to_all(x, ('grp', 'dev'), split_axis=0, concat_axis=0, tiled=True...]
    ppermute x18, starting transfers between devices: 29.9 us -> 33.1 us  [shift(): return lax.ppermute(x, ('grp', 'dev'), perm)]
    slice x2 -> x0, local copies, waits for them, and re-layouts: 1.43 us -> none  [local(): h2, h2b = (along_x(h1[:128], 1), along_x(h3[128:], 3))]
  transfers between devices with their start and end apart: 20 -> 20, of which waited for: 12 -> 8; matrix products, arithmetic and copies ran while one was open for 2% -> 1% of each run, Pallas kernels for 5% -> 5%
where the time goes in v4:
time: 133 us; the launch traced here: 132 us
  starting transfers between devices  60.2 us (45%)
  blocking collectives  22.3 us (17%)
  Pallas kernels  21 us (16%)
  waiting for transfers between devices  14.2 us (11%)
  local copies, waits for them, and re-layouts  11.7 us (9%)
  between operations  1.5 us (1%)
    ppermute x18, starting transfers between devices, shift(): return lax.ppermute(x, ('grp', 'dev'), perm)  33.1 us
    all_to_all x1, blocking collectives, exchange(): lax.all_to_all(x, ('grp', 'dev'), split_axis=0, concat_axis=0, tiled=True...  22.3 us
    pallas_call x6, Pallas kernels, call(): pl.pallas_call(kernel, out_shape=out, in_specs=[pl.BlockSpec(memory_space...  21 us
    all_to_all x1, starting transfers between devices, exchange(): lax.all_to_all(x, ('grp', 'dev'), split_axis=0, concat_axis=0, tiled=True...  15.8 us
    ppermute x18, waiting for transfers between devices, shift(): return lax.ppermute(x, ('grp', 'dev'), perm)  12.8 us
    all_to_all x1, starting transfers between devices, local(): lax.all_to_all(after(info, got), ('grp', 'dev'), split_axis=0, concat_axi...  11.3 us
    unnamed x36, local copies, waits for them, and re-layouts  10.7 us
  transfers between devices with their start and end apart: 20, of which 8 were waited for; matrix products, arithmetic and copies ran while one was open for 1% of the time, Pallas kernels for 5%

profile of v4, /device:TPU:1, one launch (start us, length us, event | category | flops | bytes accessed | tf_op | source)
XLA Modules:
  0.0 131.7 jit_solution(4927519706545690)
XLA Ops:
  0.0 2.0 %collective-permute-start = (bf16[256,1024]{1,0:T(8,128)(2,1)}, bf16[256,1024]{1,0:T(8,128)(2,1)S(1)}, u32[]{:S(2)}, u32[]{:S(2)}) collective-permute-start(bf16[256,1024]{1,0:T(8,128)(2,1)} %bitcast.15), channel_id=1, source_target_pairs={{0,8},{1,9},{2,10},{3,11},{4,12},{5,13},{6,14},{7,15},{8,16},{9,17... | collective-permute-start | bytes 1572872 | tf_op jit(solution)/shard_map/ppermute | solution.py:219
  2.0 1.3 collective-permute-start.2
  4.7 1.0 copy-done.1
  5.8 0.9 copy-done.3
  7.3 5.9 %collective-permute-start.3 = (bf16[128,384]{1,0:T(8,128)(2,1)S(1)}, bf16[128,384]{1,0:T(8,128)(2,1)S(1)}, u32[]{:S(2)}, u32[]{:S(2)}) collective-permute-start(bf16[128,384]{1,0:T(8,128)(2,1)S(1)} %shard_map.91), channel_id=1, source_target_pairs={{0,134},{1,135},{2,132},{3,133},{4,130},{5,131},{6,128},{7,129},{8... | collective-permute-start | bytes 294920 | tf_op jit(solution)/shard_map/ppermute | solution.py:219
  13.9 4.1 %collective-permute-done.3 = bf16[128,384]{1,0:T(8,128)(2,1)S(1)} collective-permute-done((bf16[128,384]{1,0:T(8,128)(2,1)S(1)}, bf16[128,384]{1,0:T(8,128)(2,1)S(1)}, u32[]{:S(2)}, u32[]{:S(2)}) %collective-permute-start.3) | collective-permute-done | bytes 98336 | tf_op jit(solution)/shard_map/ppermute | solution.py:219
  18.0 11.3 %all-to-all-start = ((f32[256,1,128]{2,1,0:T(1,128)}), f32[256,1,128]{2,1,0:T(1,128)S(1)}, u32[]{:S(2)}, u32[]{:S(2)}) async-start(f32[256,1,128]{2,1,0:T(1,128)} %fusion), calls=%async_computation | async-start | bytes 262144 | tf_op jit(solution)/shard_map/all_to_all | solution.py:259
  29.4 1.5 %collective-permute-start.1 = (bf16[256,1024]{1,0:T(8,128)(2,1)S(1)}, bf16[256,1024]{1,0:T(8,128)(2,1)S(1)}, u32[]{:S(2)}, u32[]{:S(2)}) collective-permute-start(bf16[256,1024]{1,0:T(8,128)(2,1)S(1)} %collective-permute-done.h1), channel_id=1, source_target_pairs={{0,8},{1,9},{2,10},{3,11},{4,12},{5,13},{6,14},{7,15},{8,16},{9,17... | collective-permute-start | bytes 1572872 | tf_op jit(solution)/shard_map/ppermute | solution.py:219
  30.9 1.3 collective-permute-start.4
  32.1 2.5 %collective-permute-start.5 = (bf16[256,384]{1,0:T(8,128)(2,1)S(1)}, bf16[256,384]{1,0:T(8,128)(2,1)}, u32[]{:S(2)}, u32[]{:S(2)}) collective-permute-start(bf16[256,384]{1,0:T(8,128)(2,1)S(1)} %pad_maximum_fusion.n0), channel_id=1, source_target_pairs={{0,64},{1,65},{2,66},{3,67},{4,68},{5,69},{6,70},{7,71},{8,72},{9,... | collective-permute-start | bytes 589832 | tf_op jit(solution)/shard_map/ppermute | solution.py:219
  34.6 1.1 collective-permute-start.6
  35.7 7.5 %collective-permute-start.7 = (bf16[128,1024]{1,0:T(8,128)(2,1)}, bf16[128,1024]{1,0:T(8,128)(2,1)S(1)}, u32[]{:S(2)}, u32[]{:S(2)}) collective-permute-start(bf16[128,1024]{1,0:T(8,128)(2,1)} %param.12), channel_id=1, source_target_pairs={{0,0},{1,134},{2,2},{3,132},{4,4},{5,130},{6,6},{7,128},{8,32},{9,... | collective-permute-start | bytes 786440 | tf_op jit(solution)/shard_map/ppermute | solution.py:219
  43.3 1.3 shard_map.93
  44.6 1.3 collective-permute-start.13
  45.9 4.5 %collective-permute-done.7.out_ref = bf16[128,1024]{1,0:T(8,128)(2,1)S(1)} collective-permute-done((bf16[128,1024]{1,0:T(8,128)(2,1)}, bf16[128,1024]{1,0:T(8,128)(2,1)S(1)}, u32[]{:S(2)}, u32[]{:S(2)}) %collective-permute-start.7) | collective-permute-done | bytes 262176 | tf_op jit(solution)/shard_map/ppermute | solution.py:219
  56.1 15.8 %all-to-all-start.1 = ((bf16[32,4,1024]{2,1,0:T(4,128)(2,1)}), bf16[32,4,1024]{2,1,0:T(4,128)(2,1)S(1)}, u32[]{:S(2)}, u32[]{:S(2)}) async-start(bf16[32,4,1024]{2,1,0:T(4,128)(2,1)} %reshape.60), calls=%async_computation.1 | async-start | bytes 524288 | tf_op jit(solution)/shard_map/all_to_all | solution.py:27
  77.2 4.9 %shard_map.92.part_ref = f32[4,1024]{1,0:T(4,128)S(1)} custom-call(s32[7]{0:T(128)S(1)} %copy-done.15, bf16[256,1024]{1,0:T(8,128)(2,1)S(1)} %bitcast.17, bf16[256,1024]{1,0:T(8,128)(2,1)S(1)} %collective-permute-done.h1, bf16[256,1024]{1,0:T(8,128)(2,1)S(1)} %collective-permute-done.1.h2, bf16[256,1024]{1,0:T(8,128)(2,1)S(1)} %collective-permute-done.2.h3, ...), custom_call_target="tpu_custom_call" | custom-call | flops 1073741824 | bytes 1048576 | tf_op jit(solution)/shard_map/pallas_call | solution.py:43
  82.1 1.5 %all-to-all-done.1.old_ref = bf16[32,4,1024]{2,1,0:T(4,128)(2,1)S(1)} async-done(((bf16[32,4,1024]{2,1,0:T(4,128)(2,1)}), bf16[32,4,1024]{2,1,0:T(4,128)(2,1)S(1)}, u32[]{:S(2)}, u32[]{:S(2)}) %all-to-all-start.1) | async-done | bytes 262176 | tf_op jit(solution)/shard_map/all_to_all | solution.py:27
  83.8 2.6 %collective-permute-start.15 = (f32[8,1024]{1,0:T(8,128)S(1)}, f32[8,1024]{1,0:T(8,128)S(1)}, u32[]{:S(2)}, u32[]{:S(2)}) collective-permute-start(f32[8,1024]{1,0:T(8,128)S(1)} %shard_map.94.t0), channel_id=1, source_target_pairs={{0,16},{1,17},{2,18},{3,19},{4,20},{5,21},{6,22},{7,23},{8,24},{9,... | collective-permute-start | bytes 98312 | tf_op jit(solution)/shard_map/ppermute | solution.py:219
  88.1 1.0 collective-permute-done.16.t3
  89.5 22.3 %all_to_all.15 = bf16[32,8,1024]{2,1,0:T(8,128)(2,1)S(1)} all-to-all(bf16[32,8,1024]{2,1,0:T(8,128)(2,1)S(1)} %broadcast_in_dim.21), channel_id=1, replica_groups={{0,32,64,96,2,34,66,98,4,36,68,100,6,38,70,102,128,160,192,224,130,162,..., dimensions={0} | all-to-all | bytes 1048576 | tf_op jit(solution)/shard_map/all_to_all | solution.py:27
  111.8 4.6 %collective-permute-start.17 = (bf16[32,8,1024]{2,1,0:T(8,128)(2,1)S(1)}, bf16[32,8,1024]{2,1,0:T(8,128)(2,1)S(1)}, u32[]{:S(2)}, u32[]{:S(2)}) collective-permute-start(bf16[32,8,1024]{2,1,0:T(8,128)(2,1)S(1)} %all_to_all.15), channel_id=1, source_target_pairs={{0,1},{1,0},{2,3},{3,2},{4,5},{5,4},{6,7},{7,6},{8,9},{9,8},{10,11... | collective-permute-start | bytes 1572872 | tf_op jit(solution)/shard_map/ppermute | solution.py:219
  116.3 1.5 %collective-permute-done.17 = bf16[32,8,1024]{2,1,0:T(8,128)(2,1)S(1)} collective-permute-done((bf16[32,8,1024]{2,1,0:T(8,128)(2,1)S(1)}, bf16[32,8,1024]{2,1,0:T(8,128)(2,1)S(1)}, u32[]{:S(2)}, u32[]{:S(2)}) %collective-permute-start.17) | collective-permute-done | bytes 524320 | tf_op jit(solution)/shard_map/ppermute | solution.py:219
  117.9 13.9 %shard_map.96 = bf16[256,1024]{1,0:T(8,128)(2,1)} custom-call(bf16[256,1024]{1,0:T(8,128)(2,1)S(1)} %bitcast.18, bf16[256,1024]{1,0:T(8,128)(2,1)S(1)} %bitcast.22, bf16[256,1024]{1,0:T(8,128)(2,1)S(1)} %copy-done.2), custom_call_target="tpu_custom_call" | custom-call | flops 2147483648 | bytes 1048576 | tf_op jit(solution)/shard_map/pallas_call | solution.py:43
  (67 shorter events, 14.8 us)
Async XLA Ops:
  0.0 29.4 %collective-permute-start = (bf16[256,1024]{1,0:T(8,128)(2,1)}, bf16[256,1024]{1,0:T(8,128)(2,1)S(1)}, u32[]{:S(2)}, u32[]{:S(2)}) collective-permute-start(bf16[256,1024]{1,0:T(8,128)(2,1)} %bitcast.15), channel_id=1, source_target_pairs={{0,8},{1,9},{2,10},{3,11},{4,12},{5,13},{6,14},{7,15},{8,16},{9,17... | collective-permute-start | bytes 1572872 | tf_op jit(solution)/shard_map/ppermute | solution.py:219
  2.0 28.8 %collective-permute-start.2 = (bf16[256,1024]{1,0:T(8,128)(2,1)}, bf16[256,1024]{1,0:T(8,128)(2,1)S(1)}, u32[]{:S(2)}, u32[]{:S(2)}) collective-permute-start(bf16[256,1024]{1,0:T(8,128)(2,1)} %bitcast.16), channel_id=1, source_target_pairs={{0,24},{1,25},{2,26},{3,27},{4,28},{5,29},{6,30},{7,31},{8,0},{9,1... | collective-permute-start | bytes 1572872 | tf_op jit(solution)/shard_map/ppermute | solution.py:219
  6.7 36.6 %copy-start.14 = (s32[7]{0:T(128)}, s32[7]{0:T(128)S(1)}, u32[]{:S(2)}) copy-start(s32[7]{0:T(128)S(1)} %stack.23.where) | copy-start | bytes 88
  7.3 36.0 %copy-start.2 = (bf16[256,1024]{1,0:T(8,128)(2,1)S(1)}, bf16[256,1024]{1,0:T(8,128)(2,1)}, u32[]{:S(2)}) copy-start(bf16[256,1024]{1,0:T(8,128)(2,1)} %bank_ref.3) | copy-start | bytes 1572868
  7.3 10.7 %collective-permute-start.3 = (bf16[128,384]{1,0:T(8,128)(2,1)S(1)}, bf16[128,384]{1,0:T(8,128)(2,1)S(1)}, u32[]{:S(2)}, u32[]{:S(2)}) collective-permute-start(bf16[128,384]{1,0:T(8,128)(2,1)S(1)} %shard_map.91), channel_id=1, source_target_pairs={{0,134},{1,135},{2,132},{3,133},{4,130},{5,131},{6,128},{7,129},{8... | collective-permute-start | bytes 294920 | tf_op jit(solution)/shard_map/ppermute | solution.py:219
  18.0 25.2 %all-to-all-start = ((f32[256,1,128]{2,1,0:T(1,128)}), f32[256,1,128]{2,1,0:T(1,128)S(1)}, u32[]{:S(2)}, u32[]{:S(2)}) async-start(f32[256,1,128]{2,1,0:T(1,128)} %fusion), calls=%async_computation | async-start | bytes 262144 | tf_op jit(solution)/shard_map/all_to_all | solution.py:259
  29.4 21.5 %collective-permute-start.1 = (bf16[256,1024]{1,0:T(8,128)(2,1)S(1)}, bf16[256,1024]{1,0:T(8,128)(2,1)S(1)}, u32[]{:S(2)}, u32[]{:S(2)}) collective-permute-start(bf16[256,1024]{1,0:T(8,128)(2,1)S(1)} %collective-permute-done.h1), channel_id=1, source_target_pairs={{0,8},{1,9},{2,10},{3,11},{4,12},{5,13},{6,14},{7,15},{8,16},{9,17... | collective-permute-start | bytes 1572872 | tf_op jit(solution)/shard_map/ppermute | solution.py:219
  30.9 13.7 %collective-permute-start.4 = (bf16[256,384]{1,0:T(8,128)(2,1)S(1)}, bf16[256,384]{1,0:T(8,128)(2,1)S(1)}, u32[]{:S(2)}, u32[]{:S(2)}) collective-permute-start(bf16[256,384]{1,0:T(8,128)(2,1)S(1)} %pad_maximum_fusion.n0), channel_id=1, source_target_pairs={{0,32},{1,33},{2,34},{3,35},{4,36},{5,37},{6,38},{7,39},{8,40},{9,... | collective-permute-start | bytes 589832 | tf_op jit(solution)/shard_map/ppermute | solution.py:219
  32.1 12.4 %collective-permute-start.5 = (bf16[256,384]{1,0:T(8,128)(2,1)S(1)}, bf16[256,384]{1,0:T(8,128)(2,1)}, u32[]{:S(2)}, u32[]{:S(2)}) collective-permute-start(bf16[256,384]{1,0:T(8,128)(2,1)S(1)} %pad_maximum_fusion.n0), channel_id=1, source_target_pairs={{0,64},{1,65},{2,66},{3,67},{4,68},{5,69},{6,70},{7,71},{8,72},{9,... | collective-permute-start | bytes 589832 | tf_op jit(solution)/shard_map/ppermute | solution.py:219
  34.6 10.0 %collective-permute-start.6 = (bf16[256,384]{1,0:T(8,128)(2,1)S(1)}, bf16[256,384]{1,0:T(8,128)(2,1)}, u32[]{:S(2)}, u32[]{:S(2)}) collective-permute-start(bf16[256,384]{1,0:T(8,128)(2,1)S(1)} %pad_maximum_fusion.n0), channel_id=1, source_target_pairs={{0,96},{1,97},{2,98},{3,99},{4,100},{5,101},{6,102},{7,103},{8,104... | collective-permute-start | bytes 589832 | tf_op jit(solution)/shard_map/ppermute | solution.py:219
  35.7 14.6 %collective-permute-start.7 = (bf16[128,1024]{1,0:T(8,128)(2,1)}, bf16[128,1024]{1,0:T(8,128)(2,1)S(1)}, u32[]{:S(2)}, u32[]{:S(2)}) collective-permute-start(bf16[128,1024]{1,0:T(8,128)(2,1)} %param.12), channel_id=1, source_target_pairs={{0,0},{1,134},{2,2},{3,132},{4,4},{5,130},{6,6},{7,128},{8,32},{9,... | collective-permute-start | bytes 786440 | tf_op jit(solution)/shard_map/ppermute | solution.py:219
  44.6 6.8 %collective-permute-start.13 = (bf16[128,1024]{1,0:T(8,128)(2,1)S(1)}, bf16[128,1024]{1,0:T(8,128)(2,1)S(1)}, u32[]{:S(2)}, u32[]{:S(2)}) collective-permute-start(bf16[128,1024]{1,0:T(8,128)(2,1)S(1)} %get-tuple-element.17), channel_id=1, source_target_pairs={{0,1},{1,0},{2,3},{3,2},{4,5},{5,4},{6,7},{7,6},{8,9},{9,8},{10,11... | collective-permute-start | bytes 786440 | tf_op jit(solution)/shard_map/ppermute | solution.py:219
  50.3 1.5 %collective-permute-start.12 = (bf16[128,1024]{1,0:T(8,128)(2,1)S(1)}, bf16[128,1024]{1,0:T(8,128)(2,1)S(1)}, u32[]{:S(2)}, u32[]{:S(2)}) collective-permute-start(bf16[128,1024]{1,0:T(8,128)(2,1)S(1)} %collective-permute-done.7.out_ref), channel_id=1, source_target_pairs={{0,1},{1,0},{2,3},{3,2},{4,5},{5,4},{6,7},{7,6},{8,9},{9,8},{10,11... | collective-permute-start | bytes 786440 | tf_op jit(solution)/shard_map/ppermute | solution.py:219
  50.3 2.2 %collective-permute-start.9 = (bf16[256,384]{1,0:T(8,128)(2,1)S(1)}, bf16[256,384]{1,0:T(8,128)(2,1)S(1)}, u32[]{:S(2)}, u32[]{:S(2)}) collective-permute-start(bf16[256,384]{1,0:T(8,128)(2,1)S(1)} %collective-permute-done.4.n1), channel_id=1, source_target_pairs={{0,1},{1,0},{2,3},{3,2},{4,5},{5,4},{6,7},{7,6},{8,9},{9,8},{10,11... | collective-permute-start | bytes 589832 | tf_op jit(solution)/shard_map/ppermute | solution.py:219
  50.8 2.4 %collective-permute-start.10 = (bf16[256,384]{1,0:T(8,128)(2,1)}, bf16[256,384]{1,0:T(8,128)(2,1)S(1)}, u32[]{:S(2)}, u32[]{:S(2)}) collective-permute-start(bf16[256,384]{1,0:T(8,128)(2,1)} %collective-permute-done.5.n2), channel_id=1, source_target_pairs={{0,1},{1,0},{2,3},{3,2},{4,5},{5,4},{6,7},{7,6},{8,9},{9,8},{10,11... | collective-permute-start | bytes 589832 | tf_op jit(solution)/shard_map/ppermute | solution.py:219
  50.8 3.1 %collective-permute-start.11 = (bf16[256,384]{1,0:T(8,128)(2,1)}, bf16[256,384]{1,0:T(8,128)(2,1)S(1)}, u32[]{:S(2)}, u32[]{:S(2)}) collective-permute-start(bf16[256,384]{1,0:T(8,128)(2,1)} %collective-permute-done.6.n3), channel_id=1, source_target_pairs={{0,1},{1,0},{2,3},{3,2},{4,5},{5,4},{6,7},{7,6},{8,9},{9,8},{10,11... | collective-permute-start | bytes 589832 | tf_op jit(solution)/shard_map/ppermute | solution.py:219
  51.3 3.3 %collective-permute-start.8 = (bf16[256,384]{1,0:T(8,128)(2,1)S(1)}, bf16[256,384]{1,0:T(8,128)(2,1)S(1)}, u32[]{:S(2)}, u32[]{:S(2)}) collective-permute-start(bf16[256,384]{1,0:T(8,128)(2,1)S(1)} %pad_maximum_fusion.n0), channel_id=1, source_target_pairs={{0,1},{1,0},{2,3},{3,2},{4,5},{5,4},{6,7},{7,6},{8,9},{9,8},{10,11... | collective-permute-start | bytes 589832 | tf_op jit(solution)/shard_map/ppermute | solution.py:219
  51.5 20.4 %copy-start = (bf16[1,256,1024]{2,1,0:T(8,128)(2,1)S(1)}, bf16[1,256,1024]{2,1,0:T(8,128)(2,1)}, u32[]{:S(2)}) copy-start(bf16[1,256,1024]{2,1,0:T(8,128)(2,1)} %param.9) | copy-start | bytes 1572868
  56.1 27.4 %all-to-all-start.1 = ((bf16[32,4,1024]{2,1,0:T(4,128)(2,1)}), bf16[32,4,1024]{2,1,0:T(4,128)(2,1)S(1)}, u32[]{:S(2)}, u32[]{:S(2)}) async-start(bf16[32,4,1024]{2,1,0:T(4,128)(2,1)} %reshape.60), calls=%async_computation.1 | async-start | bytes 524288 | tf_op jit(solution)/shard_map/all_to_all | solution.py:27
  83.5 5.6 %copy-start.17 = (f32[1024]{0:T(1024)S(1)}, f32[1024]{0:T(1024)}, u32[]{:S(2)}) copy-start(f32[1024]{0:T(1024)} %param.14) | copy-start | bytes 12292
  83.7 4.0 %collective-permute-start.14 = (f32[8,1024]{1,0:T(8,128)S(1)}, f32[8,1024]{1,0:T(8,128)S(1)}, u32[]{:S(2)}, u32[]{:S(2)}) collective-permute-start(f32[8,1024]{1,0:T(8,128)S(1)} %shard_map.94.t0), channel_id=1, source_target_pairs={{0,8},{1,9},{2,10},{3,11},{4,12},{5,13},{6,14},{7,15},{8,16},{9,17... | collective-permute-start | bytes 98312 | tf_op jit(solution)/shard_map/ppermute | solution.py:219
  83.8 4.4 %collective-permute-start.15 = (f32[8,1024]{1,0:T(8,128)S(1)}, f32[8,1024]{1,0:T(8,128)S(1)}, u32[]{:S(2)}, u32[]{:S(2)}) collective-permute-start(f32[8,1024]{1,0:T(8,128)S(1)} %shard_map.94.t0), channel_id=1, source_target_pairs={{0,16},{1,17},{2,18},{3,19},{4,20},{5,21},{6,22},{7,23},{8,24},{9,... | collective-permute-start | bytes 98312 | tf_op jit(solution)/shard_map/ppermute | solution.py:219
  86.3 2.8 %collective-permute-start.16 = (f32[8,1024]{1,0:T(8,128)S(1)}, f32[8,1024]{1,0:T(8,128)S(1)}, u32[]{:S(2)}, u32[]{:S(2)}) collective-permute-start(f32[8,1024]{1,0:T(8,128)S(1)} %shard_map.94.t0), channel_id=1, source_target_pairs={{0,24},{1,25},{2,26},{3,27},{4,28},{5,29},{6,30},{7,31},{8,0},{9,1... | collective-permute-start | bytes 98312 | tf_op jit(solution)/shard_map/ppermute | solution.py:219
  111.8 6.1 %collective-permute-start.17 = (bf16[32,8,1024]{2,1,0:T(8,128)(2,1)S(1)}, bf16[32,8,1024]{2,1,0:T(8,128)(2,1)S(1)}, u32[]{:S(2)}, u32[]{:S(2)}) collective-permute-start(bf16[32,8,1024]{2,1,0:T(8,128)(2,1)S(1)} %all_to_all.15), channel_id=1, source_target_pairs={{0,1},{1,0},{2,3},{3,2},{4,5},{5,4},{6,7},{7,6},{8,9},{9,8},{10,11... | collective-permute-start | bytes 1572872 | tf_op jit(solution)/shard_map/ppermute | solution.py:219
  (14 other events, 16.3 us)

commit v5 on v4

--- a/solution.py
+++ b/solution.py
@@ -247,10 +247,10 @@
     own = call(cut_kernel, shape((CUT, 3 * CUT), BF), 2**10, w_query, w_keyval, where=where)
     out1 = shift(w_out, lambda zh, y, xx, zl, c: (c, xx, y, zl if c == zh else 3 - zl, zh))
     got = mirror(own)
-    own = after(jnp.concatenate([own, got], axis=0), h1, h3)
+    own = after(jnp.concatenate([own, got], axis=0), h1, h3, out1)
     out2 = other_core(out1)
     near = [along_y(own, k) for k in range(4)]
-    near[0] = after(near[0], *near[1:], out1, h2)
+    near[0] = after(near[0], *near[1:], h2)
     far = [other_core(w) for w in near]
 
     place = (((c * 2 + zh) * 4 + zl) * 4 + y) * 4 + x
@@ -262,7 +262,7 @@
         pick_kernel, [half, half], 2**27, info, bank, where=where, scratch=[pltpu.VMEM((PLACES, PLACES), F32)]
     )
     rows = keep + other_core(after(give, *near[1:]))
-    rows = exchange(after(rows, *far, out2).reshape(32, 4, WIDTH), 1)
+    rows = exchange(after(rows, *near[1:], h2).reshape(32, 4, WIDTH), 1)
 
     part = call(
         encode_kernel,

time: 133 us -> 119 us (0.89)
  local copies, waits for them, and re-layouts: 11.7 us -> 3.61 us
  starting transfers between devices: 60.2 us -> 54.2 us
  waiting for transfers between devices: 14.2 us -> 16.1 us
  blocking collectives: 22.3 us -> 20.9 us
    unnamed x36 -> x18, local copies, waits for them, and re-layouts: 10.7 us -> 2.65 us
    all_to_all x1, starting transfers between devices: 15.8 us -> 8.82 us  [exchange(): lax.all_to_all(x, ('grp', 'dev'), split_axis=0, concat_axis=0, tiled=True...]
    all_to_all x1, waiting for transfers between devices: 0.01 us -> 6.36 us  [local(): lax.all_to_all(after(info, got), ('grp', 'dev'), split_axis=0, concat_axi...]
    ppermute x18, waiting for transfers between devices: 12.8 us -> 6.69 us  [shift(): return lax.ppermute(x, ('grp', 'dev'), perm)]
    all_to_all x1, starting transfers between devices: 11.3 us -> 14.5 us  [local(): lax.all_to_all(after(info, got), ('grp', 'dev'), split_axis=0, concat_axi...]
    ppermute x18, starting transfers between devices: 33.1 us -> 30.9 us  [shift(): return lax.ppermute(x, ('grp', 'dev'), perm)]
    all_to_all x1, waiting for transfers between devices: 1.46 us -> 3.03 us  [exchange(): lax.all_to_all(x, ('grp', 'dev'), split_axis=0, concat_axis=0, tiled=True...]
    all_to_all x1, blocking collectives: 22.3 us -> 20.9 us  [exchange(): lax.all_to_all(x, ('grp', 'dev'), split_axis=0, concat_axis=0, tiled=True...]
  transfers between devices with their start and end apart: 20 -> 20, of which waited for: 8 -> 13; matrix products, arithmetic and copies ran while one was open for 1% -> 1% of each run, Pallas kernels for 5% -> 6%
where the time goes in v5:
time: 119 us; the launch traced here: 118 us
  starting transfers between devices  54.2 us (46%)
  Pallas kernels  21 us (18%)
  blocking collectives  20.9 us (18%)
  waiting for transfers between devices  16.1 us (14%)
  local copies, waits for them, and re-layouts  3.61 us (3%)
  between operations  1.51 us (1%)
    ppermute x18, starting transfers between devices, shift(): return lax.ppermute(x, ('grp', 'dev'), perm)  30.9 us
    pallas_call x6, Pallas kernels, call(): pl.pallas_call(kernel, out_shape=out, in_specs=[pl.BlockSpec(memory_space...  21 us
    all_to_all x1, blocking collectives, exchange(): lax.all_to_all(x, ('grp', 'dev'), split_axis=0, concat_axis=0, tiled=True...  20.9 us
    all_to_all x1, starting transfers between devices, local(): lax.all_to_all(after(info, got), ('grp', 'dev'), split_axis=0, concat_axi...  14.5 us
    all_to_all x1, starting transfers between devices, exchange(): lax.all_to_all(x, ('grp', 'dev'), split_axis=0, concat_axis=0, tiled=True...  8.82 us
    ppermute x18, waiting for transfers between devices, shift(): return lax.ppermute(x, ('grp', 'dev'), perm)  6.69 us
    all_to_all x1, waiting for transfers between devices, local(): lax.all_to_all(after(info, got), ('grp', 'dev'), split_axis=0, concat_axi...  6.36 us
    all_to_all x1, waiting for transfers between devices, exchange(): lax.all_to_all(x, ('grp', 'dev'), split_axis=0, concat_axis=0, tiled=True...  3.03 us
  transfers between devices with their start and end apart: 20, of which 13 were waited for; matrix products, arithmetic and copies ran while one was open for 1% of the time, Pallas kernels for 6%

profile of v5, /device:TPU:1, one launch (start us, length us, event | category | flops | bytes accessed | tf_op | source)
XLA Modules:
  0.0 118.1 jit_solution(14400860450166968002)
XLA Ops:
  0.0 2.0 %collective-permute-start = (bf16[256,1024]{1,0:T(8,128)(2,1)}, bf16[256,1024]{1,0:T(8,128)(2,1)S(1)}, u32[]{:S(2)}, u32[]{:S(2)}) collective-permute-start(bf16[256,1024]{1,0:T(8,128)(2,1)} %bitcast.15), channel_id=1, source_target_pairs={{0,8},{1,9},{2,10},{3,11},{4,12},{5,13},{6,14},{7,15},{8,16},{9,17... | collective-permute-start | bytes 1572872 | tf_op jit(solution)/shard_map/ppermute | solution.py:219
  2.0 1.3 %collective-permute-start.2 = (bf16[256,1024]{1,0:T(8,128)(2,1)}, bf16[256,1024]{1,0:T(8,128)(2,1)S(1)}, u32[]{:S(2)}, u32[]{:S(2)}) collective-permute-start(bf16[256,1024]{1,0:T(8,128)(2,1)} %bitcast.16), channel_id=1, source_target_pairs={{0,24},{1,25},{2,26},{3,27},{4,28},{5,29},{6,30},{7,31},{8,0},{9,1... | collective-permute-start | bytes 1572872 | tf_op jit(solution)/shard_map/ppermute | solution.py:219
  4.7 1.0 copy-done.1
  7.3 5.9 %collective-permute-start.3 = (bf16[128,384]{1,0:T(8,128)(2,1)S(1)}, bf16[128,384]{1,0:T(8,128)(2,1)S(1)}, u32[]{:S(2)}, u32[]{:S(2)}) collective-permute-start(bf16[128,384]{1,0:T(8,128)(2,1)S(1)} %shard_map.91), channel_id=1, source_target_pairs={{0,134},{1,135},{2,132},{3,133},{4,130},{5,131},{6,128},{7,129},{8... | collective-permute-start | bytes 294920 | tf_op jit(solution)/shard_map/ppermute | solution.py:219
  13.2 3.3 %collective-permute-start.4 = (bf16[128,1024]{1,0:T(8,128)(2,1)S(1)}, bf16[128,1024]{1,0:T(8,128)(2,1)S(1)}, u32[]{:S(2)}, u32[]{:S(2)}) collective-permute-start(bf16[128,1024]{1,0:T(8,128)(2,1)S(1)} %copy-done.8), channel_id=1, source_target_pairs={{0,0},{1,134},{2,2},{3,132},{4,4},{5,130},{6,6},{7,128},{8,32},{9,... | collective-permute-start | bytes 786440 | tf_op jit(solution)/shard_map/ppermute | solution.py:219
  18.0 14.5 %all-to-all-start = ((f32[256,1,128]{2,1,0:T(1,128)}), f32[256,1,128]{2,1,0:T(1,128)S(1)}, u32[]{:S(2)}, u32[]{:S(2)}) async-start(f32[256,1,128]{2,1,0:T(1,128)} %fusion), calls=%async_computation | async-start | bytes 262144 | tf_op jit(solution)/shard_map/all_to_all | solution.py:259
  32.5 1.5 %collective-permute-start.1 = (bf16[256,1024]{1,0:T(8,128)(2,1)S(1)}, bf16[256,1024]{1,0:T(8,128)(2,1)S(1)}, u32[]{:S(2)}, u32[]{:S(2)}) collective-permute-start(bf16[256,1024]{1,0:T(8,128)(2,1)S(1)} %collective-permute-done.h1), channel_id=1, source_target_pairs={{0,8},{1,9},{2,10},{3,11},{4,12},{5,13},{6,14},{7,15},{8,16},{9,17... | collective-permute-start | bytes 1572872 | tf_op jit(solution)/shard_map/ppermute | solution.py:219
  34.0 1.3 %collective-permute-start.5 = (bf16[256,384]{1,0:T(8,128)(2,1)S(1)}, bf16[256,384]{1,0:T(8,128)(2,1)S(1)}, u32[]{:S(2)}, u32[]{:S(2)}) collective-permute-start(bf16[256,384]{1,0:T(8,128)(2,1)S(1)} %pad_maximum_fusion.n0), channel_id=1, source_target_pairs={{0,32},{1,33},{2,34},{3,35},{4,36},{5,37},{6,38},{7,39},{8,40},{9,... | collective-permute-start | bytes 589832 | tf_op jit(solution)/shard_map/ppermute | solution.py:219
  35.3 2.5 %collective-permute-start.6 = (bf16[256,384]{1,0:T(8,128)(2,1)S(1)}, bf16[256,384]{1,0:T(8,128)(2,1)}, u32[]{:S(2)}, u32[]{:S(2)}) collective-permute-start(bf16[256,384]{1,0:T(8,128)(2,1)S(1)} %pad_maximum_fusion.n0), channel_id=1, source_target_pairs={{0,64},{1,65},{2,66},{3,67},{4,68},{5,69},{6,70},{7,71},{8,72},{9,... | collective-permute-start | bytes 589832 | tf_op jit(solution)/shard_map/ppermute | solution.py:219
  37.7 1.1 collective-permute-start.7
  38.9 6.4 %all-to-all-done = f32[256,1,128]{2,1,0:T(1,128)S(1)} async-done(((f32[256,1,128]{2,1,0:T(1,128)}), f32[256,1,128]{2,1,0:T(1,128)S(1)}, u32[]{:S(2)}, u32[]{:S(2)}) %all-to-all-start) | async-done | bytes 131104 | tf_op jit(solution)/shard_map/all_to_all | solution.py:259
  45.2 1.3 %shard_map.93 = (bf16[128,1024]{1,0:T(8,128)(2,1)S(1)}, bf16[128,1024]{1,0:T(8,128)(2,1)S(1)}) custom-call(s32[7]{0:T(128)S(1)} %stack.23.where, f32[256,128]{1,0:T(8,128)S(1)} %bitcast.19, bf16[256,1024]{1,0:T(8,128)(2,1)S(1)} %copy-done.2), custom_call_target="tpu_custom_call" | custom-call | flops 134217728 | bytes 1048576 | tf_op jit(solution)/shard_map/pallas_call | solution.py:43
  47.4 1.6 %collective-permute-start.13 = (bf16[128,1024]{1,0:T(8,128)(2,1)S(1)}, bf16[128,1024]{1,0:T(8,128)(2,1)S(1)}, u32[]{:S(2)}, u32[]{:S(2)}) collective-permute-start(bf16[128,1024]{1,0:T(8,128)(2,1)S(1)} %get-tuple-element.17), channel_id=1, source_target_pairs={{0,1},{1,0},{2,3},{3,2},{4,5},{5,4},{6,7},{7,6},{8,9},{9,8},{10,11... | collective-permute-start | bytes 786440 | tf_op jit(solution)/shard_map/ppermute | solution.py:219
  49.0 1.2 collective-permute-done.13
  51.0 8.8 %all-to-all-start.1 = ((bf16[32,4,1024]{2,1,0:T(4,128)(2,1)}), bf16[32,4,1024]{2,1,0:T(4,128)(2,1)S(1)}, u32[]{:S(2)}, u32[]{:S(2)}) async-start(bf16[32,4,1024]{2,1,0:T(4,128)(2,1)} %reshape.60), calls=%async_computation.1 | async-start | bytes 524288 | tf_op jit(solution)/shard_map/all_to_all | solution.py:27
  63.5 4.9 %shard_map.92.part_ref = f32[4,1024]{1,0:T(4,128)S(1)} custom-call(s32[7]{0:T(128)S(1)} %copy-done.5, bf16[256,1024]{1,0:T(8,128)(2,1)S(1)} %bitcast.17, bf16[256,1024]{1,0:T(8,128)(2,1)S(1)} %collective-permute-done.h1, bf16[256,1024]{1,0:T(8,128)(2,1)S(1)} %collective-permute-done.1.h2, bf16[256,1024]{1,0:T(8,128)(2,1)S(1)} %collective-permute-done.2.h3, ...), custom_call_target="tpu_custom_call" | custom-call | flops 1073741824 | bytes 1048576 | tf_op jit(solution)/shard_map/pallas_call | solution.py:43
  68.4 3.0 %all-to-all-done.1.old_ref = bf16[32,4,1024]{2,1,0:T(4,128)(2,1)S(1)} async-done(((bf16[32,4,1024]{2,1,0:T(4,128)(2,1)}), bf16[32,4,1024]{2,1,0:T(4,128)(2,1)S(1)}, u32[]{:S(2)}, u32[]{:S(2)}) %all-to-all-start.1) | async-done | bytes 262176 | tf_op jit(solution)/shard_map/all_to_all | solution.py:27
  71.6 1.3 %collective-permute-start.14 = (f32[8,1024]{1,0:T(8,128)S(1)}, f32[8,1024]{1,0:T(8,128)S(1)}, u32[]{:S(2)}, u32[]{:S(2)}) collective-permute-start(f32[8,1024]{1,0:T(8,128)S(1)} %shard_map.94.t0), channel_id=1, source_target_pairs={{0,8},{1,9},{2,10},{3,11},{4,12},{5,13},{6,14},{7,15},{8,16},{9,17... | collective-permute-start | bytes 98312 | tf_op jit(solution)/shard_map/ppermute | solution.py:219
  72.9 1.5 %collective-permute-start.15 = (f32[8,1024]{1,0:T(8,128)S(1)}, f32[8,1024]{1,0:T(8,128)S(1)}, u32[]{:S(2)}, u32[]{:S(2)}) collective-permute-start(f32[8,1024]{1,0:T(8,128)S(1)} %shard_map.94.t0), channel_id=1, source_target_pairs={{0,16},{1,17},{2,18},{3,19},{4,20},{5,21},{6,22},{7,23},{8,24},{9,... | collective-permute-start | bytes 98312 | tf_op jit(solution)/shard_map/ppermute | solution.py:219
  74.3 1.8 %collective-permute-start.16 = (f32[8,1024]{1,0:T(8,128)S(1)}, f32[8,1024]{1,0:T(8,128)S(1)}, u32[]{:S(2)}, u32[]{:S(2)}) collective-permute-start(f32[8,1024]{1,0:T(8,128)S(1)} %shard_map.94.t0), channel_id=1, source_target_pairs={{0,24},{1,25},{2,26},{3,27},{4,28},{5,29},{6,30},{7,31},{8,0},{9,1... | collective-permute-start | bytes 98312 | tf_op jit(solution)/shard_map/ppermute | solution.py:219
  77.5 20.9 %all_to_all.15 = bf16[32,8,1024]{2,1,0:T(8,128)(2,1)S(1)} all-to-all(bf16[32,8,1024]{2,1,0:T(8,128)(2,1)S(1)} %broadcast_in_dim.21), channel_id=1, replica_groups={{0,32,64,96,2,34,66,98,4,36,68,100,6,38,70,102,128,160,192,224,130,162,..., dimensions={0} | all-to-all | bytes 1048576 | tf_op jit(solution)/shard_map/all_to_all | solution.py:27
  98.4 4.3 %collective-permute-start.17 = (bf16[32,8,1024]{2,1,0:T(8,128)(2,1)S(1)}, bf16[32,8,1024]{2,1,0:T(8,128)(2,1)S(1)}, u32[]{:S(2)}, u32[]{:S(2)}) collective-permute-start(bf16[32,8,1024]{2,1,0:T(8,128)(2,1)S(1)} %all_to_all.15), channel_id=1, source_target_pairs={{0,1},{1,0},{2,3},{3,2},{4,5},{5,4},{6,7},{7,6},{8,9},{9,8},{10,11... | collective-permute-start | bytes 1572872 | tf_op jit(solution)/shard_map/ppermute | solution.py:219
  102.7 1.5 %collective-permute-done.17 = bf16[32,8,1024]{2,1,0:T(8,128)(2,1)S(1)} collective-permute-done((bf16[32,8,1024]{2,1,0:T(8,128)(2,1)S(1)}, bf16[32,8,1024]{2,1,0:T(8,128)(2,1)S(1)}, u32[]{:S(2)}, u32[]{:S(2)}) %collective-permute-start.17) | collective-permute-done | bytes 524320 | tf_op jit(solution)/shard_map/ppermute | solution.py:219
  104.2 13.9 %shard_map.96 = bf16[256,1024]{1,0:T(8,128)(2,1)} custom-call(bf16[256,1024]{1,0:T(8,128)(2,1)S(1)} %bitcast.18, bf16[256,1024]{1,0:T(8,128)(2,1)S(1)} %bitcast.22, bf16[256,1024]{1,0:T(8,128)(2,1)S(1)} %copy-done.2), custom_call_target="tpu_custom_call" | custom-call | flops 2147483648 | bytes 1048576 | tf_op jit(solution)/shard_map/pallas_call | solution.py:43
  (49 shorter events, 10.1 us)
Async XLA Ops:
  0.0 32.5 %collective-permute-start = (bf16[256,1024]{1,0:T(8,128)(2,1)}, bf16[256,1024]{1,0:T(8,128)(2,1)S(1)}, u32[]{:S(2)}, u32[]{:S(2)}) collective-permute-start(bf16[256,1024]{1,0:T(8,128)(2,1)} %bitcast.15), channel_id=1, source_target_pairs={{0,8},{1,9},{2,10},{3,11},{4,12},{5,13},{6,14},{7,15},{8,16},{9,17... | collective-permute-start | bytes 1572872 | tf_op jit(solution)/shard_map/ppermute | solution.py:219
  2.0 32.0 %collective-permute-start.2 = (bf16[256,1024]{1,0:T(8,128)(2,1)}, bf16[256,1024]{1,0:T(8,128)(2,1)S(1)}, u32[]{:S(2)}, u32[]{:S(2)}) collective-permute-start(bf16[256,1024]{1,0:T(8,128)(2,1)} %bitcast.16), channel_id=1, source_target_pairs={{0,24},{1,25},{2,26},{3,27},{4,28},{5,29},{6,30},{7,31},{8,0},{9,1... | collective-permute-start | bytes 1572872 | tf_op jit(solution)/shard_map/ppermute | solution.py:219
  6.7 38.5 %copy-start.4 = (s32[7]{0:T(128)}, s32[7]{0:T(128)S(1)}, u32[]{:S(2)}) copy-start(s32[7]{0:T(128)S(1)} %stack.23.where) | copy-start | bytes 88
  6.7 6.5 %copy-start.8 = (bf16[128,1024]{1,0:T(8,128)(2,1)S(1)}, bf16[128,1024]{1,0:T(8,128)(2,1)}, u32[]{:S(2)}) copy-start(bf16[128,1024]{1,0:T(8,128)(2,1)} %param.12) | copy-start | bytes 786436
  7.3 37.9 %copy-start.2 = (bf16[256,1024]{1,0:T(8,128)(2,1)S(1)}, bf16[256,1024]{1,0:T(8,128)(2,1)}, u32[]{:S(2)}) copy-start(bf16[256,1024]{1,0:T(8,128)(2,1)} %bank_ref.3) | copy-start | bytes 1572868
  7.3 10.7 %collective-permute-start.3 = (bf16[128,384]{1,0:T(8,128)(2,1)S(1)}, bf16[128,384]{1,0:T(8,128)(2,1)S(1)}, u32[]{:S(2)}, u32[]{:S(2)}) collective-permute-start(bf16[128,384]{1,0:T(8,128)(2,1)S(1)} %shard_map.91), channel_id=1, source_target_pairs={{0,134},{1,135},{2,132},{3,133},{4,130},{5,131},{6,128},{7,129},{8... | collective-permute-start | bytes 294920 | tf_op jit(solution)/shard_map/ppermute | solution.py:219
  13.2 20.8 %collective-permute-start.4 = (bf16[128,1024]{1,0:T(8,128)(2,1)S(1)}, bf16[128,1024]{1,0:T(8,128)(2,1)S(1)}, u32[]{:S(2)}, u32[]{:S(2)}) collective-permute-start(bf16[128,1024]{1,0:T(8,128)(2,1)S(1)} %copy-done.8), channel_id=1, source_target_pairs={{0,0},{1,134},{2,2},{3,132},{4,4},{5,130},{6,6},{7,128},{8,32},{9,... | collective-permute-start | bytes 786440 | tf_op jit(solution)/shard_map/ppermute | solution.py:219
  18.0 27.2 %all-to-all-start = ((f32[256,1,128]{2,1,0:T(1,128)}), f32[256,1,128]{2,1,0:T(1,128)S(1)}, u32[]{:S(2)}, u32[]{:S(2)}) async-start(f32[256,1,128]{2,1,0:T(1,128)} %fusion), calls=%async_computation | async-start | bytes 262144 | tf_op jit(solution)/shard_map/all_to_all | solution.py:259
  32.5 17.7 %collective-permute-start.1 = (bf16[256,1024]{1,0:T(8,128)(2,1)S(1)}, bf16[256,1024]{1,0:T(8,128)(2,1)S(1)}, u32[]{:S(2)}, u32[]{:S(2)}) collective-permute-start(bf16[256,1024]{1,0:T(8,128)(2,1)S(1)} %collective-permute-done.h1), channel_id=1, source_target_pairs={{0,8},{1,9},{2,10},{3,11},{4,12},{5,13},{6,14},{7,15},{8,16},{9,17... | collective-permute-start | bytes 1572872 | tf_op jit(solution)/shard_map/ppermute | solution.py:219
  34.0 12.5 %collective-permute-start.5 = (bf16[256,384]{1,0:T(8,128)(2,1)S(1)}, bf16[256,384]{1,0:T(8,128)(2,1)S(1)}, u32[]{:S(2)}, u32[]{:S(2)}) collective-permute-start(bf16[256,384]{1,0:T(8,128)(2,1)S(1)} %pad_maximum_fusion.n0), channel_id=1, source_target_pairs={{0,32},{1,33},{2,34},{3,35},{4,36},{5,37},{6,38},{7,39},{8,40},{9,... | collective-permute-start | bytes 589832 | tf_op jit(solution)/shard_map/ppermute | solution.py:219
  35.3 12.1 %collective-permute-start.6 = (bf16[256,384]{1,0:T(8,128)(2,1)S(1)}, bf16[256,384]{1,0:T(8,128)(2,1)}, u32[]{:S(2)}, u32[]{:S(2)}) collective-permute-start(bf16[256,384]{1,0:T(8,128)(2,1)S(1)} %pad_maximum_fusion.n0), channel_id=1, source_target_pairs={{0,64},{1,65},{2,66},{3,67},{4,68},{5,69},{6,70},{7,71},{8,72},{9,... | collective-permute-start | bytes 589832 | tf_op jit(solution)/shard_map/ppermute | solution.py:219
  37.7 9.7 %collective-permute-start.7 = (bf16[256,384]{1,0:T(8,128)(2,1)S(1)}, bf16[256,384]{1,0:T(8,128)(2,1)}, u32[]{:S(2)}, u32[]{:S(2)}) collective-permute-start(bf16[256,384]{1,0:T(8,128)(2,1)S(1)} %pad_maximum_fusion.n0), channel_id=1, source_target_pairs={{0,96},{1,97},{2,98},{3,99},{4,100},{5,101},{6,102},{7,103},{8,104... | collective-permute-start | bytes 589832 | tf_op jit(solution)/shard_map/ppermute | solution.py:219
  47.4 2.7 %collective-permute-start.13 = (bf16[128,1024]{1,0:T(8,128)(2,1)S(1)}, bf16[128,1024]{1,0:T(8,128)(2,1)S(1)}, u32[]{:S(2)}, u32[]{:S(2)}) collective-permute-start(bf16[128,1024]{1,0:T(8,128)(2,1)S(1)} %get-tuple-element.17), channel_id=1, source_target_pairs={{0,1},{1,0},{2,3},{3,2},{4,5},{5,4},{6,7},{7,6},{8,9},{9,8},{10,11... | collective-permute-start | bytes 786440 | tf_op jit(solution)/shard_map/ppermute | solution.py:219
  50.2 12.7 %copy-start = (bf16[1,256,1024]{2,1,0:T(8,128)(2,1)S(1)}, bf16[1,256,1024]{2,1,0:T(8,128)(2,1)}, u32[]{:S(2)}) copy-start(bf16[1,256,1024]{2,1,0:T(8,128)(2,1)} %param.9) | copy-start | bytes 1572868
  51.0 20.4 %all-to-all-start.1 = ((bf16[32,4,1024]{2,1,0:T(4,128)(2,1)}), bf16[32,4,1024]{2,1,0:T(4,128)(2,1)S(1)}, u32[]{:S(2)}, u32[]{:S(2)}) async-start(bf16[32,4,1024]{2,1,0:T(4,128)(2,1)} %reshape.60), calls=%async_computation.1 | async-start | bytes 524288 | tf_op jit(solution)/shard_map/all_to_all | solution.py:27
  59.9 1.9 %collective-permute-start.12 = (bf16[128,1024]{1,0:T(8,128)(2,1)S(1)}, bf16[128,1024]{1,0:T(8,128)(2,1)S(1)}, u32[]{:S(2)}, u32[]{:S(2)}) collective-permute-start(bf16[128,1024]{1,0:T(8,128)(2,1)S(1)} %collective-permute-done.4.out_ref), channel_id=1, source_target_pairs={{0,1},{1,0},{2,3},{3,2},{4,5},{5,4},{6,7},{7,6},{8,9},{9,8},{10,11... | collective-permute-start | bytes 786440 | tf_op jit(solution)/shard_map/ppermute | solution.py:219
  60.6 1.4 %collective-permute-start.9 = (bf16[256,384]{1,0:T(8,128)(2,1)S(1)}, bf16[256,384]{1,0:T(8,128)(2,1)S(1)}, u32[]{:S(2)}, u32[]{:S(2)}) collective-permute-start(bf16[256,384]{1,0:T(8,128)(2,1)S(1)} %collective-permute-done.5.n1), channel_id=1, source_target_pairs={{0,1},{1,0},{2,3},{3,2},{4,5},{5,4},{6,7},{7,6},{8,9},{9,8},{10,11... | collective-permute-start | bytes 589832 | tf_op jit(solution)/shard_map/ppermute | solution.py:219
  60.7 1.8 %collective-permute-start.10 = (bf16[256,384]{1,0:T(8,128)(2,1)}, bf16[256,384]{1,0:T(8,128)(2,1)S(1)}, u32[]{:S(2)}, u32[]{:S(2)}) collective-permute-start(bf16[256,384]{1,0:T(8,128)(2,1)} %collective-permute-done.6.n2), channel_id=1, source_target_pairs={{0,1},{1,0},{2,3},{3,2},{4,5},{5,4},{6,7},{7,6},{8,9},{9,8},{10,11... | collective-permute-start | bytes 589832 | tf_op jit(solution)/shard_map/ppermute | solution.py:219
  61.1 1.7 %collective-permute-start.11 = (bf16[256,384]{1,0:T(8,128)(2,1)}, bf16[256,384]{1,0:T(8,128)(2,1)S(1)}, u32[]{:S(2)}, u32[]{:S(2)}) collective-permute-start(bf16[256,384]{1,0:T(8,128)(2,1)} %collective-permute-done.7.n3), channel_id=1, source_target_pairs={{0,1},{1,0},{2,3},{3,2},{4,5},{5,4},{6,7},{7,6},{8,9},{9,8},{10,11... | collective-permute-start | bytes 589832 | tf_op jit(solution)/shard_map/ppermute | solution.py:219
  61.2 1.7 %collective-permute-start.8 = (bf16[256,384]{1,0:T(8,128)(2,1)S(1)}, bf16[256,384]{1,0:T(8,128)(2,1)S(1)}, u32[]{:S(2)}, u32[]{:S(2)}) collective-permute-start(bf16[256,384]{1,0:T(8,128)(2,1)S(1)} %pad_maximum_fusion.n0), channel_id=1, source_target_pairs={{0,1},{1,0},{2,3},{3,2},{4,5},{5,4},{6,7},{7,6},{8,9},{9,8},{10,11... | collective-permute-start | bytes 589832 | tf_op jit(solution)/shard_map/ppermute | solution.py:219
  71.6 4.6 %collective-permute-start.14 = (f32[8,1024]{1,0:T(8,128)S(1)}, f32[8,1024]{1,0:T(8,128)S(1)}, u32[]{:S(2)}, u32[]{:S(2)}) collective-permute-start(f32[8,1024]{1,0:T(8,128)S(1)} %shard_map.94.t0), channel_id=1, source_target_pairs={{0,8},{1,9},{2,10},{3,11},{4,12},{5,13},{6,14},{7,15},{8,16},{9,17... | collective-permute-start | bytes 98312 | tf_op jit(solution)/shard_map/ppermute | solution.py:219
  72.9 4.3 %collective-permute-start.15 = (f32[8,1024]{1,0:T(8,128)S(1)}, f32[8,1024]{1,0:T(8,128)S(1)}, u32[]{:S(2)}, u32[]{:S(2)}) collective-permute-start(f32[8,1024]{1,0:T(8,128)S(1)} %shard_map.94.t0), channel_id=1, source_target_pairs={{0,16},{1,17},{2,18},{3,19},{4,20},{5,21},{6,22},{7,23},{8,24},{9,... | collective-permute-start | bytes 98312 | tf_op jit(solution)/shard_map/ppermute | solution.py:219
  74.3 2.9 %collective-permute-start.16 = (f32[8,1024]{1,0:T(8,128)S(1)}, f32[8,1024]{1,0:T(8,128)S(1)}, u32[]{:S(2)}, u32[]{:S(2)}) collective-permute-start(f32[8,1024]{1,0:T(8,128)S(1)} %shard_map.94.t0), channel_id=1, source_target_pairs={{0,24},{1,25},{2,26},{3,27},{4,28},{5,29},{6,30},{7,31},{8,0},{9,1... | collective-permute-start | bytes 98312 | tf_op jit(solution)/shard_map/ppermute | solution.py:219
  98.4 5.8 %collective-permute-start.17 = (bf16[32,8,1024]{2,1,0:T(8,128)(2,1)S(1)}, bf16[32,8,1024]{2,1,0:T(8,128)(2,1)S(1)}, u32[]{:S(2)}, u32[]{:S(2)}) collective-permute-start(bf16[32,8,1024]{2,1,0:T(8,128)(2,1)S(1)} %all_to_all.15), channel_id=1, source_target_pairs={{0,1},{1,0},{2,3},{3,2},{4,5},{5,4},{6,7},{7,6},{8,9},{9,8},{10,11... | collective-permute-start | bytes 1572872 | tf_op jit(solution)/shard_map/ppermute | solution.py:219
  (5 other events, 14.1 us)

commit v6 on v5

--- a/solution.py
+++ b/solution.py
@@ -75,14 +75,6 @@
     row = lax.broadcasted_iota(jnp.int32, (rows, 4 * HEAD), 0)
     col = lax.broadcasted_iota(jnp.int32, (rows, 4 * HEAD), 1)
     return lax.rem(row, 4) == lax.div(col, HEAD)
-
-
-def cut_kernel(where, query_ref, keyval_ref, own_ref):
-    block = 4 * where[3] + where[2]
-    at = pl.ds(pl.multiple_of(block * CUT, CUT), CUT)
-    own_ref[:, :CUT] = query_ref[:, at]
-    own_ref[:, CUT : 2 * CUT] = keyval_ref[:, at]
-    own_ref[:, 2 * CUT :] = keyval_ref[:, pl.ds(pl.multiple_of(block * CUT + WIDTH, CUT), CUT)]
 
 
 def pick_kernel(where, info_ref, bank_ref, keep_ref, give_ref, select_ref):
@@ -189,9 +181,9 @@
         return 2.0 * t, size(r), x + both[:n], r
 
     def more(state):
-        return (state[0] < 9.0) & (state[1] > 1e-4)
-
-    r = exact(r, r)
+        return (state[0] < 7.0) & (state[1] > 1e-3)
+
+    r = lax.cond(norm < 512.0 * ridge, product, exact, r, r)
     state = (2.0 * c * ridge, size(r), x, r)
     state = lax.while_loop(lambda s: more(s) & (norm < 512.0 * ridge), lambda s: step(product, s), state)
     x = lax.while_loop(more, lambda s: step(exact, s), state)[2]
@@ -199,10 +191,10 @@
     def refine(state):
         i, _, x = state
         e = eye - exact(a, x)
-        return i + 1, jnp.sum(e * e), x + exact(x, e)
+        return i + 1, jnp.sum(e * e), x + product(x, e)
 
     _, _, x = lax.while_loop(
-        lambda s: (s[0] == 0) | ((s[1] > 1e-7) & (s[0] < 4)), refine, (jnp.int32(0), jnp.float32(1.0), x)
+        lambda s: (s[0] == 0) | ((s[1] > 1e-6) & (s[0] < 4)), refine, (jnp.int32(0), jnp.float32(1.0), x)
     )
     high, mid, low = terms(x)
     z1, z2, z3 = terms(dot(low, fresh) + dot(mid, fresh) + dot(high, fresh))
@@ -244,7 +236,9 @@
     h1, h3 = along_x(hidden, 1), along_x(hidden, 3)
     h2 = along_x(h1, 1)
 
-    own = call(cut_kernel, shape((CUT, 3 * CUT), BF), 2**10, w_query, w_keyval, where=where)
+    at = (4 * c + x) * CUT
+    own = [(w_query, at), (w_keyval, at), (w_keyval, at + WIDTH)]
+    own = jnp.concatenate([lax.dynamic_slice_in_dim(w, at, CUT, 1) for w, at in own], axis=1)
     out1 = shift(w_out, lambda zh, y, xx, zl, c: (c, xx, y, zl if c == zh else 3 - zl, zh))
     got = mirror(own)
     own = after(jnp.concatenate([own, got], axis=0), h1, h3, out1)

time: 119 us -> 118 us (level)
  waiting for transfers between devices: 16.1 us -> 12.9 us
  blocking collectives: 20.9 us -> 23.9 us
  local copies, waits for them, and re-layouts: 3.61 us -> 5.67 us
  Pallas kernels: 21 us -> 19.4 us
    all_to_all x1, blocking collectives: 20.9 us -> 23.9 us  [exchange(): lax.all_to_all(x, ('grp', 'dev'), split_axis=0, concat_axis=0, tiled=True...]
    all_to_all x1, waiting for transfers between devices: 3.03 us -> 0.75 us  [exchange(): lax.all_to_all(x, ('grp', 'dev'), split_axis=0, concat_axis=0, tiled=True...]
    pallas_call x6 -> x5, Pallas kernels: 21 us -> 19.4 us  [call(): pl.pallas_call(kernel, out_shape=out, in_specs=[pl.BlockSpec(memory_space...]
    unnamed x18 -> x28, local copies, waits for them, and re-layouts: 2.65 us -> 3.93 us
  transfers between devices with their start and end apart: 20 -> 20, of which waited for: 13 -> 12; matrix products, arithmetic and copies ran while one was open for 1% -> 1% of each run, Pallas kernels for 6% -> 5%
where the time goes in v6:
time: 118 us; the launch traced here: 117 us
  starting transfers between devices  53.2 us (45%)
  blocking collectives  23.9 us (20%)
  Pallas kernels  19.4 us (16%)
  waiting for transfers between devices  12.9 us (11%)
  local copies, waits for them, and re-layouts  5.67 us (5%)
  between operations  1.52 us (1%)
    ppermute x18, starting transfers between devices, shift(): return lax.ppermute(x, ('grp', 'dev'), perm)  30.4 us
    all_to_all x1, blocking collectives, exchange(): lax.all_to_all(x, ('grp', 'dev'), split_axis=0, concat_axis=0, tiled=True...  23.9 us
    pallas_call x5, Pallas kernels, call(): pl.pallas_call(kernel, out_shape=out, in_specs=[pl.BlockSpec(memory_space...  19.4 us
    all_to_all x1, starting transfers between devices, local(): lax.all_to_all(after(info, got), ('grp', 'dev'), split_axis=0, concat_axi...  14.1 us
    all_to_all x1, starting transfers between devices, exchange(): lax.all_to_all(x, ('grp', 'dev'), split_axis=0, concat_axis=0, tiled=True...  8.72 us
    all_to_all x1, waiting for transfers between devices, local(): lax.all_to_all(after(info, got), ('grp', 'dev'), split_axis=0, concat_axi...  6.29 us
    ppermute x18, waiting for transfers between devices, shift(): return lax.ppermute(x, ('grp', 'dev'), perm)  5.81 us
    unnamed x28, local copies, waits for them, and re-layouts  3.93 us
  transfers between devices with their start and end apart: 20, of which 12 were waited for; matrix products, arithmetic and copies ran while one was open for 1% of the time, Pallas kernels for 5%

profile of v6, /device:TPU:1, one launch (start us, length us, event | category | flops | bytes accessed | tf_op | source)
XLA Modules:
  0.0 117.4 jit_solution(16772123829208522051)
XLA Ops:
  0.0 2.0 %collective-permute-start = (bf16[256,1024]{1,0:T(8,128)(2,1)}, bf16[256,1024]{1,0:T(8,128)(2,1)S(1)}, u32[]{:S(2)}, u32[]{:S(2)}) collective-permute-start(bf16[256,1024]{1,0:T(8,128)(2,1)} %bitcast.15), channel_id=1, source_target_pairs={{0,8},{1,9},{2,10},{3,11},{4,12},{5,13},{6,14},{7,15},{8,16},{9,17... | collective-permute-start | bytes 1572872 | tf_op jit(solution)/shard_map/ppermute | solution.py:211
  2.0 1.4 %collective-permute-start.2 = (bf16[256,1024]{1,0:T(8,128)(2,1)}, bf16[256,1024]{1,0:T(8,128)(2,1)S(1)}, u32[]{:S(2)}, u32[]{:S(2)}) collective-permute-start(bf16[256,1024]{1,0:T(8,128)(2,1)} %bitcast.16), channel_id=1, source_target_pairs={{0,24},{1,25},{2,26},{3,27},{4,28},{5,29},{6,30},{7,31},{8,0},{9,1... | collective-permute-start | bytes 1572872 | tf_op jit(solution)/shard_map/ppermute | solution.py:211
  4.2 5.8 %collective-permute-start.3 = (bf16[128,384]{1,0:T(8,128)(2,1)S(1)}, bf16[128,384]{1,0:T(8,128)(2,1)S(1)}, u32[]{:S(2)}, u32[]{:S(2)}) collective-permute-start(bf16[128,384]{1,0:T(8,128)(2,1)S(1)} %pad_maximum_fusion.1), channel_id=1, source_target_pairs={{0,134},{1,135},{2,132},{3,133},{4,130},{5,131},{6,128},{7,129},{8... | collective-permute-start | bytes 294920 | tf_op jit(solution)/shard_map/ppermute | solution.py:211
  10.0 3.2 %collective-permute-start.4 = (bf16[128,1024]{1,0:T(8,128)(2,1)S(1)}, bf16[128,1024]{1,0:T(8,128)(2,1)S(1)}, u32[]{:S(2)}, u32[]{:S(2)}) collective-permute-start(bf16[128,1024]{1,0:T(8,128)(2,1)S(1)} %copy-done.13), channel_id=1, source_target_pairs={{0,0},{1,134},{2,2},{3,132},{4,4},{5,130},{6,6},{7,128},{8,32},{9,... | collective-permute-start | bytes 786440 | tf_op jit(solution)/shard_map/ppermute | solution.py:211
  15.3 14.1 %all-to-all-start = ((f32[256,1,128]{2,1,0:T(1,128)}), f32[256,1,128]{2,1,0:T(1,128)S(1)}, u32[]{:S(2)}, u32[]{:S(2)}) async-start(f32[256,1,128]{2,1,0:T(1,128)} %fusion), calls=%async_computation | async-start | bytes 262144 | tf_op jit(solution)/shard_map/all_to_all | solution.py:253
  29.4 1.5 %collective-permute-start.1 = (bf16[256,1024]{1,0:T(8,128)(2,1)S(1)}, bf16[256,1024]{1,0:T(8,128)(2,1)S(1)}, u32[]{:S(2)}, u32[]{:S(2)}) collective-permute-start(bf16[256,1024]{1,0:T(8,128)(2,1)S(1)} %collective-permute-done.h1), channel_id=1, source_target_pairs={{0,8},{1,9},{2,10},{3,11},{4,12},{5,13},{6,14},{7,15},{8,16},{9,17... | collective-permute-start | bytes 1572872 | tf_op jit(solution)/shard_map/ppermute | solution.py:211
  30.9 1.3 %collective-permute-start.5 = (bf16[256,384]{1,0:T(8,128)(2,1)S(1)}, bf16[256,384]{1,0:T(8,128)(2,1)S(1)}, u32[]{:S(2)}, u32[]{:S(2)}) collective-permute-start(bf16[256,384]{1,0:T(8,128)(2,1)S(1)} %pad_maximum_fusion.n0), channel_id=1, source_target_pairs={{0,32},{1,33},{2,34},{3,35},{4,36},{5,37},{6,38},{7,39},{8,40},{9,... | collective-permute-start | bytes 589832 | tf_op jit(solution)/shard_map/ppermute | solution.py:211
  32.2 2.5 %collective-permute-start.6 = (bf16[256,384]{1,0:T(8,128)(2,1)S(1)}, bf16[256,384]{1,0:T(8,128)(2,1)S(1)}, u32[]{:S(2)}, u32[]{:S(2)}) collective-permute-start(bf16[256,384]{1,0:T(8,128)(2,1)S(1)} %pad_maximum_fusion.n0), channel_id=1, source_target_pairs={{0,64},{1,65},{2,66},{3,67},{4,68},{5,69},{6,70},{7,71},{8,72},{9,... | collective-permute-start | bytes 589832 | tf_op jit(solution)/shard_map/ppermute | solution.py:211
  34.6 1.1 collective-permute-start.7
  35.8 6.3 %all-to-all-done = f32[256,1,128]{2,1,0:T(1,128)S(1)} async-done(((f32[256,1,128]{2,1,0:T(1,128)}), f32[256,1,128]{2,1,0:T(1,128)S(1)}, u32[]{:S(2)}, u32[]{:S(2)}) %all-to-all-start) | async-done | bytes 131104 | tf_op jit(solution)/shard_map/all_to_all | solution.py:253
  42.1 1.3 %shard_map.92 = (bf16[128,1024]{1,0:T(8,128)(2,1)S(1)}, bf16[128,1024]{1,0:T(8,128)(2,1)S(1)}) custom-call(s32[7]{0:T(128)S(1)} %stack.23.where, f32[256,128]{1,0:T(8,128)S(1)} %bitcast.19, bf16[256,1024]{1,0:T(8,128)(2,1)S(1)} %copy-done.2), custom_call_target="tpu_custom_call" | custom-call | flops 134217728 | bytes 1048576 | tf_op jit(solution)/shard_map/pallas_call | solution.py:43
  44.3 1.6 %collective-permute-start.13 = (bf16[128,1024]{1,0:T(8,128)(2,1)S(1)}, bf16[128,1024]{1,0:T(8,128)(2,1)S(1)}, u32[]{:S(2)}, u32[]{:S(2)}) collective-permute-start(bf16[128,1024]{1,0:T(8,128)(2,1)S(1)} %get-tuple-element.17), channel_id=1, source_target_pairs={{0,1},{1,0},{2,3},{3,2},{4,5},{5,4},{6,7},{7,6},{8,9},{9,8},{10,11... | collective-permute-start | bytes 786440 | tf_op jit(solution)/shard_map/ppermute | solution.py:211
  45.9 1.2 collective-permute-done.13
  47.9 8.7 %all-to-all-start.1 = ((bf16[32,4,1024]{2,1,0:T(4,128)(2,1)}), bf16[32,4,1024]{2,1,0:T(4,128)(2,1)S(1)}, u32[]{:S(2)}, u32[]{:S(2)}) async-start(bf16[32,4,1024]{2,1,0:T(4,128)(2,1)} %reshape.60), calls=%async_computation.1 | async-start | bytes 524288 | tf_op jit(solution)/shard_map/all_to_all | solution.py:27
  59.7 0.9 copy-done.4
  63.1 4.4 %shard_map.91.part_ref = f32[4,1024]{1,0:T(4,128)S(1)} custom-call(s32[7]{0:T(128)S(1)} %copy-done.10, bf16[256,1024]{1,0:T(8,128)(2,1)S(1)} %bitcast.17, bf16[256,1024]{1,0:T(8,128)(2,1)S(1)} %collective-permute-done.h1, bf16[256,1024]{1,0:T(8,128)(2,1)S(1)} %collective-permute-done.1.h2, bf16[256,1024]{1,0:T(8,128)(2,1)S(1)} %collective-permute-done.2.h3, ...), custom_call_target="tpu_custom_call" | custom-call | flops 1073741824 | bytes 1048576 | tf_op jit(solution)/shard_map/pallas_call | solution.py:43
  68.4 1.3 %collective-permute-start.14 = (f32[8,1024]{1,0:T(8,128)S(1)}, f32[8,1024]{1,0:T(8,128)S(1)}, u32[]{:S(2)}, u32[]{:S(2)}) collective-permute-start(f32[8,1024]{1,0:T(8,128)S(1)} %shard_map.93.t0), channel_id=1, source_target_pairs={{0,8},{1,9},{2,10},{3,11},{4,12},{5,13},{6,14},{7,15},{8,16},{9,17... | collective-permute-start | bytes 98312 | tf_op jit(solution)/shard_map/ppermute | solution.py:211
  69.6 2.0 %collective-permute-start.15 = (f32[8,1024]{1,0:T(8,128)S(1)}, f32[8,1024]{1,0:T(8,128)S(1)}, u32[]{:S(2)}, u32[]{:S(2)}) collective-permute-start(f32[8,1024]{1,0:T(8,128)S(1)} %shard_map.93.t0), channel_id=1, source_target_pairs={{0,16},{1,17},{2,18},{3,19},{4,20},{5,21},{6,22},{7,23},{8,24},{9,... | collective-permute-start | bytes 98312 | tf_op jit(solution)/shard_map/ppermute | solution.py:211
  71.6 1.3 %collective-permute-start.16 = (f32[8,1024]{1,0:T(8,128)S(1)}, f32[8,1024]{1,0:T(8,128)S(1)}, u32[]{:S(2)}, u32[]{:S(2)}) collective-permute-start(f32[8,1024]{1,0:T(8,128)S(1)} %shard_map.93.t0), channel_id=1, source_target_pairs={{0,24},{1,25},{2,26},{3,27},{4,28},{5,29},{6,30},{7,31},{8,0},{9,1... | collective-permute-start | bytes 98312 | tf_op jit(solution)/shard_map/ppermute | solution.py:211
  72.9 1.0 collective-permute-done.15.t2
  74.7 23.9 %all_to_all.15 = bf16[32,8,1024]{2,1,0:T(8,128)(2,1)S(1)} all-to-all(bf16[32,8,1024]{2,1,0:T(8,128)(2,1)S(1)} %broadcast_in_dim.21), channel_id=1, replica_groups={{0,32,64,96,2,34,66,98,4,36,68,100,6,38,70,102,128,160,192,224,130,162,..., dimensions={0} | all-to-all | bytes 1048576 | tf_op jit(solution)/shard_map/all_to_all | solution.py:27
  98.7 3.8 %collective-permute-start.17 = (bf16[32,8,1024]{2,1,0:T(8,128)(2,1)S(1)}, bf16[32,8,1024]{2,1,0:T(8,128)(2,1)S(1)}, u32[]{:S(2)}, u32[]{:S(2)}) collective-permute-start(bf16[32,8,1024]{2,1,0:T(8,128)(2,1)S(1)} %all_to_all.15), channel_id=1, source_target_pairs={{0,1},{1,0},{2,3},{3,2},{4,5},{5,4},{6,7},{7,6},{8,9},{9,8},{10,11... | collective-permute-start | bytes 1572872 | tf_op jit(solution)/shard_map/ppermute | solution.py:211
  102.5 1.5 %collective-permute-done.17 = bf16[32,8,1024]{2,1,0:T(8,128)(2,1)S(1)} collective-permute-done((bf16[32,8,1024]{2,1,0:T(8,128)(2,1)S(1)}, bf16[32,8,1024]{2,1,0:T(8,128)(2,1)S(1)}, u32[]{:S(2)}, u32[]{:S(2)}) %collective-permute-start.17) | collective-permute-done | bytes 524320 | tf_op jit(solution)/shard_map/ppermute | solution.py:211
  104.0 13.3 %shard_map.95 = bf16[256,1024]{1,0:T(8,128)(2,1)} custom-call(bf16[256,1024]{1,0:T(8,128)(2,1)S(1)} %bitcast.18, bf16[256,1024]{1,0:T(8,128)(2,1)S(1)} %bitcast.22, bf16[256,1024]{1,0:T(8,128)(2,1)S(1)} %copy-done.2), custom_call_target="tpu_custom_call" | custom-call | flops 2147483648 | bytes 1048576 | tf_op jit(solution)/shard_map/pallas_call | solution.py:43
  (61 shorter events, 10.6 us)
Async XLA Ops:
  0.0 10.0 %copy-start.13 = (bf16[128,1024]{1,0:T(8,128)(2,1)S(1)}, bf16[128,1024]{1,0:T(8,128)(2,1)}, u32[]{:S(2)}) copy-start(bf16[128,1024]{1,0:T(8,128)(2,1)} %param.12) | copy-start | bytes 786436
  0.0 29.4 %collective-permute-start = (bf16[256,1024]{1,0:T(8,128)(2,1)}, bf16[256,1024]{1,0:T(8,128)(2,1)S(1)}, u32[]{:S(2)}, u32[]{:S(2)}) collective-permute-start(bf16[256,1024]{1,0:T(8,128)(2,1)} %bitcast.15), channel_id=1, source_target_pairs={{0,8},{1,9},{2,10},{3,11},{4,12},{5,13},{6,14},{7,15},{8,16},{9,17... | collective-permute-start | bytes 1572872 | tf_op jit(solution)/shard_map/ppermute | solution.py:211
  2.0 28.8 %collective-permute-start.2 = (bf16[256,1024]{1,0:T(8,128)(2,1)}, bf16[256,1024]{1,0:T(8,128)(2,1)S(1)}, u32[]{:S(2)}, u32[]{:S(2)}) collective-permute-start(bf16[256,1024]{1,0:T(8,128)(2,1)} %bitcast.16), channel_id=1, source_target_pairs={{0,24},{1,25},{2,26},{3,27},{4,28},{5,29},{6,30},{7,31},{8,0},{9,1... | collective-permute-start | bytes 1572872 | tf_op jit(solution)/shard_map/ppermute | solution.py:211
  4.2 37.9 %copy-start.2 = (bf16[256,1024]{1,0:T(8,128)(2,1)S(1)}, bf16[256,1024]{1,0:T(8,128)(2,1)}, u32[]{:S(2)}) copy-start(bf16[256,1024]{1,0:T(8,128)(2,1)} %bank_ref.3) | copy-start | bytes 1572868
  4.2 11.1 %collective-permute-start.3 = (bf16[128,384]{1,0:T(8,128)(2,1)S(1)}, bf16[128,384]{1,0:T(8,128)(2,1)S(1)}, u32[]{:S(2)}, u32[]{:S(2)}) collective-permute-start(bf16[128,384]{1,0:T(8,128)(2,1)S(1)} %pad_maximum_fusion.1), channel_id=1, source_target_pairs={{0,134},{1,135},{2,132},{3,133},{4,130},{5,131},{6,128},{7,129},{8... | collective-permute-start | bytes 294920 | tf_op jit(solution)/shard_map/ppermute | solution.py:211
  10.0 20.9 %collective-permute-start.4 = (bf16[128,1024]{1,0:T(8,128)(2,1)S(1)}, bf16[128,1024]{1,0:T(8,128)(2,1)S(1)}, u32[]{:S(2)}, u32[]{:S(2)}) collective-permute-start(bf16[128,1024]{1,0:T(8,128)(2,1)S(1)} %copy-done.13), channel_id=1, source_target_pairs={{0,0},{1,134},{2,2},{3,132},{4,4},{5,130},{6,6},{7,128},{8,32},{9,... | collective-permute-start | bytes 786440 | tf_op jit(solution)/shard_map/ppermute | solution.py:211
  15.3 26.8 %all-to-all-start = ((f32[256,1,128]{2,1,0:T(1,128)}), f32[256,1,128]{2,1,0:T(1,128)S(1)}, u32[]{:S(2)}, u32[]{:S(2)}) async-start(f32[256,1,128]{2,1,0:T(1,128)} %fusion), calls=%async_computation | async-start | bytes 262144 | tf_op jit(solution)/shard_map/all_to_all | solution.py:253
  29.4 17.8 %collective-permute-start.1 = (bf16[256,1024]{1,0:T(8,128)(2,1)S(1)}, bf16[256,1024]{1,0:T(8,128)(2,1)S(1)}, u32[]{:S(2)}, u32[]{:S(2)}) collective-permute-start(bf16[256,1024]{1,0:T(8,128)(2,1)S(1)} %collective-permute-done.h1), channel_id=1, source_target_pairs={{0,8},{1,9},{2,10},{3,11},{4,12},{5,13},{6,14},{7,15},{8,16},{9,17... | collective-permute-start | bytes 1572872 | tf_op jit(solution)/shard_map/ppermute | solution.py:211
  30.9 12.5 %copy-start.3 = (bf16[128,1024]{1,0:T(8,128)(2,1)}, bf16[128,1024]{1,0:T(8,128)(2,1)S(1)}, u32[]{:S(2)}) copy-start(bf16[128,1024]{1,0:T(8,128)(2,1)S(1)} %collective-permute-done.4.out_ref) | copy-start | bytes 786436
  30.9 13.0 %collective-permute-start.5 = (bf16[256,384]{1,0:T(8,128)(2,1)S(1)}, bf16[256,384]{1,0:T(8,128)(2,1)S(1)}, u32[]{:S(2)}, u32[]{:S(2)}) collective-permute-start(bf16[256,384]{1,0:T(8,128)(2,1)S(1)} %pad_maximum_fusion.n0), channel_id=1, source_target_pairs={{0,32},{1,33},{2,34},{3,35},{4,36},{5,37},{6,38},{7,39},{8,40},{9,... | collective-permute-start | bytes 589832 | tf_op jit(solution)/shard_map/ppermute | solution.py:211
  32.2 12.1 %collective-permute-start.6 = (bf16[256,384]{1,0:T(8,128)(2,1)S(1)}, bf16[256,384]{1,0:T(8,128)(2,1)S(1)}, u32[]{:S(2)}, u32[]{:S(2)}) collective-permute-start(bf16[256,384]{1,0:T(8,128)(2,1)S(1)} %pad_maximum_fusion.n0), channel_id=1, source_target_pairs={{0,64},{1,65},{2,66},{3,67},{4,68},{5,69},{6,70},{7,71},{8,72},{9,... | collective-permute-start | bytes 589832 | tf_op jit(solution)/shard_map/ppermute | solution.py:211
  34.6 9.7 %collective-permute-start.7 = (bf16[256,384]{1,0:T(8,128)(2,1)S(1)}, bf16[256,384]{1,0:T(8,128)(2,1)S(1)}, u32[]{:S(2)}, u32[]{:S(2)}) collective-permute-start(bf16[256,384]{1,0:T(8,128)(2,1)S(1)} %pad_maximum_fusion.n0), channel_id=1, source_target_pairs={{0,96},{1,97},{2,98},{3,99},{4,100},{5,101},{6,102},{7,103},{8,104... | collective-permute-start | bytes 589832 | tf_op jit(solution)/shard_map/ppermute | solution.py:211
  44.3 2.8 %collective-permute-start.13 = (bf16[128,1024]{1,0:T(8,128)(2,1)S(1)}, bf16[128,1024]{1,0:T(8,128)(2,1)S(1)}, u32[]{:S(2)}, u32[]{:S(2)}) collective-permute-start(bf16[128,1024]{1,0:T(8,128)(2,1)S(1)} %get-tuple-element.17), channel_id=1, source_target_pairs={{0,1},{1,0},{2,3},{3,2},{4,5},{5,4},{6,7},{7,6},{8,9},{9,8},{10,11... | collective-permute-start | bytes 786440 | tf_op jit(solution)/shard_map/ppermute | solution.py:211
  47.1 12.6 %copy-start.1 = (bf16[1,256,1024]{2,1,0:T(8,128)(2,1)S(1)}, bf16[1,256,1024]{2,1,0:T(8,128)(2,1)}, u32[]{:S(2)}) copy-start(bf16[1,256,1024]{2,1,0:T(8,128)(2,1)} %param.9) | copy-start | bytes 1572868
  47.9 20.3 %all-to-all-start.1 = ((bf16[32,4,1024]{2,1,0:T(4,128)(2,1)}), bf16[32,4,1024]{2,1,0:T(4,128)(2,1)S(1)}, u32[]{:S(2)}, u32[]{:S(2)}) async-start(bf16[32,4,1024]{2,1,0:T(4,128)(2,1)} %reshape.60), calls=%async_computation.1 | async-start | bytes 524288 | tf_op jit(solution)/shard_map/all_to_all | solution.py:27
  56.6 2.1 %collective-permute-start.12 = (bf16[128,1024]{1,0:T(8,128)(2,1)}, bf16[128,1024]{1,0:T(8,128)(2,1)S(1)}, u32[]{:S(2)}, u32[]{:S(2)}) collective-permute-start(bf16[128,1024]{1,0:T(8,128)(2,1)} %copy-done.3), channel_id=1, source_target_pairs={{0,1},{1,0},{2,3},{3,2},{4,5},{5,4},{6,7},{7,6},{8,9},{9,8},{10,11... | collective-permute-start | bytes 786440 | tf_op jit(solution)/shard_map/ppermute | solution.py:211
  57.4 1.4 %collective-permute-start.9 = (bf16[256,384]{1,0:T(8,128)(2,1)S(1)}, bf16[256,384]{1,0:T(8,128)(2,1)S(1)}, u32[]{:S(2)}, u32[]{:S(2)}) collective-permute-start(bf16[256,384]{1,0:T(8,128)(2,1)S(1)} %collective-permute-done.5.n1), channel_id=1, source_target_pairs={{0,1},{1,0},{2,3},{3,2},{4,5},{5,4},{6,7},{7,6},{8,9},{9,8},{10,11... | collective-permute-start | bytes 589832 | tf_op jit(solution)/shard_map/ppermute | solution.py:211
  57.5 1.8 %collective-permute-start.10 = (bf16[256,384]{1,0:T(8,128)(2,1)}, bf16[256,384]{1,0:T(8,128)(2,1)S(1)}, u32[]{:S(2)}, u32[]{:S(2)}) collective-permute-start(bf16[256,384]{1,0:T(8,128)(2,1)} %copy-done.5), channel_id=1, source_target_pairs={{0,1},{1,0},{2,3},{3,2},{4,5},{5,4},{6,7},{7,6},{8,9},{9,8},{10,11... | collective-permute-start | bytes 589832 | tf_op jit(solution)/shard_map/ppermute | solution.py:211
  57.9 1.7 %collective-permute-start.11 = (bf16[256,384]{1,0:T(8,128)(2,1)}, bf16[256,384]{1,0:T(8,128)(2,1)S(1)}, u32[]{:S(2)}, u32[]{:S(2)}) collective-permute-start(bf16[256,384]{1,0:T(8,128)(2,1)} %copy-done.7), channel_id=1, source_target_pairs={{0,1},{1,0},{2,3},{3,2},{4,5},{5,4},{6,7},{7,6},{8,9},{9,8},{10,11... | collective-permute-start | bytes 589832 | tf_op jit(solution)/shard_map/ppermute | solution.py:211
  58.0 1.7 %collective-permute-start.8 = (bf16[256,384]{1,0:T(8,128)(2,1)S(1)}, bf16[256,384]{1,0:T(8,128)(2,1)S(1)}, u32[]{:S(2)}, u32[]{:S(2)}) collective-permute-start(bf16[256,384]{1,0:T(8,128)(2,1)S(1)} %pad_maximum_fusion.n0), channel_id=1, source_target_pairs={{0,1},{1,0},{2,3},{3,2},{4,5},{5,4},{6,7},{7,6},{8,9},{9,8},{10,11... | collective-permute-start | bytes 589832 | tf_op jit(solution)/shard_map/ppermute | solution.py:211
  68.4 4.6 %collective-permute-start.14 = (f32[8,1024]{1,0:T(8,128)S(1)}, f32[8,1024]{1,0:T(8,128)S(1)}, u32[]{:S(2)}, u32[]{:S(2)}) collective-permute-start(f32[8,1024]{1,0:T(8,128)S(1)} %shard_map.93.t0), channel_id=1, source_target_pairs={{0,8},{1,9},{2,10},{3,11},{4,12},{5,13},{6,14},{7,15},{8,16},{9,17... | collective-permute-start | bytes 98312 | tf_op jit(solution)/shard_map/ppermute | solution.py:211
  69.6 4.3 %collective-permute-start.15 = (f32[8,1024]{1,0:T(8,128)S(1)}, f32[8,1024]{1,0:T(8,128)S(1)}, u32[]{:S(2)}, u32[]{:S(2)}) collective-permute-start(f32[8,1024]{1,0:T(8,128)S(1)} %shard_map.93.t0), channel_id=1, source_target_pairs={{0,16},{1,17},{2,18},{3,19},{4,20},{5,21},{6,22},{7,23},{8,24},{9,... | collective-permute-start | bytes 98312 | tf_op jit(solution)/shard_map/ppermute | solution.py:211
  71.6 2.8 %collective-permute-start.16 = (f32[8,1024]{1,0:T(8,128)S(1)}, f32[8,1024]{1,0:T(8,128)S(1)}, u32[]{:S(2)}, u32[]{:S(2)}) collective-permute-start(f32[8,1024]{1,0:T(8,128)S(1)} %shard_map.93.t0), channel_id=1, source_target_pairs={{0,24},{1,25},{2,26},{3,27},{4,28},{5,29},{6,30},{7,31},{8,0},{9,1... | collective-permute-start | bytes 98312 | tf_op jit(solution)/shard_map/ppermute | solution.py:211
  98.7 5.4 %collective-permute-start.17 = (bf16[32,8,1024]{2,1,0:T(8,128)(2,1)S(1)}, bf16[32,8,1024]{2,1,0:T(8,128)(2,1)S(1)}, u32[]{:S(2)}, u32[]{:S(2)}) collective-permute-start(bf16[32,8,1024]{2,1,0:T(8,128)(2,1)S(1)} %all_to_all.15), channel_id=1, source_target_pairs={{0,1},{1,0},{2,3},{3,2},{4,5},{5,4},{6,7},{7,6},{8,9},{9,8},{10,11... | collective-permute-start | bytes 1572872 | tf_op jit(solution)/shard_map/ppermute | solution.py:211
  (10 other events, 25.1 us)

commit v7 on v6

--- a/solution.py
+++ b/solution.py
@@ -181,9 +181,9 @@
         return 2.0 * t, size(r), x + both[:n], r
 
     def more(state):
-        return (state[0] < 7.0) & (state[1] > 1e-3)
-
-    r = lax.cond(norm < 512.0 * ridge, product, exact, r, r)
+        return (state[0] < 9.0) & (state[1] > 1e-4)
+
+    r = exact(r, r)
     state = (2.0 * c * ridge, size(r), x, r)
     state = lax.while_loop(lambda s: more(s) & (norm < 512.0 * ridge), lambda s: step(product, s), state)
     x = lax.while_loop(more, lambda s: step(exact, s), state)[2]
@@ -191,10 +191,10 @@
     def refine(state):
         i, _, x = state
         e = eye - exact(a, x)
-        return i + 1, jnp.sum(e * e), x + product(x, e)
+        return i + 1, jnp.sum(e * e), x + exact(x, e)
 
     _, _, x = lax.while_loop(
-        lambda s: (s[0] == 0) | ((s[1] > 1e-6) & (s[0] < 4)), refine, (jnp.int32(0), jnp.float32(1.0), x)
+        lambda s: (s[0] == 0) | ((s[1] > 1e-7) & (s[0] < 4)), refine, (jnp.int32(0), jnp.float32(1.0), x)
     )
     high, mid, low = terms(x)
     z1, z2, z3 = terms(dot(low, fresh) + dot(mid, fresh) + dot(high, fresh))
@@ -258,6 +258,7 @@
     rows = keep + other_core(after(give, *near[1:]))
     rows = exchange(after(rows, *near[1:], h2).reshape(32, 4, WIDTH), 1)
 
+    here = jnp.stack([after(zh, h2), y, x, c])
     part = call(
         encode_kernel,
         shape((4, WIDTH), F32),
@@ -270,7 +271,7 @@
         *far,
         out1,
         out2,
-        where=where,
+        where=here,
         scratch=[pltpu.VMEM((WIDTH, 6 * CUT), BF)],
     )
     both = call(pack_kernel, shape((8, WIDTH), F32), 2**18, part, rows)

time: 118 us -> 118 us (level)
    unnamed x28 -> x24, local copies, waits for them, and re-layouts: 3.93 us -> 2.84 us
  transfers between devices with their start and end apart: 20 -> 20, of which waited for: 12 -> 12; matrix products, arithmetic and copies ran while one was open for 1% -> 2% of each run, Pallas kernels for 5% -> 5%
where the time goes in v7:
time: 118 us; the launch traced here: 117 us
  starting transfers between devices  53.3 us (45%)
  blocking collectives  23.2 us (20%)
  Pallas kernels  19.9 us (17%)
  waiting for transfers between devices  13.8 us (12%)
  local copies, waits for them, and re-layouts  4.59 us (4%)
  between operations  1.52 us (1%)
    ppermute x18, starting transfers between devices, shift(): return lax.ppermute(x, ('grp', 'dev'), perm)  30.5 us
    all_to_all x1, blocking collectives, exchange(): lax.all_to_all(x, ('grp', 'dev'), split_axis=0, concat_axis=0, tiled=True...  23.2 us
    pallas_call x5, Pallas kernels, call(): pl.pallas_call(kernel, out_shape=out, in_specs=[pl.BlockSpec(memory_space...  19.9 us
    all_to_all x1, starting transfers between devices, local(): lax.all_to_all(after(info, got), ('grp', 'dev'), split_axis=0, concat_axi...  14.1 us
    all_to_all x1, starting transfers between devices, exchange(): lax.all_to_all(x, ('grp', 'dev'), split_axis=0, concat_axis=0, tiled=True...  8.69 us
    all_to_all x1, waiting for transfers between devices, local(): lax.all_to_all(after(info, got), ('grp', 'dev'), split_axis=0, concat_axi...  6.32 us
    ppermute x18, waiting for transfers between devices, shift(): return lax.ppermute(x, ('grp', 'dev'), perm)  6.18 us
    unnamed x24, local copies, waits for them, and re-layouts  2.84 us
  transfers between devices with their start and end apart: 20, of which 12 were waited for; matrix products, arithmetic and copies ran while one was open for 2% of the time, Pallas kernels for 5%

profile of v7, /device:TPU:1, one launch (start us, length us, event | category | flops | bytes accessed | tf_op | source)
XLA Modules:
  0.0 117.3 jit_solution(16924852903667360033)
XLA Ops:
  0.0 2.0 %collective-permute-start = (bf16[256,1024]{1,0:T(8,128)(2,1)}, bf16[256,1024]{1,0:T(8,128)(2,1)S(1)}, u32[]{:S(2)}, u32[]{:S(2)}) collective-permute-start(bf16[256,1024]{1,0:T(8,128)(2,1)} %bitcast.16), channel_id=1, source_target_pairs={{0,8},{1,9},{2,10},{3,11},{4,12},{5,13},{6,14},{7,15},{8,16},{9,17... | collective-permute-start | bytes 1572872 | tf_op jit(solution)/shard_map/ppermute | solution.py:211
  2.0 1.4 %collective-permute-start.2 = (bf16[256,1024]{1,0:T(8,128)(2,1)}, bf16[256,1024]{1,0:T(8,128)(2,1)S(1)}, u32[]{:S(2)}, u32[]{:S(2)}) collective-permute-start(bf16[256,1024]{1,0:T(8,128)(2,1)} %bitcast.17), channel_id=1, source_target_pairs={{0,24},{1,25},{2,26},{3,27},{4,28},{5,29},{6,30},{7,31},{8,0},{9,1... | collective-permute-start | bytes 1572872 | tf_op jit(solution)/shard_map/ppermute | solution.py:211
  4.2 5.8 %collective-permute-start.3 = (bf16[128,384]{1,0:T(8,128)(2,1)S(1)}, bf16[128,384]{1,0:T(8,128)(2,1)S(1)}, u32[]{:S(2)}, u32[]{:S(2)}) collective-permute-start(bf16[128,384]{1,0:T(8,128)(2,1)S(1)} %pad_maximum_fusion.1), channel_id=1, source_target_pairs={{0,134},{1,135},{2,132},{3,133},{4,130},{5,131},{6,128},{7,129},{8... | collective-permute-start | bytes 294920 | tf_op jit(solution)/shard_map/ppermute | solution.py:211
  10.0 3.2 %collective-permute-start.4 = (bf16[128,1024]{1,0:T(8,128)(2,1)S(1)}, bf16[128,1024]{1,0:T(8,128)(2,1)S(1)}, u32[]{:S(2)}, u32[]{:S(2)}) collective-permute-start(bf16[128,1024]{1,0:T(8,128)(2,1)S(1)} %copy-done.11), channel_id=1, source_target_pairs={{0,0},{1,134},{2,2},{3,132},{4,4},{5,130},{6,6},{7,128},{8,32},{9,... | collective-permute-start | bytes 786440 | tf_op jit(solution)/shard_map/ppermute | solution.py:211
  15.3 14.1 %all-to-all-start = ((f32[256,1,128]{2,1,0:T(1,128)}), f32[256,1,128]{2,1,0:T(1,128)S(1)}, u32[]{:S(2)}, u32[]{:S(2)}) async-start(f32[256,1,128]{2,1,0:T(1,128)} %fusion), calls=%async_computation | async-start | bytes 262144 | tf_op jit(solution)/shard_map/all_to_all | solution.py:253
  29.4 1.5 %collective-permute-start.1 = (bf16[256,1024]{1,0:T(8,128)(2,1)S(1)}, bf16[256,1024]{1,0:T(8,128)(2,1)S(1)}, u32[]{:S(2)}, u32[]{:S(2)}) collective-permute-start(bf16[256,1024]{1,0:T(8,128)(2,1)S(1)} %collective-permute-done.h1), channel_id=1, source_target_pairs={{0,8},{1,9},{2,10},{3,11},{4,12},{5,13},{6,14},{7,15},{8,16},{9,17... | collective-permute-start | bytes 1572872 | tf_op jit(solution)/shard_map/ppermute | solution.py:211
  30.9 1.3 %collective-permute-start.5 = (bf16[256,384]{1,0:T(8,128)(2,1)S(1)}, bf16[256,384]{1,0:T(8,128)(2,1)S(1)}, u32[]{:S(2)}, u32[]{:S(2)}) collective-permute-start(bf16[256,384]{1,0:T(8,128)(2,1)S(1)} %pad_maximum_fusion.n0), channel_id=1, source_target_pairs={{0,32},{1,33},{2,34},{3,35},{4,36},{5,37},{6,38},{7,39},{8,40},{9,... | collective-permute-start | bytes 589832 | tf_op jit(solution)/shard_map/ppermute | solution.py:211
  32.2 2.5 %collective-permute-start.6 = (bf16[256,384]{1,0:T(8,128)(2,1)S(1)}, bf16[256,384]{1,0:T(8,128)(2,1)S(1)}, u32[]{:S(2)}, u32[]{:S(2)}) collective-permute-start(bf16[256,384]{1,0:T(8,128)(2,1)S(1)} %pad_maximum_fusion.n0), channel_id=1, source_target_pairs={{0,64},{1,65},{2,66},{3,67},{4,68},{5,69},{6,70},{7,71},{8,72},{9,... | collective-permute-start | bytes 589832 | tf_op jit(solution)/shard_map/ppermute | solution.py:211
  34.6 1.1 collective-permute-start.7
  35.8 6.3 %all-to-all-done = f32[256,1,128]{2,1,0:T(1,128)S(1)} async-done(((f32[256,1,128]{2,1,0:T(1,128)}), f32[256,1,128]{2,1,0:T(1,128)S(1)}, u32[]{:S(2)}, u32[]{:S(2)}) %all-to-all-start) | async-done | bytes 131104 | tf_op jit(solution)/shard_map/all_to_all | solution.py:253
  42.1 1.3 %shard_map.92 = (bf16[128,1024]{1,0:T(8,128)(2,1)S(1)}, bf16[128,1024]{1,0:T(8,128)(2,1)S(1)}) custom-call(s32[7]{0:T(128)S(1)} %stack.34.where, f32[256,128]{1,0:T(8,128)S(1)} %bitcast.20, bf16[256,1024]{1,0:T(8,128)(2,1)S(1)} %copy-done.2), custom_call_target="tpu_custom_call" | custom-call | flops 134217728 | bytes 1048576 | tf_op jit(solution)/shard_map/pallas_call | solution.py:43
  44.3 1.6 %collective-permute-start.13 = (bf16[128,1024]{1,0:T(8,128)(2,1)S(1)}, bf16[128,1024]{1,0:T(8,128)(2,1)S(1)}, u32[]{:S(2)}, u32[]{:S(2)}) collective-permute-start(bf16[128,1024]{1,0:T(8,128)(2,1)S(1)} %get-tuple-element.19), channel_id=1, source_target_pairs={{0,1},{1,0},{2,3},{3,2},{4,5},{5,4},{6,7},{7,6},{8,9},{9,8},{10,11... | collective-permute-start | bytes 786440 | tf_op jit(solution)/shard_map/ppermute | solution.py:211
  45.9 1.2 collective-permute-done.13
  47.9 8.7 %all-to-all-start.1 = ((bf16[32,4,1024]{2,1,0:T(4,128)(2,1)}), bf16[32,4,1024]{2,1,0:T(4,128)(2,1)S(1)}, u32[]{:S(2)}, u32[]{:S(2)}) async-start(bf16[32,4,1024]{2,1,0:T(4,128)(2,1)} %reshape.60), calls=%async_computation.1 | async-start | bytes 524288 | tf_op jit(solution)/shard_map/all_to_all | solution.py:27
  62.5 4.4 %shard_map.91.part_ref = f32[4,1024]{1,0:T(4,128)S(1)} custom-call(s32[4]{0:T(128)S(1)} %pad_add_fusion.where, bf16[256,1024]{1,0:T(8,128)(2,1)S(1)} %bitcast.18, bf16[256,1024]{1,0:T(8,128)(2,1)S(1)} %collective-permute-done.h1, bf16[256,1024]{1,0:T(8,128)(2,1)S(1)} %collective-permute-done.1.h2, bf16[256,1024]{1,0:T(8,128)(2,1)S(1)} %collective-permute-done.2.h3, ...), custom_call_target="tpu_custom_call" | custom-call | flops 1073741824 | bytes 1048576 | tf_op jit(solution)/shard_map/pallas_call | solution.py:43
  66.8 1.3 %all-to-all-done.1.old_ref = bf16[32,4,1024]{2,1,0:T(4,128)(2,1)S(1)} async-done(((bf16[32,4,1024]{2,1,0:T(4,128)(2,1)}), bf16[32,4,1024]{2,1,0:T(4,128)(2,1)S(1)}, u32[]{:S(2)}, u32[]{:S(2)}) %all-to-all-start.1) | async-done | bytes 262176 | tf_op jit(solution)/shard_map/all_to_all | solution.py:27
  68.3 1.3 %collective-permute-start.14 = (f32[8,1024]{1,0:T(8,128)S(1)}, f32[8,1024]{1,0:T(8,128)S(1)}, u32[]{:S(2)}, u32[]{:S(2)}) collective-permute-start(f32[8,1024]{1,0:T(8,128)S(1)} %shard_map.93.t0), channel_id=1, source_target_pairs={{0,8},{1,9},{2,10},{3,11},{4,12},{5,13},{6,14},{7,15},{8,16},{9,17... | collective-permute-start | bytes 98312 | tf_op jit(solution)/shard_map/ppermute | solution.py:211
  69.6 2.0 %collective-permute-start.15 = (f32[8,1024]{1,0:T(8,128)S(1)}, f32[8,1024]{1,0:T(8,128)S(1)}, u32[]{:S(2)}, u32[]{:S(2)}) collective-permute-start(f32[8,1024]{1,0:T(8,128)S(1)} %shard_map.93.t0), channel_id=1, source_target_pairs={{0,16},{1,17},{2,18},{3,19},{4,20},{5,21},{6,22},{7,23},{8,24},{9,... | collective-permute-start | bytes 98312 | tf_op jit(solution)/shard_map/ppermute | solution.py:211
  71.6 1.3 %collective-permute-start.16 = (f32[8,1024]{1,0:T(8,128)S(1)}, f32[8,1024]{1,0:T(8,128)S(1)}, u32[]{:S(2)}, u32[]{:S(2)}) collective-permute-start(f32[8,1024]{1,0:T(8,128)S(1)} %shard_map.93.t0), channel_id=1, source_target_pairs={{0,24},{1,25},{2,26},{3,27},{4,28},{5,29},{6,30},{7,31},{8,0},{9,1... | collective-permute-start | bytes 98312 | tf_op jit(solution)/shard_map/ppermute | solution.py:211
  72.9 1.0 collective-permute-done.15.t2
  74.7 23.2 %all_to_all.15 = bf16[32,8,1024]{2,1,0:T(8,128)(2,1)S(1)} all-to-all(bf16[32,8,1024]{2,1,0:T(8,128)(2,1)S(1)} %broadcast_in_dim.21), channel_id=1, replica_groups={{0,32,64,96,2,34,66,98,4,36,68,100,6,38,70,102,128,160,192,224,130,162,..., dimensions={0} | all-to-all | bytes 1048576 | tf_op jit(solution)/shard_map/all_to_all | solution.py:27
  98.0 3.9 %collective-permute-start.17 = (bf16[32,8,1024]{2,1,0:T(8,128)(2,1)S(1)}, bf16[32,8,1024]{2,1,0:T(8,128)(2,1)S(1)}, u32[]{:S(2)}, u32[]{:S(2)}) collective-permute-start(bf16[32,8,1024]{2,1,0:T(8,128)(2,1)S(1)} %all_to_all.15), channel_id=1, source_target_pairs={{0,1},{1,0},{2,3},{3,2},{4,5},{5,4},{6,7},{7,6},{8,9},{9,8},{10,11... | collective-permute-start | bytes 1572872 | tf_op jit(solution)/shard_map/ppermute | solution.py:211
  101.9 1.5 %collective-permute-done.17 = bf16[32,8,1024]{2,1,0:T(8,128)(2,1)S(1)} collective-permute-done((bf16[32,8,1024]{2,1,0:T(8,128)(2,1)S(1)}, bf16[32,8,1024]{2,1,0:T(8,128)(2,1)S(1)}, u32[]{:S(2)}, u32[]{:S(2)}) %collective-permute-start.17) | collective-permute-done | bytes 524320 | tf_op jit(solution)/shard_map/ppermute | solution.py:211
  103.4 13.9 %shard_map.95 = bf16[256,1024]{1,0:T(8,128)(2,1)} custom-call(bf16[256,1024]{1,0:T(8,128)(2,1)S(1)} %bitcast.19, bf16[256,1024]{1,0:T(8,128)(2,1)S(1)} %bitcast.23, bf16[256,1024]{1,0:T(8,128)(2,1)S(1)} %copy-done.2), custom_call_target="tpu_custom_call" | custom-call | flops 2147483648 | bytes 1048576 | tf_op jit(solution)/shard_map/pallas_call | solution.py:43
  (58 shorter events, 10.2 us)
Async XLA Ops:
  0.0 10.0 %copy-start.11 = (bf16[128,1024]{1,0:T(8,128)(2,1)S(1)}, bf16[128,1024]{1,0:T(8,128)(2,1)}, u32[]{:S(2)}) copy-start(bf16[128,1024]{1,0:T(8,128)(2,1)} %param.12) | copy-start | bytes 786436
  0.0 29.4 %collective-permute-start = (bf16[256,1024]{1,0:T(8,128)(2,1)}, bf16[256,1024]{1,0:T(8,128)(2,1)S(1)}, u32[]{:S(2)}, u32[]{:S(2)}) collective-permute-start(bf16[256,1024]{1,0:T(8,128)(2,1)} %bitcast.16), channel_id=1, source_target_pairs={{0,8},{1,9},{2,10},{3,11},{4,12},{5,13},{6,14},{7,15},{8,16},{9,17... | collective-permute-start | bytes 1572872 | tf_op jit(solution)/shard_map/ppermute | solution.py:211
  2.0 28.8 %collective-permute-start.2 = (bf16[256,1024]{1,0:T(8,128)(2,1)}, bf16[256,1024]{1,0:T(8,128)(2,1)S(1)}, u32[]{:S(2)}, u32[]{:S(2)}) collective-permute-start(bf16[256,1024]{1,0:T(8,128)(2,1)} %bitcast.17), channel_id=1, source_target_pairs={{0,24},{1,25},{2,26},{3,27},{4,28},{5,29},{6,30},{7,31},{8,0},{9,1... | collective-permute-start | bytes 1572872 | tf_op jit(solution)/shard_map/ppermute | solution.py:211
  4.2 37.9 %copy-start.2 = (bf16[256,1024]{1,0:T(8,128)(2,1)S(1)}, bf16[256,1024]{1,0:T(8,128)(2,1)}, u32[]{:S(2)}) copy-start(bf16[256,1024]{1,0:T(8,128)(2,1)} %bank_ref.3) | copy-start | bytes 1572868
  4.2 11.1 %collective-permute-start.3 = (bf16[128,384]{1,0:T(8,128)(2,1)S(1)}, bf16[128,384]{1,0:T(8,128)(2,1)S(1)}, u32[]{:S(2)}, u32[]{:S(2)}) collective-permute-start(bf16[128,384]{1,0:T(8,128)(2,1)S(1)} %pad_maximum_fusion.1), channel_id=1, source_target_pairs={{0,134},{1,135},{2,132},{3,133},{4,130},{5,131},{6,128},{7,129},{8... | collective-permute-start | bytes 294920 | tf_op jit(solution)/shard_map/ppermute | solution.py:211
  10.0 20.9 %collective-permute-start.4 = (bf16[128,1024]{1,0:T(8,128)(2,1)S(1)}, bf16[128,1024]{1,0:T(8,128)(2,1)S(1)}, u32[]{:S(2)}, u32[]{:S(2)}) collective-permute-start(bf16[128,1024]{1,0:T(8,128)(2,1)S(1)} %copy-done.11), channel_id=1, source_target_pairs={{0,0},{1,134},{2,2},{3,132},{4,4},{5,130},{6,6},{7,128},{8,32},{9,... | collective-permute-start | bytes 786440 | tf_op jit(solution)/shard_map/ppermute | solution.py:211
  15.3 26.9 %all-to-all-start = ((f32[256,1,128]{2,1,0:T(1,128)}), f32[256,1,128]{2,1,0:T(1,128)S(1)}, u32[]{:S(2)}, u32[]{:S(2)}) async-start(f32[256,1,128]{2,1,0:T(1,128)} %fusion), calls=%async_computation | async-start | bytes 262144 | tf_op jit(solution)/shard_map/all_to_all | solution.py:253
  29.4 17.7 %collective-permute-start.1 = (bf16[256,1024]{1,0:T(8,128)(2,1)S(1)}, bf16[256,1024]{1,0:T(8,128)(2,1)S(1)}, u32[]{:S(2)}, u32[]{:S(2)}) collective-permute-start(bf16[256,1024]{1,0:T(8,128)(2,1)S(1)} %collective-permute-done.h1), channel_id=1, source_target_pairs={{0,8},{1,9},{2,10},{3,11},{4,12},{5,13},{6,14},{7,15},{8,16},{9,17... | collective-permute-start | bytes 1572872 | tf_op jit(solution)/shard_map/ppermute | solution.py:211
  30.9 12.5 %copy-start.3 = (bf16[128,1024]{1,0:T(8,128)(2,1)}, bf16[128,1024]{1,0:T(8,128)(2,1)S(1)}, u32[]{:S(2)}) copy-start(bf16[128,1024]{1,0:T(8,128)(2,1)S(1)} %collective-permute-done.4.out_ref) | copy-start | bytes 786436
  30.9 12.5 %collective-permute-start.5 = (bf16[256,384]{1,0:T(8,128)(2,1)S(1)}, bf16[256,384]{1,0:T(8,128)(2,1)S(1)}, u32[]{:S(2)}, u32[]{:S(2)}) collective-permute-start(bf16[256,384]{1,0:T(8,128)(2,1)S(1)} %pad_maximum_fusion.n0), channel_id=1, source_target_pairs={{0,32},{1,33},{2,34},{3,35},{4,36},{5,37},{6,38},{7,39},{8,40},{9,... | collective-permute-start | bytes 589832 | tf_op jit(solution)/shard_map/ppermute | solution.py:211
  32.2 12.1 %collective-permute-start.6 = (bf16[256,384]{1,0:T(8,128)(2,1)S(1)}, bf16[256,384]{1,0:T(8,128)(2,1)S(1)}, u32[]{:S(2)}, u32[]{:S(2)}) collective-permute-start(bf16[256,384]{1,0:T(8,128)(2,1)S(1)} %pad_maximum_fusion.n0), channel_id=1, source_target_pairs={{0,64},{1,65},{2,66},{3,67},{4,68},{5,69},{6,70},{7,71},{8,72},{9,... | collective-permute-start | bytes 589832 | tf_op jit(solution)/shard_map/ppermute | solution.py:211
  34.6 9.6 %collective-permute-start.7 = (bf16[256,384]{1,0:T(8,128)(2,1)S(1)}, bf16[256,384]{1,0:T(8,128)(2,1)S(1)}, u32[]{:S(2)}, u32[]{:S(2)}) collective-permute-start(bf16[256,384]{1,0:T(8,128)(2,1)S(1)} %pad_maximum_fusion.n0), channel_id=1, source_target_pairs={{0,96},{1,97},{2,98},{3,99},{4,100},{5,101},{6,102},{7,103},{8,104... | collective-permute-start | bytes 589832 | tf_op jit(solution)/shard_map/ppermute | solution.py:211
  44.3 2.8 %collective-permute-start.13 = (bf16[128,1024]{1,0:T(8,128)(2,1)S(1)}, bf16[128,1024]{1,0:T(8,128)(2,1)S(1)}, u32[]{:S(2)}, u32[]{:S(2)}) collective-permute-start(bf16[128,1024]{1,0:T(8,128)(2,1)S(1)} %get-tuple-element.19), channel_id=1, source_target_pairs={{0,1},{1,0},{2,3},{3,2},{4,5},{5,4},{6,7},{7,6},{8,9},{9,8},{10,11... | collective-permute-start | bytes 786440 | tf_op jit(solution)/shard_map/ppermute | solution.py:211
  47.1 12.5 %copy-start.1 = (bf16[1,256,1024]{2,1,0:T(8,128)(2,1)S(1)}, bf16[1,256,1024]{2,1,0:T(8,128)(2,1)}, u32[]{:S(2)}) copy-start(bf16[1,256,1024]{2,1,0:T(8,128)(2,1)} %param.9) | copy-start | bytes 1572868
  47.9 20.3 %all-to-all-start.1 = ((bf16[32,4,1024]{2,1,0:T(4,128)(2,1)}), bf16[32,4,1024]{2,1,0:T(4,128)(2,1)S(1)}, u32[]{:S(2)}, u32[]{:S(2)}) async-start(bf16[32,4,1024]{2,1,0:T(4,128)(2,1)} %reshape.60), calls=%async_computation.1 | async-start | bytes 524288 | tf_op jit(solution)/shard_map/all_to_all | solution.py:27
  56.6 2.1 %collective-permute-start.12 = (bf16[128,1024]{1,0:T(8,128)(2,1)}, bf16[128,1024]{1,0:T(8,128)(2,1)S(1)}, u32[]{:S(2)}, u32[]{:S(2)}) collective-permute-start(bf16[128,1024]{1,0:T(8,128)(2,1)} %copy-done.3), channel_id=1, source_target_pairs={{0,1},{1,0},{2,3},{3,2},{4,5},{5,4},{6,7},{7,6},{8,9},{9,8},{10,11... | collective-permute-start | bytes 786440 | tf_op jit(solution)/shard_map/ppermute | solution.py:211
  57.4 1.4 %collective-permute-start.9 = (bf16[256,384]{1,0:T(8,128)(2,1)S(1)}, bf16[256,384]{1,0:T(8,128)(2,1)S(1)}, u32[]{:S(2)}, u32[]{:S(2)}) collective-permute-start(bf16[256,384]{1,0:T(8,128)(2,1)S(1)} %collective-permute-done.5.n1), channel_id=1, source_target_pairs={{0,1},{1,0},{2,3},{3,2},{4,5},{5,4},{6,7},{7,6},{8,9},{9,8},{10,11... | collective-permute-start | bytes 589832 | tf_op jit(solution)/shard_map/ppermute | solution.py:211
  57.5 1.8 %collective-permute-start.10 = (bf16[256,384]{1,0:T(8,128)(2,1)}, bf16[256,384]{1,0:T(8,128)(2,1)S(1)}, u32[]{:S(2)}, u32[]{:S(2)}) collective-permute-start(bf16[256,384]{1,0:T(8,128)(2,1)} %copy-done.5), channel_id=1, source_target_pairs={{0,1},{1,0},{2,3},{3,2},{4,5},{5,4},{6,7},{7,6},{8,9},{9,8},{10,11... | collective-permute-start | bytes 589832 | tf_op jit(solution)/shard_map/ppermute | solution.py:211
  57.9 1.7 %collective-permute-start.11 = (bf16[256,384]{1,0:T(8,128)(2,1)}, bf16[256,384]{1,0:T(8,128)(2,1)S(1)}, u32[]{:S(2)}, u32[]{:S(2)}) collective-permute-start(bf16[256,384]{1,0:T(8,128)(2,1)} %copy-done.7), channel_id=1, source_target_pairs={{0,1},{1,0},{2,3},{3,2},{4,5},{5,4},{6,7},{7,6},{8,9},{9,8},{10,11... | collective-permute-start | bytes 589832 | tf_op jit(solution)/shard_map/ppermute | solution.py:211
  58.0 1.7 %collective-permute-start.8 = (bf16[256,384]{1,0:T(8,128)(2,1)S(1)}, bf16[256,384]{1,0:T(8,128)(2,1)S(1)}, u32[]{:S(2)}, u32[]{:S(2)}) collective-permute-start(bf16[256,384]{1,0:T(8,128)(2,1)S(1)} %pad_maximum_fusion.n0), channel_id=1, source_target_pairs={{0,1},{1,0},{2,3},{3,2},{4,5},{5,4},{6,7},{7,6},{8,9},{9,8},{10,11... | collective-permute-start | bytes 589832 | tf_op jit(solution)/shard_map/ppermute | solution.py:211
  68.3 4.6 %collective-permute-start.14 = (f32[8,1024]{1,0:T(8,128)S(1)}, f32[8,1024]{1,0:T(8,128)S(1)}, u32[]{:S(2)}, u32[]{:S(2)}) collective-permute-start(f32[8,1024]{1,0:T(8,128)S(1)} %shard_map.93.t0), channel_id=1, source_target_pairs={{0,8},{1,9},{2,10},{3,11},{4,12},{5,13},{6,14},{7,15},{8,16},{9,17... | collective-permute-start | bytes 98312 | tf_op jit(solution)/shard_map/ppermute | solution.py:211
  69.6 4.3 %collective-permute-start.15 = (f32[8,1024]{1,0:T(8,128)S(1)}, f32[8,1024]{1,0:T(8,128)S(1)}, u32[]{:S(2)}, u32[]{:S(2)}) collective-permute-start(f32[8,1024]{1,0:T(8,128)S(1)} %shard_map.93.t0), channel_id=1, source_target_pairs={{0,16},{1,17},{2,18},{3,19},{4,20},{5,21},{6,22},{7,23},{8,24},{9,... | collective-permute-start | bytes 98312 | tf_op jit(solution)/shard_map/ppermute | solution.py:211
  71.6 2.8 %collective-permute-start.16 = (f32[8,1024]{1,0:T(8,128)S(1)}, f32[8,1024]{1,0:T(8,128)S(1)}, u32[]{:S(2)}, u32[]{:S(2)}) collective-permute-start(f32[8,1024]{1,0:T(8,128)S(1)} %shard_map.93.t0), channel_id=1, source_target_pairs={{0,24},{1,25},{2,26},{3,27},{4,28},{5,29},{6,30},{7,31},{8,0},{9,1... | collective-permute-start | bytes 98312 | tf_op jit(solution)/shard_map/ppermute | solution.py:211
  98.0 5.4 %collective-permute-start.17 = (bf16[32,8,1024]{2,1,0:T(8,128)(2,1)S(1)}, bf16[32,8,1024]{2,1,0:T(8,128)(2,1)S(1)}, u32[]{:S(2)}, u32[]{:S(2)}) collective-permute-start(bf16[32,8,1024]{2,1,0:T(8,128)(2,1)S(1)} %all_to_all.15), channel_id=1, source_target_pairs={{0,1},{1,0},{2,3},{3,2},{4,5},{5,4},{6,7},{7,6},{8,9},{9,8},{10,11... | collective-permute-start | bytes 1572872 | tf_op jit(solution)/shard_map/ppermute | solution.py:211
  (8 other events, 24.1 us)

commit v8 on v5

--- a/solution.py
+++ b/solution.py
@@ -191,7 +191,7 @@
     def more(state):
         return (state[0] < 9.0) & (state[1] > 1e-4)
 
-    r = exact(r, r)
+    r = lax.cond(norm < 512.0 * ridge, product, exact, r, r)
     state = (2.0 * c * ridge, size(r), x, r)
     state = lax.while_loop(lambda s: more(s) & (norm < 512.0 * ridge), lambda s: step(product, s), state)
     x = lax.while_loop(more, lambda s: step(exact, s), state)[2]
@@ -199,7 +199,7 @@
     def refine(state):
         i, _, x = state
         e = eye - exact(a, x)
-        return i + 1, jnp.sum(e * e), x + exact(x, e)
+        return i + 1, jnp.sum(e * e), x + product(x, e)
 
     _, _, x = lax.while_loop(
         lambda s: (s[0] == 0) | ((s[1] > 1e-7) & (s[0] < 4)), refine, (jnp.int32(0), jnp.float32(1.0), x)

time: 119 us -> 118 us (level)
  no operation moved by 1% of the time
where the time goes in v8:
time: 118 us
  starting transfers between devices  54.2 us (46%)
  blocking collectives  20.9 us (18%)
  Pallas kernels  20.5 us (17%)
  waiting for transfers between devices  16.1 us (14%)
  local copies, waits for them, and re-layouts  3.61 us (3%)
  between operations  1.51 us (1%)
    ppermute x18, starting transfers between devices, shift(): return lax.ppermute(x, ('grp', 'dev'), perm)  30.9 us
    all_to_all x1, blocking collectives, exchange(): lax.all_to_all(x, ('grp', 'dev'), split_axis=0, concat_axis=0, tiled=True...  20.9 us
    pallas_call x6, Pallas kernels, call(): pl.pallas_call(kernel, out_shape=out, in_specs=[pl.BlockSpec(memory_space...  20.5 us
    all_to_all x1, starting transfers between devices, local(): lax.all_to_all(after(info, got), ('grp', 'dev'), split_axis=0, concat_axi...  14.5 us
    all_to_all x1, starting transfers between devices, exchange(): lax.all_to_all(x, ('grp', 'dev'), split_axis=0, concat_axis=0, tiled=True...  8.82 us
    ppermute x18, waiting for transfers between devices, shift(): return lax.ppermute(x, ('grp', 'dev'), perm)  6.69 us
    all_to_all x1, waiting for transfers between devices, local(): lax.all_to_all(after(info, got), ('grp', 'dev'), split_axis=0, concat_axi...  6.36 us
    all_to_all x1, waiting for transfers between devices, exchange(): lax.all_to_all(x, ('grp', 'dev'), split_axis=0, concat_axis=0, tiled=True...  3.03 us
  transfers between devices with their start and end apart: 20, of which 13 were waited for; matrix products, arithmetic and copies ran while one was open for 1% of the time, Pallas kernels for 6%

profile of v8, /device:TPU:1, one launch (start us, length us, event | category | flops | bytes accessed | tf_op | source)
XLA Modules:
  0.0 117.6 jit_solution(16874130697206536666)
XLA Ops:
  0.0 2.0 %collective-permute-start = (bf16[256,1024]{1,0:T(8,128)(2,1)}, bf16[256,1024]{1,0:T(8,128)(2,1)S(1)}, u32[]{:S(2)}, u32[]{:S(2)}) collective-permute-start(bf16[256,1024]{1,0:T(8,128)(2,1)} %bitcast.15), channel_id=1, source_target_pairs={{0,8},{1,9},{2,10},{3,11},{4,12},{5,13},{6,14},{7,15},{8,16},{9,17... | collective-permute-start | bytes 1572872 | tf_op jit(solution)/shard_map/ppermute | solution.py:219
  2.0 1.3 %collective-permute-start.2 = (bf16[256,1024]{1,0:T(8,128)(2,1)}, bf16[256,1024]{1,0:T(8,128)(2,1)S(1)}, u32[]{:S(2)}, u32[]{:S(2)}) collective-permute-start(bf16[256,1024]{1,0:T(8,128)(2,1)} %bitcast.16), channel_id=1, source_target_pairs={{0,24},{1,25},{2,26},{3,27},{4,28},{5,29},{6,30},{7,31},{8,0},{9,1... | collective-permute-start | bytes 1572872 | tf_op jit(solution)/shard_map/ppermute | solution.py:219
  4.7 1.0 copy-done.1
  7.3 5.9 %collective-permute-start.3 = (bf16[128,384]{1,0:T(8,128)(2,1)S(1)}, bf16[128,384]{1,0:T(8,128)(2,1)S(1)}, u32[]{:S(2)}, u32[]{:S(2)}) collective-permute-start(bf16[128,384]{1,0:T(8,128)(2,1)S(1)} %shard_map.91), channel_id=1, source_target_pairs={{0,134},{1,135},{2,132},{3,133},{4,130},{5,131},{6,128},{7,129},{8... | collective-permute-start | bytes 294920 | tf_op jit(solution)/shard_map/ppermute | solution.py:219
  13.2 3.3 %collective-permute-start.4 = (bf16[128,1024]{1,0:T(8,128)(2,1)S(1)}, bf16[128,1024]{1,0:T(8,128)(2,1)S(1)}, u32[]{:S(2)}, u32[]{:S(2)}) collective-permute-start(bf16[128,1024]{1,0:T(8,128)(2,1)S(1)} %copy-done.8), channel_id=1, source_target_pairs={{0,0},{1,134},{2,2},{3,132},{4,4},{5,130},{6,6},{7,128},{8,32},{9,... | collective-permute-start | bytes 786440 | tf_op jit(solution)/shard_map/ppermute | solution.py:219
  18.0 14.5 %all-to-all-start = ((f32[256,1,128]{2,1,0:T(1,128)}), f32[256,1,128]{2,1,0:T(1,128)S(1)}, u32[]{:S(2)}, u32[]{:S(2)}) async-start(f32[256,1,128]{2,1,0:T(1,128)} %fusion), calls=%async_computation | async-start | bytes 262144 | tf_op jit(solution)/shard_map/all_to_all | solution.py:259
  32.5 1.5 %collective-permute-start.1 = (bf16[256,1024]{1,0:T(8,128)(2,1)S(1)}, bf16[256,1024]{1,0:T(8,128)(2,1)S(1)}, u32[]{:S(2)}, u32[]{:S(2)}) collective-permute-start(bf16[256,1024]{1,0:T(8,128)(2,1)S(1)} %collective-permute-done.h1), channel_id=1, source_target_pairs={{0,8},{1,9},{2,10},{3,11},{4,12},{5,13},{6,14},{7,15},{8,16},{9,17... | collective-permute-start | bytes 1572872 | tf_op jit(solution)/shard_map/ppermute | solution.py:219
  34.0 1.3 %collective-permute-start.5 = (bf16[256,384]{1,0:T(8,128)(2,1)S(1)}, bf16[256,384]{1,0:T(8,128)(2,1)S(1)}, u32[]{:S(2)}, u32[]{:S(2)}) collective-permute-start(bf16[256,384]{1,0:T(8,128)(2,1)S(1)} %pad_maximum_fusion.n0), channel_id=1, source_target_pairs={{0,32},{1,33},{2,34},{3,35},{4,36},{5,37},{6,38},{7,39},{8,40},{9,... | collective-permute-start | bytes 589832 | tf_op jit(solution)/shard_map/ppermute | solution.py:219
  35.3 2.5 %collective-permute-start.6 = (bf16[256,384]{1,0:T(8,128)(2,1)S(1)}, bf16[256,384]{1,0:T(8,128)(2,1)}, u32[]{:S(2)}, u32[]{:S(2)}) collective-permute-start(bf16[256,384]{1,0:T(8,128)(2,1)S(1)} %pad_maximum_fusion.n0), channel_id=1, source_target_pairs={{0,64},{1,65},{2,66},{3,67},{4,68},{5,69},{6,70},{7,71},{8,72},{9,... | collective-permute-start | bytes 589832 | tf_op jit(solution)/shard_map/ppermute | solution.py:219
  37.7 1.1 collective-permute-start.7
  38.9 6.4 %all-to-all-done = f32[256,1,128]{2,1,0:T(1,128)S(1)} async-done(((f32[256,1,128]{2,1,0:T(1,128)}), f32[256,1,128]{2,1,0:T(1,128)S(1)}, u32[]{:S(2)}, u32[]{:S(2)}) %all-to-all-start) | async-done | bytes 131104 | tf_op jit(solution)/shard_map/all_to_all | solution.py:259
  45.2 1.3 %shard_map.93 = (bf16[128,1024]{1,0:T(8,128)(2,1)S(1)}, bf16[128,1024]{1,0:T(8,128)(2,1)S(1)}) custom-call(s32[7]{0:T(128)S(1)} %stack.23.where, f32[256,128]{1,0:T(8,128)S(1)} %bitcast.19, bf16[256,1024]{1,0:T(8,128)(2,1)S(1)} %copy-done.2), custom_call_target="tpu_custom_call" | custom-call | flops 134217728 | bytes 1048576 | tf_op jit(solution)/shard_map/pallas_call | solution.py:43
  47.4 1.6 %collective-permute-start.13 = (bf16[128,1024]{1,0:T(8,128)(2,1)S(1)}, bf16[128,1024]{1,0:T(8,128)(2,1)S(1)}, u32[]{:S(2)}, u32[]{:S(2)}) collective-permute-start(bf16[128,1024]{1,0:T(8,128)(2,1)S(1)} %get-tuple-element.17), channel_id=1, source_target_pairs={{0,1},{1,0},{2,3},{3,2},{4,5},{5,4},{6,7},{7,6},{8,9},{9,8},{10,11... | collective-permute-start | bytes 786440 | tf_op jit(solution)/shard_map/ppermute | solution.py:219
  49.0 1.2 collective-permute-done.13
  51.0 8.8 %all-to-all-start.1 = ((bf16[32,4,1024]{2,1,0:T(4,128)(2,1)}), bf16[32,4,1024]{2,1,0:T(4,128)(2,1)S(1)}, u32[]{:S(2)}, u32[]{:S(2)}) async-start(bf16[32,4,1024]{2,1,0:T(4,128)(2,1)} %reshape.60), calls=%async_computation.1 | async-start | bytes 524288 | tf_op jit(solution)/shard_map/all_to_all | solution.py:27
  63.5 4.9 %shard_map.92.part_ref = f32[4,1024]{1,0:T(4,128)S(1)} custom-call(s32[7]{0:T(128)S(1)} %copy-done.5, bf16[256,1024]{1,0:T(8,128)(2,1)S(1)} %bitcast.17, bf16[256,1024]{1,0:T(8,128)(2,1)S(1)} %collective-permute-done.h1, bf16[256,1024]{1,0:T(8,128)(2,1)S(1)} %collective-permute-done.1.h2, bf16[256,1024]{1,0:T(8,128)(2,1)S(1)} %collective-permute-done.2.h3, ...), custom_call_target="tpu_custom_call" | custom-call | flops 1073741824 | bytes 1048576 | tf_op jit(solution)/shard_map/pallas_call | solution.py:43
  68.4 3.0 %all-to-all-done.1.old_ref = bf16[32,4,1024]{2,1,0:T(4,128)(2,1)S(1)} async-done(((bf16[32,4,1024]{2,1,0:T(4,128)(2,1)}), bf16[32,4,1024]{2,1,0:T(4,128)(2,1)S(1)}, u32[]{:S(2)}, u32[]{:S(2)}) %all-to-all-start.1) | async-done | bytes 262176 | tf_op jit(solution)/shard_map/all_to_all | solution.py:27
  71.6 1.3 %collective-permute-start.14 = (f32[8,1024]{1,0:T(8,128)S(1)}, f32[8,1024]{1,0:T(8,128)S(1)}, u32[]{:S(2)}, u32[]{:S(2)}) collective-permute-start(f32[8,1024]{1,0:T(8,128)S(1)} %shard_map.94.t0), channel_id=1, source_target_pairs={{0,8},{1,9},{2,10},{3,11},{4,12},{5,13},{6,14},{7,15},{8,16},{9,17... | collective-permute-start | bytes 98312 | tf_op jit(solution)/shard_map/ppermute | solution.py:219
  72.9 1.5 %collective-permute-start.15 = (f32[8,1024]{1,0:T(8,128)S(1)}, f32[8,1024]{1,0:T(8,128)S(1)}, u32[]{:S(2)}, u32[]{:S(2)}) collective-permute-start(f32[8,1024]{1,0:T(8,128)S(1)} %shard_map.94.t0), channel_id=1, source_target_pairs={{0,16},{1,17},{2,18},{3,19},{4,20},{5,21},{6,22},{7,23},{8,24},{9,... | collective-permute-start | bytes 98312 | tf_op jit(solution)/shard_map/ppermute | solution.py:219
  74.3 1.8 %collective-permute-start.16 = (f32[8,1024]{1,0:T(8,128)S(1)}, f32[8,1024]{1,0:T(8,128)S(1)}, u32[]{:S(2)}, u32[]{:S(2)}) collective-permute-start(f32[8,1024]{1,0:T(8,128)S(1)} %shard_map.94.t0), channel_id=1, source_target_pairs={{0,24},{1,25},{2,26},{3,27},{4,28},{5,29},{6,30},{7,31},{8,0},{9,1... | collective-permute-start | bytes 98312 | tf_op jit(solution)/shard_map/ppermute | solution.py:219
  77.5 20.9 %all_to_all.15 = bf16[32,8,1024]{2,1,0:T(8,128)(2,1)S(1)} all-to-all(bf16[32,8,1024]{2,1,0:T(8,128)(2,1)S(1)} %broadcast_in_dim.21), channel_id=1, replica_groups={{0,32,64,96,2,34,66,98,4,36,68,100,6,38,70,102,128,160,192,224,130,162,..., dimensions={0} | all-to-all | bytes 1048576 | tf_op jit(solution)/shard_map/all_to_all | solution.py:27
  98.4 4.3 %collective-permute-start.17 = (bf16[32,8,1024]{2,1,0:T(8,128)(2,1)S(1)}, bf16[32,8,1024]{2,1,0:T(8,128)(2,1)S(1)}, u32[]{:S(2)}, u32[]{:S(2)}) collective-permute-start(bf16[32,8,1024]{2,1,0:T(8,128)(2,1)S(1)} %all_to_all.15), channel_id=1, source_target_pairs={{0,1},{1,0},{2,3},{3,2},{4,5},{5,4},{6,7},{7,6},{8,9},{9,8},{10,11... | collective-permute-start | bytes 1572872 | tf_op jit(solution)/shard_map/ppermute | solution.py:219
  102.7 1.5 %collective-permute-done.17 = bf16[32,8,1024]{2,1,0:T(8,128)(2,1)S(1)} collective-permute-done((bf16[32,8,1024]{2,1,0:T(8,128)(2,1)S(1)}, bf16[32,8,1024]{2,1,0:T(8,128)(2,1)S(1)}, u32[]{:S(2)}, u32[]{:S(2)}) %collective-permute-start.17) | collective-permute-done | bytes 524320 | tf_op jit(solution)/shard_map/ppermute | solution.py:219
  104.2 13.3 %shard_map.96 = bf16[256,1024]{1,0:T(8,128)(2,1)} custom-call(bf16[256,1024]{1,0:T(8,128)(2,1)S(1)} %bitcast.18, bf16[256,1024]{1,0:T(8,128)(2,1)S(1)} %bitcast.22, bf16[256,1024]{1,0:T(8,128)(2,1)S(1)} %copy-done.2), custom_call_target="tpu_custom_call" | custom-call | flops 2147483648 | bytes 1048576 | tf_op jit(solution)/shard_map/pallas_call | solution.py:43
  (49 shorter events, 10.1 us)
Async XLA Ops:
  0.0 32.5 %collective-permute-start = (bf16[256,1024]{1,0:T(8,128)(2,1)}, bf16[256,1024]{1,0:T(8,128)(2,1)S(1)}, u32[]{:S(2)}, u32[]{:S(2)}) collective-permute-start(bf16[256,1024]{1,0:T(8,128)(2,1)} %bitcast.15), channel_id=1, source_target_pairs={{0,8},{1,9},{2,10},{3,11},{4,12},{5,13},{6,14},{7,15},{8,16},{9,17... | collective-permute-start | bytes 1572872 | tf_op jit(solution)/shard_map/ppermute | solution.py:219
  2.0 32.0 %collective-permute-start.2 = (bf16[256,1024]{1,0:T(8,128)(2,1)}, bf16[256,1024]{1,0:T(8,128)(2,1)S(1)}, u32[]{:S(2)}, u32[]{:S(2)}) collective-permute-start(bf16[256,1024]{1,0:T(8,128)(2,1)} %bitcast.16), channel_id=1, source_target_pairs={{0,24},{1,25},{2,26},{3,27},{4,28},{5,29},{6,30},{7,31},{8,0},{9,1... | collective-permute-start | bytes 1572872 | tf_op jit(solution)/shard_map/ppermute | solution.py:219
  6.7 38.5 %copy-start.4 = (s32[7]{0:T(128)}, s32[7]{0:T(128)S(1)}, u32[]{:S(2)}) copy-start(s32[7]{0:T(128)S(1)} %stack.23.where) | copy-start | bytes 88
  6.7 6.5 %copy-start.8 = (bf16[128,1024]{1,0:T(8,128)(2,1)S(1)}, bf16[128,1024]{1,0:T(8,128)(2,1)}, u32[]{:S(2)}) copy-start(bf16[128,1024]{1,0:T(8,128)(2,1)} %param.12) | copy-start | bytes 786436
  7.3 37.9 %copy-start.2 = (bf16[256,1024]{1,0:T(8,128)(2,1)S(1)}, bf16[256,1024]{1,0:T(8,128)(2,1)}, u32[]{:S(2)}) copy-start(bf16[256,1024]{1,0:T(8,128)(2,1)} %bank_ref.3) | copy-start | bytes 1572868
  7.3 10.7 %collective-permute-start.3 = (bf16[128,384]{1,0:T(8,128)(2,1)S(1)}, bf16[128,384]{1,0:T(8,128)(2,1)S(1)}, u32[]{:S(2)}, u32[]{:S(2)}) collective-permute-start(bf16[128,384]{1,0:T(8,128)(2,1)S(1)} %shard_map.91), channel_id=1, source_target_pairs={{0,134},{1,135},{2,132},{3,133},{4,130},{5,131},{6,128},{7,129},{8... | collective-permute-start | bytes 294920 | tf_op jit(solution)/shard_map/ppermute | solution.py:219
  13.2 20.8 %collective-permute-start.4 = (bf16[128,1024]{1,0:T(8,128)(2,1)S(1)}, bf16[128,1024]{1,0:T(8,128)(2,1)S(1)}, u32[]{:S(2)}, u32[]{:S(2)}) collective-permute-start(bf16[128,1024]{1,0:T(8,128)(2,1)S(1)} %copy-done.8), channel_id=1, source_target_pairs={{0,0},{1,134},{2,2},{3,132},{4,4},{5,130},{6,6},{7,128},{8,32},{9,... | collective-permute-start | bytes 786440 | tf_op jit(solution)/shard_map/ppermute | solution.py:219
  18.0 27.2 %all-to-all-start = ((f32[256,1,128]{2,1,0:T(1,128)}), f32[256,1,128]{2,1,0:T(1,128)S(1)}, u32[]{:S(2)}, u32[]{:S(2)}) async-start(f32[256,1,128]{2,1,0:T(1,128)} %fusion), calls=%async_computation | async-start | bytes 262144 | tf_op jit(solution)/shard_map/all_to_all | solution.py:259
  32.5 17.7 %collective-permute-start.1 = (bf16[256,1024]{1,0:T(8,128)(2,1)S(1)}, bf16[256,1024]{1,0:T(8,128)(2,1)S(1)}, u32[]{:S(2)}, u32[]{:S(2)}) collective-permute-start(bf16[256,1024]{1,0:T(8,128)(2,1)S(1)} %collective-permute-done.h1), channel_id=1, source_target_pairs={{0,8},{1,9},{2,10},{3,11},{4,12},{5,13},{6,14},{7,15},{8,16},{9,17... | collective-permute-start | bytes 1572872 | tf_op jit(solution)/shard_map/ppermute | solution.py:219
  34.0 12.5 %collective-permute-start.5 = (bf16[256,384]{1,0:T(8,128)(2,1)S(1)}, bf16[256,384]{1,0:T(8,128)(2,1)S(1)}, u32[]{:S(2)}, u32[]{:S(2)}) collective-permute-start(bf16[256,384]{1,0:T(8,128)(2,1)S(1)} %pad_maximum_fusion.n0), channel_id=1, source_target_pairs={{0,32},{1,33},{2,34},{3,35},{4,36},{5,37},{6,38},{7,39},{8,40},{9,... | collective-permute-start | bytes 589832 | tf_op jit(solution)/shard_map/ppermute | solution.py:219
  35.3 12.1 %collective-permute-start.6 = (bf16[256,384]{1,0:T(8,128)(2,1)S(1)}, bf16[256,384]{1,0:T(8,128)(2,1)}, u32[]{:S(2)}, u32[]{:S(2)}) collective-permute-start(bf16[256,384]{1,0:T(8,128)(2,1)S(1)} %pad_maximum_fusion.n0), channel_id=1, source_target_pairs={{0,64},{1,65},{2,66},{3,67},{4,68},{5,69},{6,70},{7,71},{8,72},{9,... | collective-permute-start | bytes 589832 | tf_op jit(solution)/shard_map/ppermute | solution.py:219
  37.7 9.7 %collective-permute-start.7 = (bf16[256,384]{1,0:T(8,128)(2,1)S(1)}, bf16[256,384]{1,0:T(8,128)(2,1)}, u32[]{:S(2)}, u32[]{:S(2)}) collective-permute-start(bf16[256,384]{1,0:T(8,128)(2,1)S(1)} %pad_maximum_fusion.n0), channel_id=1, source_target_pairs={{0,96},{1,97},{2,98},{3,99},{4,100},{5,101},{6,102},{7,103},{8,104... | collective-permute-start | bytes 589832 | tf_op jit(solution)/shard_map/ppermute | solution.py:219
  47.4 2.7 %collective-permute-start.13 = (bf16[128,1024]{1,0:T(8,128)(2,1)S(1)}, bf16[128,1024]{1,0:T(8,128)(2,1)S(1)}, u32[]{:S(2)}, u32[]{:S(2)}) collective-permute-start(bf16[128,1024]{1,0:T(8,128)(2,1)S(1)} %get-tuple-element.17), channel_id=1, source_target_pairs={{0,1},{1,0},{2,3},{3,2},{4,5},{5,4},{6,7},{7,6},{8,9},{9,8},{10,11... | collective-permute-start | bytes 786440 | tf_op jit(solution)/shard_map/ppermute | solution.py:219
  50.2 12.7 %copy-start = (bf16[1,256,1024]{2,1,0:T(8,128)(2,1)S(1)}, bf16[1,256,1024]{2,1,0:T(8,128)(2,1)}, u32[]{:S(2)}) copy-start(bf16[1,256,1024]{2,1,0:T(8,128)(2,1)} %param.9) | copy-start | bytes 1572868
  51.0 20.4 %all-to-all-start.1 = ((bf16[32,4,1024]{2,1,0:T(4,128)(2,1)}), bf16[32,4,1024]{2,1,0:T(4,128)(2,1)S(1)}, u32[]{:S(2)}, u32[]{:S(2)}) async-start(bf16[32,4,1024]{2,1,0:T(4,128)(2,1)} %reshape.60), calls=%async_computation.1 | async-start | bytes 524288 | tf_op jit(solution)/shard_map/all_to_all | solution.py:27
  59.9 1.9 %collective-permute-start.12 = (bf16[128,1024]{1,0:T(8,128)(2,1)S(1)}, bf16[128,1024]{1,0:T(8,128)(2,1)S(1)}, u32[]{:S(2)}, u32[]{:S(2)}) collective-permute-start(bf16[128,1024]{1,0:T(8,128)(2,1)S(1)} %collective-permute-done.4.out_ref), channel_id=1, source_target_pairs={{0,1},{1,0},{2,3},{3,2},{4,5},{5,4},{6,7},{7,6},{8,9},{9,8},{10,11... | collective-permute-start | bytes 786440 | tf_op jit(solution)/shard_map/ppermute | solution.py:219
  60.6 1.4 %collective-permute-start.9 = (bf16[256,384]{1,0:T(8,128)(2,1)S(1)}, bf16[256,384]{1,0:T(8,128)(2,1)S(1)}, u32[]{:S(2)}, u32[]{:S(2)}) collective-permute-start(bf16[256,384]{1,0:T(8,128)(2,1)S(1)} %collective-permute-done.5.n1), channel_id=1, source_target_pairs={{0,1},{1,0},{2,3},{3,2},{4,5},{5,4},{6,7},{7,6},{8,9},{9,8},{10,11... | collective-permute-start | bytes 589832 | tf_op jit(solution)/shard_map/ppermute | solution.py:219
  60.7 1.8 %collective-permute-start.10 = (bf16[256,384]{1,0:T(8,128)(2,1)}, bf16[256,384]{1,0:T(8,128)(2,1)S(1)}, u32[]{:S(2)}, u32[]{:S(2)}) collective-permute-start(bf16[256,384]{1,0:T(8,128)(2,1)} %collective-permute-done.6.n2), channel_id=1, source_target_pairs={{0,1},{1,0},{2,3},{3,2},{4,5},{5,4},{6,7},{7,6},{8,9},{9,8},{10,11... | collective-permute-start | bytes 589832 | tf_op jit(solution)/shard_map/ppermute | solution.py:219
  61.1 1.7 %collective-permute-start.11 = (bf16[256,384]{1,0:T(8,128)(2,1)}, bf16[256,384]{1,0:T(8,128)(2,1)S(1)}, u32[]{:S(2)}, u32[]{:S(2)}) collective-permute-start(bf16[256,384]{1,0:T(8,128)(2,1)} %collective-permute-done.7.n3), channel_id=1, source_target_pairs={{0,1},{1,0},{2,3},{3,2},{4,5},{5,4},{6,7},{7,6},{8,9},{9,8},{10,11... | collective-permute-start | bytes 589832 | tf_op jit(solution)/shard_map/ppermute | solution.py:219
  61.2 1.7 %collective-permute-start.8 = (bf16[256,384]{1,0:T(8,128)(2,1)S(1)}, bf16[256,384]{1,0:T(8,128)(2,1)S(1)}, u32[]{:S(2)}, u32[]{:S(2)}) collective-permute-start(bf16[256,384]{1,0:T(8,128)(2,1)S(1)} %pad_maximum_fusion.n0), channel_id=1, source_target_pairs={{0,1},{1,0},{2,3},{3,2},{4,5},{5,4},{6,7},{7,6},{8,9},{9,8},{10,11... | collective-permute-start | bytes 589832 | tf_op jit(solution)/shard_map/ppermute | solution.py:219
  71.6 4.6 %collective-permute-start.14 = (f32[8,1024]{1,0:T(8,128)S(1)}, f32[8,1024]{1,0:T(8,128)S(1)}, u32[]{:S(2)}, u32[]{:S(2)}) collective-permute-start(f32[8,1024]{1,0:T(8,128)S(1)} %shard_map.94.t0), channel_id=1, source_target_pairs={{0,8},{1,9},{2,10},{3,11},{4,12},{5,13},{6,14},{7,15},{8,16},{9,17... | collective-permute-start | bytes 98312 | tf_op jit(solution)/shard_map/ppermute | solution.py:219
  72.9 4.3 %collective-permute-start.15 = (f32[8,1024]{1,0:T(8,128)S(1)}, f32[8,1024]{1,0:T(8,128)S(1)}, u32[]{:S(2)}, u32[]{:S(2)}) collective-permute-start(f32[8,1024]{1,0:T(8,128)S(1)} %shard_map.94.t0), channel_id=1, source_target_pairs={{0,16},{1,17},{2,18},{3,19},{4,20},{5,21},{6,22},{7,23},{8,24},{9,... | collective-permute-start | bytes 98312 | tf_op jit(solution)/shard_map/ppermute | solution.py:219
  74.3 2.9 %collective-permute-start.16 = (f32[8,1024]{1,0:T(8,128)S(1)}, f32[8,1024]{1,0:T(8,128)S(1)}, u32[]{:S(2)}, u32[]{:S(2)}) collective-permute-start(f32[8,1024]{1,0:T(8,128)S(1)} %shard_map.94.t0), channel_id=1, source_target_pairs={{0,24},{1,25},{2,26},{3,27},{4,28},{5,29},{6,30},{7,31},{8,0},{9,1... | collective-permute-start | bytes 98312 | tf_op jit(solution)/shard_map/ppermute | solution.py:219
  98.4 5.8 %collective-permute-start.17 = (bf16[32,8,1024]{2,1,0:T(8,128)(2,1)S(1)}, bf16[32,8,1024]{2,1,0:T(8,128)(2,1)S(1)}, u32[]{:S(2)}, u32[]{:S(2)}) collective-permute-start(bf16[32,8,1024]{2,1,0:T(8,128)(2,1)S(1)} %all_to_all.15), channel_id=1, source_target_pairs={{0,1},{1,0},{2,3},{3,2},{4,5},{5,4},{6,7},{7,6},{8,9},{9,8},{10,11... | collective-permute-start | bytes 1572872 | tf_op jit(solution)/shard_map/ppermute | solution.py:219
  (5 other events, 14.1 us)
